TPU v7x, 256 devices: a whole 4x4x8 slice. The times are simulated.
256 devices in a mesh: source: 8 (over z_hi, y), profile: 8 (over z_lo, core), line: 4 (over x).
Axes of the slice: x: 4, y: 4, z: 8 (z_hi: 2, z_lo: 4; z = z_hi * 4 + z_lo), core: 2. Of those that a mesh axis runs over, the one named last changes fastest.
Arguments:
- source_grad: bfloat16 [8, 3, 256, 256, 512], P('source', None, 'profile', 'line'), may hold values from -30 to 30
- adjoint_grad: bfloat16 [8, 3, 256, 256, 512], P('source', None, 'profile', 'line'), may hold values from -6 to 6
- log_model: float32 [256, 256, 512], P('profile', 'line'), may hold values from -3 to 3
- surface_depth: int32 [256, 256], P('profile', 'line'), may hold values from 0 to 63
- source_columns: int32 [8], replicated, may hold values from 0 to 65535
- receiver_columns: int32 [256], replicated, may hold values from 0 to 65535
Outputs:
- search_direction: float32 [256, 256, 512], P('profile', 'line')
All inputs are finite; a program needn't handle non-finite values.
Results may differ from a plain program's by a relative error of at most 0.0003.
Values sent between devices are 32-bit elements; how exact they have to be, the bound alone decides.
No kernel may reach another device: no remote copies, remote signals or barrier semaphores. Data moves between devices by JAX's collectives and lax.ppermute only.
A program may use at most 128 MiB of HBM per device.

v0:
```python
import jax
import jax.numpy as jnp
from jax import lax
from jax.sharding import PartitionSpec as P

smoothing_rate = 0.15
support_width = 0.3
floor_eps = 1e-06
mark_radius = 3


def with_halo(array, sides, width):
    for axis, dim in sides:
        size, length = (lax.axis_size(axis), array.shape[dim])
        up = [(i, (i + 1) % size) for i in range(size - 1)]
        down = [(j, i) for i, j in up]
        last = lax.slice_in_dim(array, length - width, length, axis=dim)
        leading = lax.slice_in_dim(array, 0, width, axis=dim)
        before = lax.ppermute(last, axis, up)
        after = lax.ppermute(leading, axis, down)
        array = jnp.concatenate([before, array, after], axis=dim)
    return array


def diffuse(framed_field, framed_weight):
    centre = framed_field[1:-1, 1:-1]
    weight_mid = framed_weight[1:-1, 1:-1]
    depth_field = jnp.pad(centre, ((0, 0), (0, 0), (1, 1)))
    depth_weight = jnp.pad(weight_mid, ((0, 0), (0, 0), (1, 1)))
    neighbour_pairs = (
        (framed_field[2:, 1:-1], framed_weight[2:, 1:-1]),
        (framed_field[:-2, 1:-1], framed_weight[:-2, 1:-1]),
        (framed_field[1:-1, 2:], framed_weight[1:-1, 2:]),
        (framed_field[1:-1, :-2], framed_weight[1:-1, :-2]),
        (depth_field[:, :, 2:], depth_weight[:, :, 2:]),
        (depth_field[:, :, :-2], depth_weight[:, :, :-2]),
    )
    flux_total = jnp.zeros_like(centre)
    for neighbour, weight_nb in neighbour_pairs:
        flux_total = flux_total + jnp.sqrt(weight_mid * weight_nb) * (neighbour - centre)
    return centre + smoothing_rate * flux_total


def shards(source_grad, adjoint_grad, log_model, surface_depth, source_columns, receiver_columns):
    tile_x, tile_y, depth_cells = log_model.shape
    forward = source_grad.astype(jnp.float32)
    backward = adjoint_grad.astype(jnp.float32)
    correlation = jnp.sum(jnp.sum(forward * backward, axis=1), axis=0)
    energy = jnp.sum(
        jnp.sum(forward * forward, axis=1) * jnp.sum(backward * backward, axis=1), axis=0
    )
    correlation, energy = lax.psum((correlation, energy), "source")
    scaled = correlation / jnp.sqrt(energy + floor_eps)
    depth_index = lax.broadcasted_iota(jnp.int32, (tile_x, tile_y, depth_cells), 2)
    active = (depth_index >= surface_depth[:, :, None]).astype(jnp.float32)
    total_y = tile_y * lax.axis_size("line")
    columns = jnp.concatenate([source_columns, receiver_columns])
    electrode_x = columns // total_y
    electrode_y = columns % total_y
    global_x = lax.broadcasted_iota(jnp.int32, (1, tile_x), 1) + lax.axis_index("profile") * tile_x
    global_y = lax.broadcasted_iota(jnp.int32, (1, tile_y), 1) + lax.axis_index("line") * tile_y
    near_x = (jnp.abs(global_x - electrode_x[:, None]) <= mark_radius).astype(jnp.float32)
    near_y = (jnp.abs(global_y - electrode_y[:, None]) <= mark_radius).astype(jnp.float32)
    covered = jnp.einsum("ex,ey->xy", near_x, near_y, precision=lax.Precision.HIGHEST)
    band_depth = depth_cells // 16
    shallow = (depth_index < surface_depth[:, :, None] + band_depth).astype(jnp.float32)
    electrode_marks = (covered > 0.5).astype(jnp.float32)[:, :, None] * shallow
    direction = scaled * active * (1.0 - electrode_marks)
    weight = (
        active
        * (support_width * support_width)
        / (log_model * log_model + support_width * support_width)
    )
    stacked = jnp.stack([weight, direction])
    framed = with_halo(stacked, (("profile", 1), ("line", 2)), 1)
    framed_weight = framed[0]
    direction = diffuse(framed[1], framed_weight)
    framed_field = with_halo(direction, (("profile", 0), ("line", 1)), 1)
    direction = diffuse(framed_field, framed_weight)
    return direction


def solution(mesh):
    placed = (
        P("source", None, "profile", "line", None),
        P("source", None, "profile", "line", None),
        P("profile", "line", None),
        P("profile", "line"),
        P(),
        P(),
    )
    return jax.shard_map(
        shards, mesh=mesh, in_specs=placed, out_specs=P("profile", "line", None), check_vma=False
    )
```

profile of v0, /device:TPU:33, one launch (start us, length us, event | category | flops | bytes accessed | tf_op | source)
XLA Modules:
  0.0 477.1 jit_solution(3963497023386467815)
XLA Ops:
  6.5 0.0 all-reduce.6.cloned.1.call-start
  6.5 13.2 %fusion.2 = (f32[32,64,512]{2,1,0:T(8,128)S(1)}, f32[32,64,512]{2,1,0:T(8,128)}, f32[32,64,512]{2,1,0:T(8,128)S(1)}) fusion(bf16[1,3,32,64,512]{4,3,2,1,0:T(8,128)(2,1)} %param.7, bf16[1,3,32,64,512]{4,3,2,1,0:T(8,128)(2,1)} %param.6), kind=kLoop, calls=%fused_computation.5 | loop fusion | flops 22020096 | bytes 25165824 | tf_op jit(solution)/shard_map/reduce_sum | solution.py:50
  19.7 3.0 mul.112
  22.7 0.0 copy-start.1
  22.7 0.0 copy-start.2
  22.7 0.0 copy-start
  22.7 0.0 all-reduce.6.cloned.1.call-update
  22.8 0.6 copy-done.1
  23.4 0.0 copy-done.2
  23.4 0.1 add_select_fusion.1
  23.5 0.3 fusion.45
  23.8 0.0 copy-done
  23.8 353.2 %all-reduce.6.cloned.1.call-done = (f32[32,64,512]{2,1,0:T(8,128)}, f32[32,64,512]{2,1,0:T(8,128)}) async-done(((f32[32,64,512]{2,1,0:T(8,128)}, f32[32,64,512]{2,1,0:T(8,128)}), (f32[32,64,512]{2,1,0:T(8,128)}, f32[32,64,512]{2,1,0:T(8,128)})) %all-reduce.6.cloned.1.call-update) | async-done | bytes 8388624 | tf_op jit(solution)/shard_map/psum | solution.py:52
  377.0 6.1 %divide_bitcast_fusion = (f32[1,32,64,512]{3,2,1,0:T(8,128)S(1)}, f32[1,32,64,512]{3,2,1,0:T(8,128)S(1)}) fusion(f32[32,64,512]{2,1,0:T(8,128)} %param.8, s32[32,64]{1,0:T(8,128)S(1)} %copy-done, f32[32,64]{1,0:T(8,128)S(1)} %fusion.45, s32[32,64]{1,0:T(8,128)S(1)} %broadcast_add_fusion, f32[32,64,512]{2,1,0:T(8,128)} %get-tuple-element.8, ...), kind=kLoop, calls=%fused_computation.75 | loop fusion | flops 12582912 | bytes 20996096 | tf_op jit(solution)/shard_map/stack | solution.py:74
  383.2 1.9 collective-permute-start
  385.1 2.5 collective-permute-start.1
  387.6 0.8 collective-permute-done
  388.4 4.4 collective-permute-done.1
  392.8 0.3 pad_maximum_fusion.14
  393.0 3.1 collective-permute-start.2
  396.1 1.5 collective-permute-start.3
  397.6 0.5 collective-permute-done.2
  398.1 3.8 collective-permute-done.3
  401.9 8.6 %pad_maximum_fusion = f32[2,34,66,512]{3,2,1,0:T(8,128)} fusion(f32[2,34,1,512]{3,2,1,0:T(1,128)S(1)} %collective-permute-done.3, f32[2,1,64,512]{3,2,1,0:T(8,128)S(1)} %collective-permute-done.1, f32[1,32,64,512]{3,2,1,0:T(8,128)S(1)} %get-tuple-element.21, f32[1,32,64,512]{3,2,1,0:T(8,128)S(1)} %get-tuple-element.20, ...), kind=kLoop, calls=%fused_computation.6 | loop fusion | flops 11489280 | bytes 18382848 | tf_op jit(solution)/shard_map/concatenate | solution.py:21
  410.6 5.1 %slice_bitcast_fusion = (f32[34,66,512]{2,1,0:T(8,128)S(1)}, f32[34,66,512]{2,1,0:T(8,128)S(1)}) fusion(f32[2,34,66,512]{3,2,1,0:T(8,128)} %pad_maximum_fusion), kind=kLoop, calls=%fused_computation.13 | loop fusion | bytes 18382848 | tf_op jit(solution)/shard_map/squeeze | solution.py:76
  415.7 0.6 slice.134
  416.3 2.6 slice.132
  418.9 15.8 %fusion.12 = f32[32,64,512]{2,1,0:T(8,128)S(1)} fusion(f32[32,64,512]{2,1,0:T(8,128)} %slice.132, f32[34,66,512]{2,1,0:T(8,128)S(1)} %get-tuple-element.11, f32[32,64,512]{2,1,0:T(8,128)S(1)} %slice.134, f32[34,66,512]{2,1,0:T(8,128)S(1)} %get-tuple-element.10), kind=kLoop, calls=%fused_computation.24 | loop fusion | flops 26214400 | bytes 46137344 | tf_op jit(solution)/shard_map/add | solution.py:41
  434.7 3.2 collective-permute-start.5
  437.9 3.0 collective-permute-start.4
  440.9 0.0 collective-permute-done.5
  440.9 3.3 collective-permute-done.4
  444.2 0.1 pad_maximum_fusion.17
  444.3 3.1 collective-permute-start.7
  447.5 1.5 collective-permute-start.6
  449.0 0.0 collective-permute-done.7
  449.0 0.1 copy.16
  449.1 3.6 collective-permute-done.6
  452.7 0.1 copy.14
  452.7 17.6 %fusion.20 = f32[32,64,512]{2,1,0:T(8,128)} fusion(f32[32,64,512]{2,1,0:T(8,128)S(1)} %fusion.12, f32[34,1,512]{2,1,0:T(1,128)S(1)} %copy.16, f32[1,64,512]{2,1,0:T(8,128)S(1)} %collective-permute-done.4, f32[1,64,512]{2,1,0:T(8,128)S(1)} %collective-permute-done.5, f32[34,1,512]{2,1,0:T(1,128)S(1)} %copy.14, f32[32,64,512]{2,1,0:T(8,128)S(1)} %slice.134, ...), kind=kLoop, calls=%fused_computation.32 | loop fusion | flops 34603008 | bytes 29761536 | tf_op jit(solution)/shard_map/add | solution.py:41
  (7 shorter events, 0.1 us)
Async XLA Ops:
  6.5 370.5 %all-reduce.6.cloned.1.call-start = ((), (), s32[]{:S(2)}) async-start(), calls=%async_computation | async-start | bytes 16777216 | tf_op jit(solution)/shard_map/psum | solution.py:52
  22.7 0.7 copy-start.1
  22.7 0.7 copy-start.2
  22.7 1.1 copy-start
  383.2 5.2 %collective-permute-start = (f32[2,1,64,512]{3,2,1,0:T(8,128)S(1)}, f32[2,1,64,512]{3,2,1,0:T(8,128)S(1)}, u32[]{:S(2)}, u32[]{:S(2)}) collective-permute-start(f32[2,1,64,512]{3,2,1,0:T(8,128)S(1)} %get-tuple-element.14), channel_id=1, source_target_pairs={{0,4},{4,8},{8,12},{12,16},{16,20},{20,24},{24,28},{1,5},{5,9},{9,... | collective-permute-start | bytes 786440 | tf_op jit(solution)/shard_map/ppermute | solution.py:19
  385.1 7.7 %collective-permute-start.1 = (f32[2,1,64,512]{3,2,1,0:T(8,128)S(1)}, f32[2,1,64,512]{3,2,1,0:T(8,128)S(1)}, u32[]{:S(2)}, u32[]{:S(2)}) collective-permute-start(f32[2,1,64,512]{3,2,1,0:T(8,128)S(1)} %get-tuple-element.15), channel_id=1, source_target_pairs={{4,0},{8,4},{12,8},{16,12},{20,16},{24,20},{28,24},{5,1},{9,5},{13... | collective-permute-start | bytes 786440 | tf_op jit(solution)/shard_map/ppermute | solution.py:20
  393.0 5.1 %collective-permute-start.2 = (f32[2,34,1,512]{3,2,1,0:T(1,128)S(1)}, f32[2,34,1,512]{3,2,1,0:T(1,128)S(1)}, u32[]{:S(2)}, u32[]{:S(2)}) collective-permute-start(f32[2,34,1,512]{3,2,1,0:T(1,128)S(1)} %get-tuple-element.12), channel_id=1, source_target_pairs={{0,1},{1,2},{2,3},{4,5},{5,6},{6,7},{8,9},{9,10},{10,11},{12,13},{... | collective-permute-start | bytes 417800 | tf_op jit(solution)/shard_map/ppermute | solution.py:19
  396.1 5.8 %collective-permute-start.3 = (f32[2,34,1,512]{3,2,1,0:T(1,128)S(1)}, f32[2,34,1,512]{3,2,1,0:T(1,128)S(1)}, u32[]{:S(2)}, u32[]{:S(2)}) collective-permute-start(f32[2,34,1,512]{3,2,1,0:T(1,128)S(1)} %get-tuple-element.13), channel_id=1, source_target_pairs={{1,0},{2,1},{3,2},{5,4},{6,5},{7,6},{9,8},{10,9},{11,10},{13,12},{... | collective-permute-start | bytes 417800 | tf_op jit(solution)/shard_map/ppermute | solution.py:20
  434.7 6.2 %collective-permute-start.5 = (f32[1,64,512]{2,1,0:T(8,128)S(1)}, f32[1,64,512]{2,1,0:T(8,128)S(1)}, u32[]{:S(2)}, u32[]{:S(2)}) collective-permute-start(f32[1,64,512]{2,1,0:T(8,128)S(1)} %get-tuple-element.18), channel_id=1, source_target_pairs={{0,4},{4,8},{8,12},{12,16},{16,20},{20,24},{24,28},{1,5},{5,9},{9,... | collective-permute-start | bytes 393224 | tf_op jit(solution)/shard_map/ppermute | solution.py:19
  437.9 6.3 %collective-permute-start.4 = (f32[1,64,512]{2,1,0:T(8,128)S(1)}, f32[1,64,512]{2,1,0:T(8,128)S(1)}, u32[]{:S(2)}, u32[]{:S(2)}) collective-permute-start(f32[1,64,512]{2,1,0:T(8,128)S(1)} %get-tuple-element.19), channel_id=1, source_target_pairs={{4,0},{8,4},{12,8},{16,12},{20,16},{24,20},{28,24},{5,1},{9,5},{13... | collective-permute-start | bytes 393224 | tf_op jit(solution)/shard_map/ppermute | solution.py:20
  444.3 4.6 collective-permute-start.7
  447.5 5.2 %collective-permute-start.6 = (f32[34,1,512]{2,0,1:T(8,128)S(1)}, f32[34,1,512]{2,0,1:T(8,128)S(1)}, u32[]{:S(2)}, u32[]{:S(2)}) collective-permute-start(f32[34,1,512]{2,0,1:T(8,128)S(1)} %copy.13), channel_id=1, source_target_pairs={{1,0},{2,1},{3,2},{5,4},{6,5},{7,6},{9,8},{10,9},{11,10},{13,12},{... | collective-permute-start | bytes 208904 | tf_op jit(solution)/shard_map/ppermute | solution.py:20
Sparse Core Ops, SparseCore 0:
  22.9 354.1 all-reduce.5
where the time goes:
time: 481 us; the launch traced here: 477 us
  waiting for transfers between devices  370 us (77%)
  other arithmetic  64.8 us (13%)
  starting transfers between devices  19.7 us (4%)
  between operations  13.6 us (3%)
  local copies, waits for them, and re-layouts  9.1 us (2%)
    psum x1, waiting for transfers between devices, shards(): correlation, energy = lax.psum((correlation, energy), 'source')  353 us
    add x2, other arithmetic, diffuse(): return centre + smoothing_rate * flux_total  33.4 us
    ppermute x4, waiting for transfers between devices, with_halo(): after = lax.ppermute(leading, axis, down)  15.1 us
    reduce_sum x1, other arithmetic, shards(): jnp.sum(backward * backward, axis=1)  13.2 us
    ppermute x4, starting transfers between devices, with_halo(): before = lax.ppermute(last, axis, up)  11.3 us
  transfers between devices with their start and end apart: 9, of which 7 were waited for; matrix products, arithmetic and copies ran while one was open for 0% of the time, Pallas kernels for 0%

commit v1 on v0

v1 whole, which is shorter than its diff:
```python
import functools

import jax
import jax.numpy as jnp
import numpy as np
from jax import lax
from jax.experimental import pallas as pl
from jax.experimental.pallas import tpu as pltpu
from jax.sharding import PartitionSpec as P

smoothing_rate = 0.15
support_width = 0.3
floor_eps = 1e-06
mark_radius = 3
ROWS = 16
RIM = 2
PAD = 8

UP = [(4 * z + y, 4 * z + (y + 1) % 4) for z in range(2) for y in range(4)]
DOWN = [(j, i) for i, j in UP]
SWAP = [(4 * z + y, 4 * (1 - z) + y) for z in range(2) for y in range(4)]


def send(x, pairs):
    return lax.ppermute(x, "source", pairs)


def block_lists(tile_x, tile_y):
    groups = tile_y // ROWS
    every = [(p, g) for p in range(tile_x) for g in range(groups)]
    inner = [(p, g) for p, g in every if 4 <= p < tile_x - 4 and 0 < g < groups - 1]
    outer = [b for b in every if b not in inner]
    return [outer, inner]


def tables(blocks):
    arr = np.array(blocks, np.int32)
    return jnp.asarray(arr[:, 0]), jnp.asarray(arr[:, 1])


def vmem(n):
    return [pl.BlockSpec(memory_space=pltpu.VMEM)] * n


def smem(n):
    return [pl.BlockSpec(memory_space=pltpu.SMEM)] * n


def partials(source_grad, adjoint_grad, blocks, starts, count):
    planes, groups = tables(blocks)
    depth = source_grad.shape[-1]
    n = len(starts)

    def body(start_ref, plane_ref, group_ref, *refs):
        for k in range(n):
            f = refs[k][0, :, 0].astype(jnp.float32)
            b = refs[n + k][0, :, 0].astype(jnp.float32)
            out = refs[2 * n + k]
            out[0, 0] = f[0] * b[0] + f[1] * b[1] + f[2] * b[2]
            out[1, 0] = (f[0] * f[0] + f[1] * f[1] + f[2] * f[2]) * (b[0] * b[0] + b[1] * b[1] + b[2] * b[2])

    def spec(k):
        def index(i, start, plane, group):
            at = start[k] + i
            return 0, 0, plane[at], group[at], 0

        return pl.BlockSpec((1, 3, 1, ROWS, depth), index)

    return pl.pallas_call(
        body,
        grid_spec=pltpu.PrefetchScalarGridSpec(
            num_scalar_prefetch=3,
            grid=(count,),
            in_specs=[spec(k) for k in range(n)] * 2,
            out_specs=[pl.BlockSpec((2, 1, ROWS, depth), lambda i, *_: (0, i, 0, 0))] * n,
        ),
        out_shape=[jax.ShapeDtypeStruct((2, count, ROWS, depth), jnp.float32)] * n,
        compiler_params=pltpu.CompilerParams(vmem_limit_bytes=32 * 2**20),
        name="partials",
    )(jnp.stack(starts).astype(jnp.int32), planes, groups, *([source_grad] * n), *([adjoint_grad] * n))


def place(pieces, starts_ref, plane_ref, group_ref, ms_ref, g_ref):
    for k, piece in enumerate(pieces):

        def one(i, _, k=k, piece=piece):
            at = starts_ref[k] + i
            p, g = plane_ref[at], group_ref[at]
            rows = pl.multiple_of(g * ROWS, ROWS)
            g_ref[p + RIM, pl.ds(pl.multiple_of(PAD + rows, 8), ROWS), :] = (
                piece[i] * ms_ref[p, pl.ds(rows, ROWS), :]
            )
            return 0

        lax.fori_loop(0, piece.shape[0], one, 0, unroll=True)


def frame_kernel(n, starts, planes, groups, *refs):
    pieces, (ms, g, low, high) = refs[:n], refs[n:]
    rows = ms.shape[1]
    zero = jnp.zeros((PAD, g.shape[2]), jnp.float32)

    def clear(p, _):
        g[p, :PAD] = zero
        g[p, PAD + rows :] = zero
        return 0

    lax.fori_loop(0, g.shape[0], clear, 0)
    place(pieces, starts, planes, groups, ms, g)

    def rim(p, _):
        low[p] = g[p + RIM, PAD : PAD + RIM]
        high[p] = g[p + RIM, PAD + rows - RIM : PAD + rows]
        return 0

    lax.fori_loop(0, ms.shape[0], rim, 0)


def rim_kernel(g_in, before, after, g, low, high):
    planes = before.shape[0]
    rows = g.shape[1] - 2 * PAD

    def fill(p, _):
        g[p + RIM] = g_in[p + RIM]
        g[p + RIM, PAD - RIM : PAD] = before[p]
        g[p + RIM, PAD + rows : PAD + rows + RIM] = after[p]
        return 0

    lax.fori_loop(0, planes, fill, 0)
    low[...] = g[RIM : 2 * RIM]
    high[...] = g[planes : planes + RIM]


def neighbours(ref, p):
    here = ref[p]
    rows, depth = here.shape
    lane = lax.broadcasted_iota(jnp.int32, here.shape, 1)
    total = ref[p + 1] + ref[p - 1]
    total = total + pltpu.roll(here, 1, 0) + pltpu.roll(here, rows - 1, 0)
    total = total + jnp.where(lane == depth - 1, 0.0, pltpu.roll(here, depth - 1, 1))
    total = total + jnp.where(lane == 0, 0.0, pltpu.roll(here, 1, 1))
    return here, total


def coefficient_kernel(s, a, t):
    planes, rows = t.shape[:2]

    def one(p, _):
        here, total = neighbours(s, p)
        value = 1.0 - smoothing_rate * here * total
        a[p] = value
        return 0

    lax.fori_loop(1, planes + 2 * RIM - 1, one, 0)

    def two(p, _):
        here = s[p + RIM, PAD : PAD + rows]
        value = a[p + RIM, PAD : PAD + rows]
        t[p] = jnp.where(here > 0.0, value / jnp.where(here > 0.0, here, 1.0), 0.0)
        return 0

    lax.fori_loop(0, planes, two, 0)


def smooth_kernel(n, starts, planes, groups, *refs):
    pieces, (ms, s, a, t, low, high, g_in, out, g, g1) = refs[:n], refs[n:]
    count, rows = out.shape[:2]

    def copy(p, _):
        g[p + RIM] = g_in[p + RIM]
        return 0

    lax.fori_loop(0, count, copy, 0)
    place(pieces, starts, planes, groups, ms, g)
    g[:RIM] = low[...]
    g[count + RIM :] = high[...]

    def first(p, _):
        here, total = neighbours(g, p)
        w = s[p]
        g1[p] = a[p] * here + smoothing_rate * w * w * total
        return 0

    lax.fori_loop(1, count + 2 * RIM - 1, first, 0)

    def second(p, _):
        here, total = neighbours(g1, p + RIM)
        inside = slice(PAD, PAD + rows)
        out[p] = t[p] * here[inside] + smoothing_rate * s[p + RIM, PAD : PAD + rows] * total[inside]
        return 0

    lax.fori_loop(0, count, second, 0)


def halo(low, high, axis):
    size = lax.axis_size(axis)
    up = [(i, i + 1) for i in range(size - 1)]
    return lax.ppermute(high, axis, up), lax.ppermute(low, axis, [(j, i) for i, j in up])


def framed(array):
    before, after = halo(array[:, :RIM], array[:, -RIM:], "line")
    fill = jnp.zeros((array.shape[0], PAD - RIM, array.shape[2]), array.dtype)
    wide = jnp.concatenate([fill, before, array, after, fill], axis=1)
    before, after = halo(wide[:RIM], wide[-RIM:], "profile")
    return jnp.concatenate([before, wide, after], axis=0)


def shards(source_grad, adjoint_grad, log_model, surface_depth, source_columns, receiver_columns):
    tile_x, tile_y, depth_cells = log_model.shape
    me = lax.axis_index("source")
    y, half = me % 4, me // 4
    lists = block_lists(tile_x, tile_y)

    def start_of(blocks, offset, z):
        part = len(blocks) // 8
        return (2 * ((y + offset) % 4) + z) * part

    reduced = []
    for blocks in lists:
        part = len(blocks) // 8
        at = functools.partial(start_of, blocks)
        far0, far1 = partials(source_grad, adjoint_grad, blocks, [at(2, 0), at(2, 1)], part)
        near_up, near_down, keep_down, keep_up, own0, own1 = partials(
            source_grad, adjoint_grad, blocks, [at(1, 0), at(-1, 1), at(-1, 0), at(1, 1), at(0, 0), at(0, 1)], part
        )
        far0 = send(far0, DOWN)
        far1 = send(far1, UP)
        got0 = send(near_up, UP)
        got1 = send(near_down, DOWN)
        got0b = send(keep_down + far0, DOWN)
        got1b = send(keep_up + far1, UP)
        own0 = own0 + got0 + got0b
        own1 = own1 + got1 + got1b
        other = send(jnp.where(half == 0, own1, own0), SWAP)
        total = jnp.where(half == 0, own0, own1) + other
        reduced.append(total[0] * lax.rsqrt(total[1] + floor_eps))

    depth_index = lax.broadcasted_iota(jnp.int32, (tile_x, tile_y, depth_cells), 2)
    total_y = tile_y * lax.axis_size("line")
    columns = jnp.concatenate([source_columns, receiver_columns])
    electrode_x = columns // total_y
    electrode_y = columns % total_y
    global_x = lax.broadcasted_iota(jnp.int32, (1, tile_x), 1) + lax.axis_index("profile") * tile_x
    global_y = lax.broadcasted_iota(jnp.int32, (1, tile_y), 1) + lax.axis_index("line") * tile_y
    near_x = (jnp.abs(global_x - electrode_x[:, None]) <= mark_radius).astype(jnp.float32)
    near_y = (jnp.abs(global_y - electrode_y[:, None]) <= mark_radius).astype(jnp.float32)
    covered = jnp.einsum("ex,ey->xy", near_x, near_y, precision=lax.Precision.HIGHEST)
    threshold = surface_depth + jnp.where(covered > 0.5, depth_cells // 16, 0)
    root = support_width * lax.rsqrt(log_model * log_model + support_width * support_width)
    root = jnp.where(depth_index >= surface_depth[:, :, None], root, 0.0)
    masked = jnp.where(depth_index >= threshold[:, :, None], root, 0.0)
    s = framed(root)
    wide = jax.ShapeDtypeStruct(s.shape, jnp.float32)
    tile = jax.ShapeDtypeStruct(log_model.shape, jnp.float32)
    big = pltpu.CompilerParams(vmem_limit_bytes=56 * 2**20)
    a, t = pl.pallas_call(
        coefficient_kernel, out_shape=(wide, tile), in_specs=vmem(1), out_specs=vmem(2), compiler_params=big, name="coefficients"
    )(s)

    def ring(piece):
        cut = piece.shape[0] // 2
        below, above = send(piece, UP), send(piece, DOWN)
        return [piece, below, above, send(below[:cut], UP), send(above[cut:], DOWN)]

    def places(blocks, z):
        cut = len(blocks) // 16
        at = functools.partial(start_of, blocks)
        return [at(0, z), at(-1, z), at(1, z), at(2, z), at(2, z) + cut]

    gathered, starts = [], []
    for blocks, piece in zip(lists, reduced, strict=True):
        other = send(piece, SWAP)
        gathered.append(ring(piece) + ring(other))
        starts.append(jnp.stack(places(blocks, half) + places(blocks, 1 - half)).astype(jnp.int32))

    rim_y = jax.ShapeDtypeStruct((tile_x, RIM, depth_cells), jnp.float32)
    rim_x = jax.ShapeDtypeStruct((RIM,) + s.shape[1:], jnp.float32)
    n = len(gathered[0])
    g, low, high = pl.pallas_call(
        functools.partial(frame_kernel, n),
        out_shape=(wide, rim_y, rim_y),
        in_specs=smem(3) + vmem(n + 1),
        out_specs=vmem(3),
        compiler_params=big,
        name="frame",
    )(starts[0], *tables(lists[0]), *gathered[0], masked)
    before, after = halo(low, high, "line")
    g, low, high = pl.pallas_call(
        rim_kernel,
        out_shape=(wide, rim_x, rim_x),
        in_specs=vmem(3),
        out_specs=vmem(3),
        compiler_params=big,
        name="rims",
    )(g, before, after)
    low, high = halo(low, high, "profile")
    return pl.pallas_call(
        functools.partial(smooth_kernel, n),
        out_shape=tile,
        in_specs=smem(3) + vmem(n + 7),
        out_specs=pl.BlockSpec(memory_space=pltpu.VMEM),
        scratch_shapes=[pltpu.VMEM(s.shape, jnp.float32)] * 2,
        compiler_params=big,
        name="smooth",
    )(starts[1], *tables(lists[1]), *gathered[1], masked, s, a, t, low, high, g)


def solution(mesh):
    placed = (
        P("source", None, "profile", "line", None),
        P("source", None, "profile", "line", None),
        P("profile", "line", None),
        P("profile", "line"),
        P(),
        P(),
    )
    return jax.shard_map(
        shards, mesh=mesh, in_specs=placed, out_specs=P("profile", "line", None), check_vma=False
    )
```

time: 481 us -> 274 us (0.57)
  waiting for transfers between devices: 370 us -> 55.6 us
  starting transfers between devices: 19.7 us -> 83.7 us
  Pallas kernels: 0 us -> 63.6 us
  other arithmetic: 64.8 us -> 22.6 us
  local copies, waits for them, and re-layouts: 9.1 us -> 44.6 us
  between operations: 13.6 us -> 0.58 us
    psum x1 -> x0, waiting for transfers between devices: 353 us -> none  [shards(): correlation, energy = lax.psum((correlation, energy), 'source')]
    ppermute x8 -> x40, starting transfers between devices: 19.7 us -> 83.7 us  [the longest x32 55.7 us: send(): return lax.ppermute(x, 'source', pairs)]
    pallas_call x0 -> x8, Pallas kernels: none -> 63.6 us  [the longest x1 22.1 us: shards(): pl.pallas_call(functools.partial(smooth_kernel, n), out_shape=tile, in_sp...]
    ppermute x8 -> x40, waiting for transfers between devices: 16.4 us -> 55.6 us  [the longest x32 50.7 us: send(): return lax.ppermute(x, 'source', pairs)]
    unnamed x6 -> x82, local copies, waits for them, and re-layouts: 0.63 us -> 26 us
    add x3 -> x6, other arithmetic: 33.4 us -> 9.94 us  [the longest x2 3.52 us: shards(): total = jnp.where(half == 0, own0, own1) + other]
    reduce_sum x1 -> x0, other arithmetic: 13.2 us -> none  [shards(): jnp.sum(backward * backward, axis=1)]
    concatenate x0 -> x1, local copies, waits for them, and re-layouts: none -> 12.1 us  [framed(): wide = jnp.concatenate([fill, before, array, after, fill], axis=1)]
  transfers between devices with their start and end apart: 9 -> 40, of which waited for: 7 -> 5; matrix products, arithmetic and copies ran while one was open for 0% -> 15% of each run, Pallas kernels for 0% -> 14%
where the time goes in v1:
time: 274 us; the launch traced here: 271 us
  starting transfers between devices  83.7 us (31%)
  Pallas kernels  63.6 us (23%)
  waiting for transfers between devices  55.6 us (20%)
  local copies, waits for them, and re-layouts  44.6 us (16%)
  other arithmetic  22.6 us (8%)
    ppermute x32, starting transfers between devices, send(): return lax.ppermute(x, 'source', pairs)  55.7 us
    ppermute x32, waiting for transfers between devices, send(): return lax.ppermute(x, 'source', pairs)  50.7 us
    unnamed x82, local copies, waits for them, and re-layouts  26 us
    pallas_call x1, Pallas kernels, shards(): pl.pallas_call(functools.partial(smooth_kernel, n), out_shape=tile, in_sp...  22.1 us
    ppermute x4, starting transfers between devices, halo(): lax.ppermute(high, axis, up)  21.5 us
    pallas_call x4, Pallas kernels, partials(): pl.pallas_call(body, grid_spec=pltpu.PrefetchScalarGridSpec(num_scalar_pr...  16 us
    pallas_call x1, Pallas kernels, shards(): pl.pallas_call(coefficient_kernel, out_shape=(wide, tile), in_specs=vmem(...  12.9 us
    concatenate x1, local copies, waits for them, and re-layouts, framed(): wide = jnp.concatenate([fill, before, array, after, fill], axis=1)  12.1 us
  transfers between devices with their start and end apart: 40, of which 5 were waited for; matrix products, arithmetic and copies ran while one was open for 15% of the time, Pallas kernels for 14%

profile of v1, /device:TPU:33, one launch (start us, length us, event | category | flops | bytes accessed | tf_op | source)
XLA Modules:
  0.0 271.0 jit_solution(6098162242318528958)
XLA Ops:
  0.1 2.8 %copy-done = bf16[1,3,32,64,512]{4,3,2,1,0:T(8,128)(2,1)S(1)} copy-done((bf16[1,3,32,64,512]{4,3,2,1,0:T(8,128)(2,1)S(1)}, bf16[1,3,32,64,512]{4,3,2,1,0:T(8,128)(2,1)}, u32[]{:S(2)}) %copy-start) | copy-done | bytes 6291480
  2.9 2.8 %copy-done.4 = bf16[1,3,32,64,512]{4,3,2,1,0:T(8,128)(2,1)S(1)} copy-done((bf16[1,3,32,64,512]{4,3,2,1,0:T(8,128)(2,1)S(1)}, bf16[1,3,32,64,512]{4,3,2,1,0:T(8,128)(2,1)}, u32[]{:S(2)}) %copy-start.4) | copy-done | bytes 6291480
  7.0 4.4 %partials.7 = (f32[2,10,16,512]{3,2,1,0:T(8,128)}, f32[2,10,16,512]{3,2,1,0:T(8,128)S(1)}) custom-call(s32[2]{0:T(128)S(1)} %pad_add_fusion.2.start_ref, s32[80]{0:T(128)S(1)} %copy-done.10, s32[80]{0:T(128)S(1)} %copy-done.8, bf16[1,3,32,64,512]{4,3,2,1,0:T(8,128)(2,1)S(1)} %copy-done, bf16[1,3,32,64,512]{4,3,2,1,0:T(8,128)(2,1)S(1)} %copy-done, ...), custom_call_target="tpu_custom_call" | custom-call | tf_op jit(solution)/shard_map/partials/pallas_call | solution.py:69
  11.3 2.7 %collective-permute-start.21 = (f32[2,10,16,512]{3,2,1,0:T(8,128)}, f32[2,10,16,512]{3,2,1,0:T(8,128)}, u32[]{:S(2)}, u32[]{:S(2)}) collective-permute-start(f32[2,10,16,512]{3,2,1,0:T(8,128)} %get-tuple-element.42), channel_id=1, source_target_pairs={{32,0},{64,32},{96,64},{0,96},{160,128},{192,160},{224,192},{128,2... | collective-permute-start | bytes 1966088 | tf_op jit(solution)/shard_map/ppermute | solution.py:25
  14.2 2.8 %copy-done.1 = bf16[1,3,32,64,512]{4,3,2,1,0:T(8,128)(2,1)S(1)} copy-done((bf16[1,3,32,64,512]{4,3,2,1,0:T(8,128)(2,1)S(1)}, bf16[1,3,32,64,512]{4,3,2,1,0:T(8,128)(2,1)}, u32[]{:S(2)}) %copy-start.1) | copy-done | bytes 6291480
  16.9 2.8 %copy-done.5 = bf16[1,3,32,64,512]{4,3,2,1,0:T(8,128)(2,1)S(1)} copy-done((bf16[1,3,32,64,512]{4,3,2,1,0:T(8,128)(2,1)S(1)}, bf16[1,3,32,64,512]{4,3,2,1,0:T(8,128)(2,1)}, u32[]{:S(2)}) %copy-start.5) | copy-done | bytes 6291480
  19.7 2.9 %partials.5 = (f32[2,6,16,512]{3,2,1,0:T(8,128)S(1)}, f32[2,6,16,512]{3,2,1,0:T(8,128)}) custom-call(s32[2]{0:T(128)S(1)} %pad_add_fusion.1.start_ref, s32[48]{0:T(128)S(1)} %copy-done.13, s32[48]{0:T(128)S(1)} %copy-done.12, bf16[1,3,32,64,512]{4,3,2,1,0:T(8,128)(2,1)S(1)} %copy-done.1, bf16[1,3,32,64,512]{4,3,2,1,0:T(8,128)(2,1)S(1)} %copy-done.1, ...), custom_call_target="tpu_custom_call" | custom-call | tf_op jit(solution)/shard_map/partials/pallas_call | solution.py:69
  23.5 2.8 %copy-done.2 = bf16[1,3,32,64,512]{4,3,2,1,0:T(8,128)(2,1)S(1)} copy-done((bf16[1,3,32,64,512]{4,3,2,1,0:T(8,128)(2,1)S(1)}, bf16[1,3,32,64,512]{4,3,2,1,0:T(8,128)(2,1)}, u32[]{:S(2)}) %copy-start.2) | copy-done | bytes 6291480
  26.3 2.8 %copy-done.6 = bf16[1,3,32,64,512]{4,3,2,1,0:T(8,128)(2,1)S(1)} copy-done((bf16[1,3,32,64,512]{4,3,2,1,0:T(8,128)(2,1)S(1)}, bf16[1,3,32,64,512]{4,3,2,1,0:T(8,128)(2,1)}, u32[]{:S(2)}) %copy-start.6) | copy-done | bytes 6291480
  29.1 5.3 %partials.6 = (f32[2,10,16,512]{3,2,1,0:T(8,128)S(1)}, f32[2,10,16,512]{3,2,1,0:T(8,128)S(1)}, f32[2,10,16,512]{3,2,1,0:T(8,128)S(1)}, f32[2,10,16,512]{3,2,1,0:...) custom-call(s32[6]{0:T(128)S(1)} %stack.164.start_ref, s32[80]{0:T(128)S(1)} %copy-done.11, ...), custom_call_target="tpu_custom_call" | custom-call | tf_op jit(solution)/shard_map/partials/pallas_call | solution.py:69
  34.4 1.4 collective-permute-start.20
  35.7 1.4 collective-permute-start.23
  37.2 2.1 add.291
  39.2 1.5 collective-permute-start.22
  40.7 2.1 add.294
  42.8 2.7 collective-permute-start.1
  45.5 2.8 %copy-done.3 = bf16[1,3,32,64,512]{4,3,2,1,0:T(8,128)(2,1)S(1)} copy-done((bf16[1,3,32,64,512]{4,3,2,1,0:T(8,128)(2,1)S(1)}, bf16[1,3,32,64,512]{4,3,2,1,0:T(8,128)(2,1)}, u32[]{:S(2)}) %copy-start.3) | copy-done | bytes 6291480
  48.3 2.8 %copy-done.7 = bf16[1,3,32,64,512]{4,3,2,1,0:T(8,128)(2,1)S(1)} copy-done((bf16[1,3,32,64,512]{4,3,2,1,0:T(8,128)(2,1)S(1)}, bf16[1,3,32,64,512]{4,3,2,1,0:T(8,128)(2,1)}, u32[]{:S(2)}) %copy-start.7) | copy-done | bytes 6291480
  51.1 3.5 %partials.4 = (f32[2,6,16,512]{3,2,1,0:T(8,128)S(1)}, f32[2,6,16,512]{3,2,1,0:T(8,128)S(1)}, f32[2,6,16,512]{3,2,1,0:T(8,128)S(1)}, f32[2,6,16,512]{3,2,1,0:T(8,...) custom-call(s32[6]{0:T(128)S(1)} %stack.143.start_ref, s32[48]{0:T(128)S(1)} %copy-done.13, ...), custom_call_target="tpu_custom_call" | custom-call | tf_op jit(solution)/shard_map/partials/pallas_call | solution.py:69
  55.0 1.3 add.275
  56.3 17.5 %collective-permute-done.1 = f32[2,6,16,512]{3,2,1,0:T(8,128)} collective-permute-done((f32[2,6,16,512]{3,2,1,0:T(8,128)}, f32[2,6,16,512]{3,2,1,0:T(8,128)}, u32[]{:S(2)}, u32[]{:S(2)}) %collective-permute-start.1) | collective-permute-done | bytes 393248 | tf_op jit(solution)/shard_map/ppermute | solution.py:25
  73.8 1.2 collective-permute-start
  75.0 1.0 add.272
  76.0 1.6 collective-permute-start.3
  78.1 1.0 collective-permute-start.5
  79.1 2.1 broadcast_select_fusion
  81.2 6.3 %collective-permute-start.26 = (f32[2,10,16,512]{3,2,1,0:T(8,128)S(1)}, f32[2,10,16,512]{3,2,1,0:T(8,128)S(1)}, u32[]{:S(2)}, u32[]{:S(2)}) collective-permute-start(f32[2,10,16,512]{3,2,1,0:T(8,128)S(1)} %broadcast_select_fusion), channel_id=1, source_target_pairs={{0,128},{32,160},{64,192},{96,224},{128,0},{160,32},{192,64},{224,... | collective-permute-start | bytes 1966088 | tf_op jit(solution)/shard_map/ppermute | solution.py:25
  87.5 3.0 %fusion = (f32[32,64,512]{2,1,0:T(8,128)}, f32[32,64,512]{2,1,0:T(8,128)S(1)}) fusion(s32[32,64]{1,0:T(8,128)S(1)} %fusion.2, f32[32,64,512]{2,1,0:T(8,128)S(1)} %copy-done.16, s32[32,64]{1,0:T(8,128)S(1)} %copy-done.38), kind=kLoop, calls=%fused_computation.4 | loop fusion | flops 7340032 | bytes 12599296 | tf_op jit(solution)/shard_map/jit(_where)/select_n | solution.py:252
  90.5 1.6 collective-permute-done.2
  92.1 1.0 broadcast_select_fusion.1
  93.1 6.0 %collective-permute-start.6 = (f32[2,6,16,512]{3,2,1,0:T(8,128)}, f32[2,6,16,512]{3,2,1,0:T(8,128)}, u32[]{:S(2)}, u32[]{:S(2)}) collective-permute-start(f32[2,6,16,512]{3,2,1,0:T(8,128)} %broadcast_select_fusion.1), channel_id=1, source_target_pairs={{0,128},{32,160},{64,192},{96,224},{128,0},{160,32},{192,64},{224,... | collective-permute-start | bytes 1179656 | tf_op jit(solution)/shard_map/ppermute | solution.py:25
  99.2 16.9 %collective-permute-done.26 = f32[2,10,16,512]{3,2,1,0:T(8,128)S(1)} collective-permute-done((f32[2,10,16,512]{3,2,1,0:T(8,128)S(1)}, f32[2,10,16,512]{3,2,1,0:T(8,128)S(1)}, u32[]{:S(2)}, u32[]{:S(2)}) %collective-permute-start.26) | collective-permute-done | bytes 655392 | tf_op jit(solution)/shard_map/ppermute | solution.py:25
  116.0 2.2 select_add_fusion
  118.3 5.5 %collective-permute-start.31 = (f32[10,16,512]{2,1,0:T(8,128)S(1)}, f32[10,16,512]{2,1,0:T(8,128)}, u32[]{:S(2)}, u32[]{:S(2)}) collective-permute-start(f32[10,16,512]{2,1,0:T(8,128)S(1)} %fusion.5.refs_0_), channel_id=1, source_target_pairs={{0,128},{32,160},{64,192},{96,224},{128,0},{160,32},{192,64},{224,... | collective-permute-start | bytes 983048 | tf_op jit(solution)/shard_map/ppermute | solution.py:25
  123.9 1.3 collective-permute-start.17
  125.2 4.0 %collective-permute-start.16 = (f32[32,2,512]{2,1,0:T(2,128)S(1)}, f32[32,2,512]{2,1,0:T(2,128)S(1)}, u32[]{:S(2)}, u32[]{:S(2)}) collective-permute-start(f32[32,2,512]{2,1,0:T(2,128)S(1)} %get-tuple-element.58), channel_id=1, source_target_pairs={{0,1},{1,2},{2,3},{4,5},{5,6},{6,7},{8,9},{9,10},{10,11},{12,13},{... | collective-permute-start | bytes 393224 | tf_op jit(solution)/shard_map/ppermute | solution.py:198
  129.2 1.8 collective-permute-start.28
  131.0 14.7 %collective-permute-done.31.refs_5_ = f32[10,16,512]{2,1,0:T(8,128)} collective-permute-done((f32[10,16,512]{2,1,0:T(8,128)S(1)}, f32[10,16,512]{2,1,0:T(8,128)}, u32[]{:S(2)}, u32[]{:S(2)}) %collective-permute-start.31) | collective-permute-done | bytes 327712 | tf_op jit(solution)/shard_map/ppermute | solution.py:25
  145.7 1.7 collective-permute-start.33
  148.2 12.1 %concatenate.33 = f32[32,80,512]{2,1,0:T(8,128)} concatenate(f32[32,6,512]{2,1,0:T(8,128)S(1)} %broadcast_in_dim.23, f32[32,2,512]{2,1,0:T(2,128)S(1)} %collective-permute-done.16, f32[32,64,512]{2,1,0:T(8,128)} %copy-done.15, f32[32,2,512]{2,1,0:T(2,128)S(1)} %collective-permute-done.17, f32[32,6,512]{2,1,0:T(8,128)S(1)} %broadcast_in_dim.23), dimensions={1} | concatenate | bytes 10485760 | tf_op jit(solution)/shard_map/concatenate | solution.py:204
  160.2 1.3 select_add_fusion.1
  161.6 0.9 slice.77
  162.5 2.7 %collective-permute-start.30 = (f32[5,16,512]{2,1,0:T(8,128)S(1)}, f32[5,16,512]{2,1,0:T(8,128)S(1)}, u32[]{:S(2)}, u32[]{:S(2)}) collective-permute-start(f32[5,16,512]{2,1,0:T(8,128)S(1)} %slice.77), channel_id=1, source_target_pairs={{32,0},{64,32},{96,64},{0,96},{160,128},{192,160},{224,192},{128,2... | collective-permute-start | bytes 491528 | tf_op jit(solution)/shard_map/ppermute | solution.py:25
  165.2 0.9 slice.76
  166.3 0.9 slice.79
  167.2 2.7 %collective-permute-start.35 = (f32[5,16,512]{2,1,0:T(8,128)S(1)}, f32[5,16,512]{2,1,0:T(8,128)S(1)}, u32[]{:S(2)}, u32[]{:S(2)}) collective-permute-start(f32[5,16,512]{2,1,0:T(8,128)S(1)} %slice.79), channel_id=1, source_target_pairs={{32,0},{64,32},{96,64},{0,96},{160,128},{192,160},{224,192},{128,2... | collective-permute-start | bytes 491528 | tf_op jit(solution)/shard_map/ppermute | solution.py:25
  171.0 5.6 %collective-permute-start.11 = (f32[6,16,512]{2,1,0:T(8,128)S(1)}, f32[6,16,512]{2,1,0:T(8,128)S(1)}, u32[]{:S(2)}, u32[]{:S(2)}) collective-permute-start(f32[6,16,512]{2,1,0:T(8,128)S(1)} %fusion.8.refs_0_), channel_id=1, source_target_pairs={{0,128},{32,160},{64,192},{96,224},{128,0},{160,32},{192,64},{224,... | collective-permute-start | bytes 589832 | tf_op jit(solution)/shard_map/ppermute | solution.py:25
  176.6 2.7 collective-permute-start.8
  180.0 6.5 %frame.1 = (f32[36,80,512]{2,1,0:T(8,128)}, f32[32,2,512]{2,1,0:T(2,128)}, f32[32,2,512]{2,1,0:T(2,128)}) custom-call(s32[10]{0:T(128)} %stack.157.starts, s32[80]{0:T(128)} %constant.191.clone.plane_ref.planes, s32[80]{0:T(128)} %constant.192.clone.group_ref.groups, f32[10,16,512]{2,1,0:T(8,128)} %copy-done.19, ...), custom_call_target="tpu_custom_call" | custom-call | tf_op jit(solution)/shard_map/frame/pallas_call | solution.py:280
  186.5 3.3 %collective-permute-start.36 = (f32[32,2,512]{2,1,0:T(2,128)}, f32[32,2,512]{2,1,0:T(2,128)S(1)}, u32[]{:S(2)}, u32[]{:S(2)}) collective-permute-start(f32[32,2,512]{2,1,0:T(2,128)} %get-tuple-element.48), channel_id=1, source_target_pairs={{0,1},{1,2},{2,3},{4,5},{5,6},{6,7},{8,9},{9,10},{10,11},{12,13},{... | collective-permute-start | bytes 393224 | tf_op jit(solution)/shard_map/ppermute | solution.py:198
  189.9 1.1 fusion.17
  191.0 8.6 %collective-permute-start.18 = (f32[2,80,512]{2,1,0:T(8,128)S(1)}, f32[2,80,512]{2,1,0:T(8,128)S(1)}, u32[]{:S(2)}, u32[]{:S(2)}) collective-permute-start(f32[2,80,512]{2,1,0:T(8,128)S(1)} %get-tuple-element.55), channel_id=1, source_target_pairs={{0,4},{4,8},{8,12},{12,16},{16,20},{20,24},{24,28},{1,5},{5,9},{9,... | collective-permute-start | bytes 983048 | tf_op jit(solution)/shard_map/ppermute | solution.py:198
  199.6 1.9 collective-permute-start.19
  201.5 1.5 collective-permute-start.13
  203.1 1.3 collective-permute-start.37
  204.4 4.9 %collective-permute-done.37.after = f32[32,2,512]{2,1,0:T(2,128)S(1)} collective-permute-done((f32[32,2,512]{2,1,0:T(2,128)}, f32[32,2,512]{2,1,0:T(2,128)S(1)}, u32[]{:S(2)}, u32[]{:S(2)}) %collective-permute-start.37) | collective-permute-done | bytes 131104 | tf_op jit(solution)/shard_map/ppermute | solution.py:198
  209.3 2.3 collective-permute-start.10
  211.7 6.0 %rims.1 = (f32[36,80,512]{2,1,0:T(8,128)}, f32[2,80,512]{2,1,0:T(8,128)}, f32[2,80,512]{2,1,0:T(8,128)}) custom-call(f32[36,80,512]{2,1,0:T(8,128)} %get-tuple-element.47.g_in, f32[32,2,512]{2,1,0:T(2,128)} %copy-done.32, f32[32,2,512]{2,1,0:T(2,128)} %copy-done.33), custom_call_target="tpu_custom_call" | custom-call | tf_op jit(solution)/shard_map/rims/pallas_call | solution.py:289
  217.7 5.6 %collective-permute-start.38 = (f32[2,80,512]{2,1,0:T(8,128)}, f32[2,80,512]{2,1,0:T(8,128)S(1)}, u32[]{:S(2)}, u32[]{:S(2)}) collective-permute-start(f32[2,80,512]{2,1,0:T(8,128)} %get-tuple-element.50), channel_id=1, source_target_pairs={{0,4},{4,8},{8,12},{12,16},{16,20},{20,24},{24,28},{1,5},{5,9},{9,... | collective-permute-start | bytes 983048 | tf_op jit(solution)/shard_map/ppermute | solution.py:198
  223.4 1.9 collective-permute-start.39
  226.1 2.7 collective-permute-start.15
  228.8 6.2 %pad_maximum_fusion.s.refs_11_ = f32[36,80,512]{2,1,0:T(8,128)} fusion(f32[2,80,512]{2,1,0:T(8,128)S(1)} %collective-permute-done.19, f32[32,80,512]{2,1,0:T(8,128)} %concatenate.33, f32[2,80,512]{2,1,0:T(8,128)S(1)} %collective-permute-done.18), kind=kLoop, calls=%fused_computation | loop fusion | flops 2949120 | bytes 11796480 | tf_op jit(solution)/shard_map/concatenate | solution.py:206
  235.0 12.9 %coefficients.1 = (f32[36,80,512]{2,1,0:T(8,128)}, f32[32,64,512]{2,1,0:T(8,128)}) custom-call(f32[36,80,512]{2,1,0:T(8,128)} %pad_maximum_fusion.s.refs_11_), custom_call_target="tpu_custom_call" | custom-call | tf_op jit(solution)/shard_map/coefficients/pallas_call | solution.py:257
  248.9 22.1 %smooth.1 = f32[32,64,512]{2,1,0:T(8,128)} custom-call(s32[10]{0:T(128)} %stack.136.starts, s32[48]{0:T(128)} %constant.193.clone.plane_ref.planes, s32[48]{0:T(128)} %constant.194.clone.group_ref.groups, f32[6,16,512]{2,1,0:T(8,128)} %copy-done.20, f32[6,16,512]{2,1,0:T(8,128)} %copy-done.22, f32[6,16,512]{2,1,0:T(8,128)} %copy-done.21, ...), custom_call_target="tpu_custom_call" | custom-call | tf_op jit(solution)/shard_map/smooth/pallas_call | solution.py:298
  (140 shorter events, 7.9 us)
Async XLA Ops:
  0.1 2.8 %copy-start = (bf16[1,3,32,64,512]{4,3,2,1,0:T(8,128)(2,1)S(1)}, bf16[1,3,32,64,512]{4,3,2,1,0:T(8,128)(2,1)}, u32[]{:S(2)}) copy-start(bf16[1,3,32,64,512]{4,3,2,1,0:T(8,128)(2,1)} %refs_1_.7) | copy-start | bytes 18874372
  7.0 7.2 %copy-start.12 = (s32[48]{0:T(128)S(1)}, s32[48]{0:T(128)}, u32[]{:S(2)}) copy-start(s32[48]{0:T(128)} %constant.194.clone.group_ref.groups) | copy-start | bytes 580
  7.0 7.2 %copy-start.13 = (s32[48]{0:T(128)S(1)}, s32[48]{0:T(128)}, u32[]{:S(2)}) copy-start(s32[48]{0:T(128)} %constant.193.clone.plane_ref.planes) | copy-start | bytes 580
  11.3 25.9 %collective-permute-start.21 = (f32[2,10,16,512]{3,2,1,0:T(8,128)}, f32[2,10,16,512]{3,2,1,0:T(8,128)}, u32[]{:S(2)}, u32[]{:S(2)}) collective-permute-start(f32[2,10,16,512]{3,2,1,0:T(8,128)} %get-tuple-element.42), channel_id=1, source_target_pairs={{32,0},{64,32},{96,64},{0,96},{160,128},{192,160},{224,192},{128,2... | collective-permute-start | bytes 1966088 | tf_op jit(solution)/shard_map/ppermute | solution.py:25
  14.1 26.6 %collective-permute-start.24 = (f32[2,10,16,512]{3,2,1,0:T(8,128)S(1)}, f32[2,10,16,512]{3,2,1,0:T(8,128)}, u32[]{:S(2)}, u32[]{:S(2)}) collective-permute-start(f32[2,10,16,512]{3,2,1,0:T(8,128)S(1)} %get-tuple-element.46), channel_id=1, source_target_pairs={{0,32},{32,64},{64,96},{96,0},{128,160},{160,192},{192,224},{224,1... | collective-permute-start | bytes 1966088 | tf_op jit(solution)/shard_map/ppermute | solution.py:25
  14.2 2.8 %copy-start.1 = (bf16[1,3,32,64,512]{4,3,2,1,0:T(8,128)(2,1)S(1)}, bf16[1,3,32,64,512]{4,3,2,1,0:T(8,128)(2,1)}, u32[]{:S(2)}) copy-start(bf16[1,3,32,64,512]{4,3,2,1,0:T(8,128)(2,1)} %refs_1_.7) | copy-start | bytes 18874372
  19.7 3.8 %copy-start.9 = (s32[80]{0:T(128)S(1)}, s32[80]{0:T(128)}, u32[]{:S(2)}) copy-start(s32[80]{0:T(128)} %constant.192.clone.group_ref.groups) | copy-start | bytes 964
  19.7 3.8 %copy-start.11 = (s32[80]{0:T(128)S(1)}, s32[80]{0:T(128)}, u32[]{:S(2)}) copy-start(s32[80]{0:T(128)} %constant.191.clone.plane_ref.planes) | copy-start | bytes 964
  23.4 19.4 %collective-permute-start.4 = (f32[2,6,16,512]{3,2,1,0:T(8,128)}, f32[2,6,16,512]{3,2,1,0:T(8,128)}, u32[]{:S(2)}, u32[]{:S(2)}) collective-permute-start(f32[2,6,16,512]{3,2,1,0:T(8,128)} %get-tuple-element.36), channel_id=1, source_target_pairs={{0,32},{32,64},{64,96},{96,0},{128,160},{160,192},{192,224},{224,1... | collective-permute-start | bytes 1179656 | tf_op jit(solution)/shard_map/ppermute | solution.py:25
  23.5 2.8 %copy-start.2 = (bf16[1,3,32,64,512]{4,3,2,1,0:T(8,128)(2,1)S(1)}, bf16[1,3,32,64,512]{4,3,2,1,0:T(8,128)(2,1)}, u32[]{:S(2)}) copy-start(bf16[1,3,32,64,512]{4,3,2,1,0:T(8,128)(2,1)} %refs_1_.7) | copy-start | bytes 18874372
  34.4 41.6 %collective-permute-start.20 = (f32[2,10,16,512]{3,2,1,0:T(8,128)S(1)}, f32[2,10,16,512]{3,2,1,0:T(8,128)}, u32[]{:S(2)}, u32[]{:S(2)}) collective-permute-start(f32[2,10,16,512]{3,2,1,0:T(8,128)S(1)} %get-tuple-element.40), channel_id=1, source_target_pairs={{0,32},{32,64},{64,96},{96,0},{128,160},{160,192},{192,224},{224,1... | collective-permute-start | bytes 1966088 | tf_op jit(solution)/shard_map/ppermute | solution.py:25
  35.7 41.9 %collective-permute-start.23 = (f32[2,10,16,512]{3,2,1,0:T(8,128)S(1)}, f32[2,10,16,512]{3,2,1,0:T(8,128)}, u32[]{:S(2)}, u32[]{:S(2)}) collective-permute-start(f32[2,10,16,512]{3,2,1,0:T(8,128)S(1)} %get-tuple-element.44), channel_id=1, source_target_pairs={{32,0},{64,32},{96,64},{0,96},{160,128},{192,160},{224,192},{128,2... | collective-permute-start | bytes 1966088 | tf_op jit(solution)/shard_map/ppermute | solution.py:25
  39.2 38.8 %collective-permute-start.22 = (f32[2,10,16,512]{3,2,1,0:T(8,128)}, f32[2,10,16,512]{3,2,1,0:T(8,128)}, u32[]{:S(2)}, u32[]{:S(2)}) collective-permute-start(f32[2,10,16,512]{3,2,1,0:T(8,128)} %add.291), channel_id=1, source_target_pairs={{32,0},{64,32},{96,64},{0,96},{160,128},{192,160},{224,192},{128,2... | collective-permute-start | bytes 1966088 | tf_op jit(solution)/shard_map/ppermute | solution.py:25
  42.8 36.3 %collective-permute-start.25 = (f32[2,10,16,512]{3,2,1,0:T(8,128)}, f32[2,10,16,512]{3,2,1,0:T(8,128)}, u32[]{:S(2)}, u32[]{:S(2)}) collective-permute-start(f32[2,10,16,512]{3,2,1,0:T(8,128)} %add.294), channel_id=1, source_target_pairs={{0,32},{32,64},{64,96},{96,0},{128,160},{160,192},{192,224},{224,1... | collective-permute-start | bytes 1966088 | tf_op jit(solution)/shard_map/ppermute | solution.py:25
  42.8 31.0 %collective-permute-start.1 = (f32[2,6,16,512]{3,2,1,0:T(8,128)}, f32[2,6,16,512]{3,2,1,0:T(8,128)}, u32[]{:S(2)}, u32[]{:S(2)}) collective-permute-start(f32[2,6,16,512]{3,2,1,0:T(8,128)} %copy-done.14), channel_id=1, source_target_pairs={{32,0},{64,32},{96,64},{0,96},{160,128},{192,160},{224,192},{128,2... | collective-permute-start | bytes 1179656 | tf_op jit(solution)/shard_map/ppermute | solution.py:25
  45.5 2.8 %copy-start.3 = (bf16[1,3,32,64,512]{4,3,2,1,0:T(8,128)(2,1)S(1)}, bf16[1,3,32,64,512]{4,3,2,1,0:T(8,128)(2,1)}, u32[]{:S(2)}) copy-start(bf16[1,3,32,64,512]{4,3,2,1,0:T(8,128)(2,1)} %refs_1_.7) | copy-start | bytes 18874372
  51.1 3.5 %copy-start.39 = (s32[256]{0:T(256)S(1)}, s32[256]{0:T(256)}, u32[]{:S(2)}) copy-start(s32[256]{0:T(256)} %param.23) | copy-start | bytes 3076
  51.1 3.5 %copy-start.40 = (s32[8]{0:T(128)S(1)}, s32[8]{0:T(128)}, u32[]{:S(2)}) copy-start(s32[8]{0:T(128)} %param.22) | copy-start | bytes 100
  51.1 3.6 %copy-start.38 = (s32[32,64]{1,0:T(8,128)S(1)}, s32[32,64]{1,0:T(8,128)}, u32[]{:S(2)}) copy-start(s32[32,64]{1,0:T(8,128)} %param.21) | copy-start | bytes 24580
  54.6 32.9 %copy-start.16 = (f32[32,64,512]{2,1,0:T(8,128)S(1)}, f32[32,64,512]{2,1,0:T(8,128)}, u32[]{:S(2)}) copy-start(f32[32,64,512]{2,1,0:T(8,128)} %param.20) | copy-start | bytes 12582916
  73.8 16.8 %collective-permute-start = (f32[2,6,16,512]{3,2,1,0:T(8,128)S(1)}, f32[2,6,16,512]{3,2,1,0:T(8,128)S(1)}, u32[]{:S(2)}, u32[]{:S(2)}) collective-permute-start(f32[2,6,16,512]{3,2,1,0:T(8,128)S(1)} %get-tuple-element.30), channel_id=1, source_target_pairs={{0,32},{32,64},{64,96},{96,0},{128,160},{160,192},{192,224},{224,1... | collective-permute-start | bytes 1179656 | tf_op jit(solution)/shard_map/ppermute | solution.py:25
  76.0 14.5 %collective-permute-start.3 = (f32[2,6,16,512]{3,2,1,0:T(8,128)S(1)}, f32[2,6,16,512]{3,2,1,0:T(8,128)S(1)}, u32[]{:S(2)}, u32[]{:S(2)}) collective-permute-start(f32[2,6,16,512]{3,2,1,0:T(8,128)S(1)} %get-tuple-element.34), channel_id=1, source_target_pairs={{32,0},{64,32},{96,64},{0,96},{160,128},{192,160},{224,192},{128,2... | collective-permute-start | bytes 1179656 | tf_op jit(solution)/shard_map/ppermute | solution.py:25
  77.6 14.5 %collective-permute-start.2 = (f32[2,6,16,512]{3,2,1,0:T(8,128)S(1)}, f32[2,6,16,512]{3,2,1,0:T(8,128)S(1)}, u32[]{:S(2)}, u32[]{:S(2)}) collective-permute-start(f32[2,6,16,512]{3,2,1,0:T(8,128)S(1)} %add.272), channel_id=1, source_target_pairs={{32,0},{64,32},{96,64},{0,96},{160,128},{192,160},{224,192},{128,2... | collective-permute-start | bytes 1179656 | tf_op jit(solution)/shard_map/ppermute | solution.py:25
  78.1 14.1 %collective-permute-start.5 = (f32[2,6,16,512]{3,2,1,0:T(8,128)S(1)}, f32[2,6,16,512]{3,2,1,0:T(8,128)S(1)}, u32[]{:S(2)}, u32[]{:S(2)}) collective-permute-start(f32[2,6,16,512]{3,2,1,0:T(8,128)S(1)} %add.275), channel_id=1, source_target_pairs={{0,32},{32,64},{64,96},{96,0},{128,160},{160,192},{192,224},{224,1... | collective-permute-start | bytes 1179656 | tf_op jit(solution)/shard_map/ppermute | solution.py:25
  81.2 34.8 %collective-permute-start.26 = (f32[2,10,16,512]{3,2,1,0:T(8,128)S(1)}, f32[2,10,16,512]{3,2,1,0:T(8,128)S(1)}, u32[]{:S(2)}, u32[]{:S(2)}) collective-permute-start(f32[2,10,16,512]{3,2,1,0:T(8,128)S(1)} %broadcast_select_fusion), channel_id=1, source_target_pairs={{0,128},{32,160},{64,192},{96,224},{128,0},{160,32},{192,64},{224,... | collective-permute-start | bytes 1966088 | tf_op jit(solution)/shard_map/ppermute | solution.py:25
  90.5 33.3 %copy-start.15 = (f32[32,64,512]{2,1,0:T(8,128)}, f32[32,64,512]{2,1,0:T(8,128)S(1)}, u32[]{:S(2)}) copy-start(f32[32,64,512]{2,1,0:T(8,128)S(1)} %get-tuple-element.54) | copy-start | bytes 12582916
  90.5 27.8 %copy-start.17 = (f32[2,6,16,512]{3,2,1,0:T(8,128)}, f32[2,6,16,512]{3,2,1,0:T(8,128)S(1)}, u32[]{:S(2)}) copy-start(f32[2,6,16,512]{3,2,1,0:T(8,128)S(1)} %collective-permute-done) | copy-start | bytes 1179652
  93.1 67.1 %collective-permute-start.6 = (f32[2,6,16,512]{3,2,1,0:T(8,128)}, f32[2,6,16,512]{3,2,1,0:T(8,128)}, u32[]{:S(2)}, u32[]{:S(2)}) collective-permute-start(f32[2,6,16,512]{3,2,1,0:T(8,128)} %broadcast_select_fusion.1), channel_id=1, source_target_pairs={{0,128},{32,160},{64,192},{96,224},{128,0},{160,32},{192,64},{224,... | collective-permute-start | bytes 1179656 | tf_op jit(solution)/shard_map/ppermute | solution.py:25
  118.3 41.9 %copy-start.19 = (f32[10,16,512]{2,1,0:T(8,128)}, f32[10,16,512]{2,1,0:T(8,128)S(1)}, u32[]{:S(2)}) copy-start(f32[10,16,512]{2,1,0:T(8,128)S(1)} %fusion.5.refs_0_) | copy-start | bytes 983044
  118.3 27.4 %collective-permute-start.31 = (f32[10,16,512]{2,1,0:T(8,128)S(1)}, f32[10,16,512]{2,1,0:T(8,128)}, u32[]{:S(2)}, u32[]{:S(2)}) collective-permute-start(f32[10,16,512]{2,1,0:T(8,128)S(1)} %fusion.5.refs_0_), channel_id=1, source_target_pairs={{0,128},{32,160},{64,192},{96,224},{128,0},{160,32},{192,64},{224,... | collective-permute-start | bytes 983048 | tf_op jit(solution)/shard_map/ppermute | solution.py:25
  123.9 7.1 %collective-permute-start.17 = (f32[32,2,512]{2,1,0:T(2,128)S(1)}, f32[32,2,512]{2,1,0:T(2,128)S(1)}, u32[]{:S(2)}, u32[]{:S(2)}) collective-permute-start(f32[32,2,512]{2,1,0:T(2,128)S(1)} %get-tuple-element.57), channel_id=1, source_target_pairs={{1,0},{2,1},{3,2},{5,4},{6,5},{7,6},{9,8},{10,9},{11,10},{13,12},{... | collective-permute-start | bytes 393224 | tf_op jit(solution)/shard_map/ppermute | solution.py:198
  125.2 22.2 %collective-permute-start.16 = (f32[32,2,512]{2,1,0:T(2,128)S(1)}, f32[32,2,512]{2,1,0:T(2,128)S(1)}, u32[]{:S(2)}, u32[]{:S(2)}) collective-permute-start(f32[32,2,512]{2,1,0:T(2,128)S(1)} %get-tuple-element.58), channel_id=1, source_target_pairs={{0,1},{1,2},{2,3},{4,5},{5,6},{6,7},{8,9},{9,10},{10,11},{12,13},{... | collective-permute-start | bytes 393224 | tf_op jit(solution)/shard_map/ppermute | solution.py:198
  129.2 32.3 %collective-permute-start.28 = (f32[10,16,512]{2,1,0:T(8,128)S(1)}, f32[10,16,512]{2,1,0:T(8,128)}, u32[]{:S(2)}, u32[]{:S(2)}) collective-permute-start(f32[10,16,512]{2,1,0:T(8,128)S(1)} %fusion.5.refs_0_), channel_id=1, source_target_pairs={{32,0},{64,32},{96,64},{0,96},{160,128},{192,160},{224,192},{128,2... | collective-permute-start | bytes 983048 | tf_op jit(solution)/shard_map/ppermute | solution.py:25
  131.0 34.2 %collective-permute-start.27 = (f32[10,16,512]{2,1,0:T(8,128)S(1)}, f32[10,16,512]{2,1,0:T(8,128)}, u32[]{:S(2)}, u32[]{:S(2)}) collective-permute-start(f32[10,16,512]{2,1,0:T(8,128)S(1)} %fusion.5.refs_0_), channel_id=1, source_target_pairs={{0,32},{32,64},{64,96},{96,0},{128,160},{160,192},{192,224},{224,1... | collective-permute-start | bytes 983048 | tf_op jit(solution)/shard_map/ppermute | solution.py:25
  145.7 20.5 %collective-permute-start.33 = (f32[10,16,512]{2,1,0:T(8,128)}, f32[10,16,512]{2,1,0:T(8,128)}, u32[]{:S(2)}, u32[]{:S(2)}) collective-permute-start(f32[10,16,512]{2,1,0:T(8,128)} %collective-permute-done.31.refs_5_), channel_id=1, source_target_pairs={{32,0},{64,32},{96,64},{0,96},{160,128},{192,160},{224,192},{128,2... | collective-permute-start | bytes 983048 | tf_op jit(solution)/shard_map/ppermute | solution.py:25
  147.4 22.5 %collective-permute-start.32 = (f32[10,16,512]{2,1,0:T(8,128)}, f32[10,16,512]{2,1,0:T(8,128)}, u32[]{:S(2)}, u32[]{:S(2)}) collective-permute-start(f32[10,16,512]{2,1,0:T(8,128)} %collective-permute-done.31.refs_5_), channel_id=1, source_target_pairs={{0,32},{32,64},{64,96},{96,0},{128,160},{160,192},{192,224},{224,1... | collective-permute-start | bytes 983048 | tf_op jit(solution)/shard_map/ppermute | solution.py:25
  148.1 12.1 %copy-start.18 = (f32[2,6,16,512]{3,2,1,0:T(8,128)S(1)}, f32[2,6,16,512]{3,2,1,0:T(8,128)}, u32[]{:S(2)}) copy-start(f32[2,6,16,512]{3,2,1,0:T(8,128)} %copy-done.17) | copy-start | bytes 1179652
  162.5 14.1 %collective-permute-start.30 = (f32[5,16,512]{2,1,0:T(8,128)S(1)}, f32[5,16,512]{2,1,0:T(8,128)S(1)}, u32[]{:S(2)}, u32[]{:S(2)}) collective-permute-start(f32[5,16,512]{2,1,0:T(8,128)S(1)} %slice.77), channel_id=1, source_target_pairs={{32,0},{64,32},{96,64},{0,96},{160,128},{192,160},{224,192},{128,2... | collective-permute-start | bytes 491528 | tf_op jit(solution)/shard_map/ppermute | solution.py:25
  166.2 13.1 %collective-permute-start.29 = (f32[5,16,512]{2,1,0:T(8,128)S(1)}, f32[5,16,512]{2,1,0:T(8,128)S(1)}, u32[]{:S(2)}, u32[]{:S(2)}) collective-permute-start(f32[5,16,512]{2,1,0:T(8,128)S(1)} %slice.76), channel_id=1, source_target_pairs={{0,32},{32,64},{64,96},{96,0},{128,160},{160,192},{192,224},{224,1... | collective-permute-start | bytes 491528 | tf_op jit(solution)/shard_map/ppermute | solution.py:25
  167.2 12.1 %collective-permute-start.35 = (f32[5,16,512]{2,1,0:T(8,128)S(1)}, f32[5,16,512]{2,1,0:T(8,128)S(1)}, u32[]{:S(2)}, u32[]{:S(2)}) collective-permute-start(f32[5,16,512]{2,1,0:T(8,128)S(1)} %slice.79), channel_id=1, source_target_pairs={{32,0},{64,32},{96,64},{0,96},{160,128},{192,160},{224,192},{128,2... | collective-permute-start | bytes 491528 | tf_op jit(solution)/shard_map/ppermute | solution.py:25
  170.9 8.4 %collective-permute-start.34 = (f32[5,16,512]{2,1,0:T(8,128)S(1)}, f32[5,16,512]{2,1,0:T(8,128)S(1)}, u32[]{:S(2)}, u32[]{:S(2)}) collective-permute-start(f32[5,16,512]{2,1,0:T(8,128)S(1)} %slice.78), channel_id=1, source_target_pairs={{0,32},{32,64},{64,96},{96,0},{128,160},{160,192},{192,224},{224,1... | collective-permute-start | bytes 491528 | tf_op jit(solution)/shard_map/ppermute | solution.py:25
  171.0 46.7 %copy-start.20 = (f32[6,16,512]{2,1,0:T(8,128)}, f32[6,16,512]{2,1,0:T(8,128)S(1)}, u32[]{:S(2)}) copy-start(f32[6,16,512]{2,1,0:T(8,128)S(1)} %fusion.8.refs_0_) | copy-start | bytes 589828
  171.0 28.6 %collective-permute-start.11 = (f32[6,16,512]{2,1,0:T(8,128)S(1)}, f32[6,16,512]{2,1,0:T(8,128)S(1)}, u32[]{:S(2)}, u32[]{:S(2)}) collective-permute-start(f32[6,16,512]{2,1,0:T(8,128)S(1)} %fusion.8.refs_0_), channel_id=1, source_target_pairs={{0,128},{32,160},{64,192},{96,224},{128,0},{160,32},{192,64},{224,... | collective-permute-start | bytes 589832 | tf_op jit(solution)/shard_map/ppermute | solution.py:25
  176.6 24.9 %collective-permute-start.8 = (f32[6,16,512]{2,1,0:T(8,128)S(1)}, f32[6,16,512]{2,1,0:T(8,128)S(1)}, u32[]{:S(2)}, u32[]{:S(2)}) collective-permute-start(f32[6,16,512]{2,1,0:T(8,128)S(1)} %fusion.8.refs_0_), channel_id=1, source_target_pairs={{32,0},{64,32},{96,64},{0,96},{160,128},{192,160},{224,192},{128,2... | collective-permute-start | bytes 589832 | tf_op jit(solution)/shard_map/ppermute | solution.py:25
  179.3 23.8 %collective-permute-start.7 = (f32[6,16,512]{2,1,0:T(8,128)S(1)}, f32[6,16,512]{2,1,0:T(8,128)S(1)}, u32[]{:S(2)}, u32[]{:S(2)}) collective-permute-start(f32[6,16,512]{2,1,0:T(8,128)S(1)} %fusion.8.refs_0_), channel_id=1, source_target_pairs={{0,32},{32,64},{64,96},{96,0},{128,160},{160,192},{192,224},{224,1... | collective-permute-start | bytes 589832 | tf_op jit(solution)/shard_map/ppermute | solution.py:25
  186.5 16.6 %collective-permute-start.36 = (f32[32,2,512]{2,1,0:T(2,128)}, f32[32,2,512]{2,1,0:T(2,128)S(1)}, u32[]{:S(2)}, u32[]{:S(2)}) collective-permute-start(f32[32,2,512]{2,1,0:T(2,128)} %get-tuple-element.48), channel_id=1, source_target_pairs={{0,1},{1,2},{2,3},{4,5},{5,6},{6,7},{8,9},{9,10},{10,11},{12,13},{... | collective-permute-start | bytes 393224 | tf_op jit(solution)/shard_map/ppermute | solution.py:198
  191.0 35.1 %collective-permute-start.18 = (f32[2,80,512]{2,1,0:T(8,128)S(1)}, f32[2,80,512]{2,1,0:T(8,128)S(1)}, u32[]{:S(2)}, u32[]{:S(2)}) collective-permute-start(f32[2,80,512]{2,1,0:T(8,128)S(1)} %get-tuple-element.55), channel_id=1, source_target_pairs={{0,4},{4,8},{8,12},{12,16},{16,20},{20,24},{24,28},{1,5},{5,9},{9,... | collective-permute-start | bytes 983048 | tf_op jit(solution)/shard_map/ppermute | solution.py:198
  199.6 35.4 %copy-start.27 = (f32[6,16,512]{2,1,0:T(8,128)}, f32[6,16,512]{2,1,0:T(8,128)S(1)}, u32[]{:S(2)}) copy-start(f32[6,16,512]{2,1,0:T(8,128)S(1)} %collective-permute-done.11.refs_5_) | copy-start | bytes 589828
  199.6 26.5 %collective-permute-start.19 = (f32[2,80,512]{2,1,0:T(8,128)S(1)}, f32[2,80,512]{2,1,0:T(8,128)S(1)}, u32[]{:S(2)}, u32[]{:S(2)}) collective-permute-start(f32[2,80,512]{2,1,0:T(8,128)S(1)} %get-tuple-element.56), channel_id=1, source_target_pairs={{4,0},{8,4},{12,8},{16,12},{20,16},{24,20},{28,24},{5,1},{9,5},{13... | collective-permute-start | bytes 983048 | tf_op jit(solution)/shard_map/ppermute | solution.py:198
  201.5 33.4 %copy-start.21 = (f32[6,16,512]{2,1,0:T(8,128)}, f32[6,16,512]{2,1,0:T(8,128)S(1)}, u32[]{:S(2)}) copy-start(f32[6,16,512]{2,1,0:T(8,128)S(1)} %collective-permute-done.8.refs_2_) | copy-start | bytes 589828
  201.5 16.2 %collective-permute-start.13 = (f32[6,16,512]{2,1,0:T(8,128)S(1)}, f32[6,16,512]{2,1,0:T(8,128)S(1)}, u32[]{:S(2)}, u32[]{:S(2)}) collective-permute-start(f32[6,16,512]{2,1,0:T(8,128)S(1)} %collective-permute-done.11.refs_5_), channel_id=1, source_target_pairs={{32,0},{64,32},{96,64},{0,96},{160,128},{192,160},{224,192},{128,2... | collective-permute-start | bytes 589832 | tf_op jit(solution)/shard_map/ppermute | solution.py:25
  203.1 31.9 %copy-start.22 = (f32[6,16,512]{2,1,0:T(8,128)}, f32[6,16,512]{2,1,0:T(8,128)S(1)}, u32[]{:S(2)}) copy-start(f32[6,16,512]{2,1,0:T(8,128)S(1)} %collective-permute-done.7.refs_1_) | copy-start | bytes 589828
  203.1 20.3 %collective-permute-start.12 = (f32[6,16,512]{2,1,0:T(8,128)S(1)}, f32[6,16,512]{2,1,0:T(8,128)S(1)}, u32[]{:S(2)}, u32[]{:S(2)}) collective-permute-start(f32[6,16,512]{2,1,0:T(8,128)S(1)} %collective-permute-done.11.refs_5_), channel_id=1, source_target_pairs={{0,32},{32,64},{64,96},{96,0},{128,160},{160,192},{192,224},{224,1... | collective-permute-start | bytes 589832 | tf_op jit(solution)/shard_map/ppermute | solution.py:25
  203.1 8.6 %copy-start.32 = (f32[32,2,512]{2,1,0:T(2,128)}, f32[32,2,512]{2,1,0:T(2,128)S(1)}, u32[]{:S(2)}) copy-start(f32[32,2,512]{2,1,0:T(2,128)S(1)} %collective-permute-done.36.before) | copy-start | bytes 393220
  203.1 6.2 %collective-permute-start.37 = (f32[32,2,512]{2,1,0:T(2,128)}, f32[32,2,512]{2,1,0:T(2,128)S(1)}, u32[]{:S(2)}, u32[]{:S(2)}) collective-permute-start(f32[32,2,512]{2,1,0:T(2,128)} %get-tuple-element.49), channel_id=1, source_target_pairs={{1,0},{2,1},{3,2},{5,4},{6,5},{7,6},{9,8},{10,9},{11,10},{13,12},{... | collective-permute-start | bytes 393224 | tf_op jit(solution)/shard_map/ppermute | solution.py:198
  209.3 19.5 %collective-permute-start.10 = (f32[3,16,512]{2,1,0:T(8,128)S(1)}, f32[3,16,512]{2,1,0:T(8,128)S(1)}, u32[]{:S(2)}, u32[]{:S(2)}) collective-permute-start(f32[3,16,512]{2,1,0:T(8,128)S(1)} %slice.67), channel_id=1, source_target_pairs={{32,0},{64,32},{96,64},{0,96},{160,128},{192,160},{224,192},{128,2... | collective-permute-start | bytes 294920 | tf_op jit(solution)/shard_map/ppermute | solution.py:25
  217.7 17.3 %copy-start.23 = (f32[6,16,512]{2,1,0:T(8,128)}, f32[6,16,512]{2,1,0:T(8,128)S(1)}, u32[]{:S(2)}) copy-start(f32[6,16,512]{2,1,0:T(8,128)S(1)} %collective-permute-done.13.refs_7_) | copy-start | bytes 589828
  217.7 30.3 %collective-permute-start.38 = (f32[2,80,512]{2,1,0:T(8,128)}, f32[2,80,512]{2,1,0:T(8,128)S(1)}, u32[]{:S(2)}, u32[]{:S(2)}) collective-permute-start(f32[2,80,512]{2,1,0:T(8,128)} %get-tuple-element.50), channel_id=1, source_target_pairs={{0,4},{4,8},{8,12},{12,16},{16,20},{20,24},{24,28},{1,5},{5,9},{9,... | collective-permute-start | bytes 983048 | tf_op jit(solution)/shard_map/ppermute | solution.py:198
  223.3 11.6 %copy-start.24 = (f32[6,16,512]{2,1,0:T(8,128)}, f32[6,16,512]{2,1,0:T(8,128)S(1)}, u32[]{:S(2)}) copy-start(f32[6,16,512]{2,1,0:T(8,128)S(1)} %collective-permute-done.12.refs_6_) | copy-start | bytes 589828
  223.4 24.6 %collective-permute-start.39 = (f32[2,80,512]{2,1,0:T(8,128)}, f32[2,80,512]{2,1,0:T(8,128)S(1)}, u32[]{:S(2)}, u32[]{:S(2)}) collective-permute-start(f32[2,80,512]{2,1,0:T(8,128)} %get-tuple-element.51), channel_id=1, source_target_pairs={{4,0},{8,4},{12,8},{16,12},{20,16},{24,20},{28,24},{5,1},{9,5},{13... | collective-permute-start | bytes 983048 | tf_op jit(solution)/shard_map/ppermute | solution.py:198
  226.0 21.9 %collective-permute-start.9 = (f32[3,16,512]{2,1,0:T(8,128)S(1)}, f32[3,16,512]{2,1,0:T(8,128)S(1)}, u32[]{:S(2)}, u32[]{:S(2)}) collective-permute-start(f32[3,16,512]{2,1,0:T(8,128)S(1)} %slice.66), channel_id=1, source_target_pairs={{0,32},{32,64},{64,96},{96,0},{128,160},{160,192},{192,224},{224,1... | collective-permute-start | bytes 294920 | tf_op jit(solution)/shard_map/ppermute | solution.py:25
  226.1 21.8 %collective-permute-start.15 = (f32[3,16,512]{2,1,0:T(8,128)S(1)}, f32[3,16,512]{2,1,0:T(8,128)S(1)}, u32[]{:S(2)}, u32[]{:S(2)}) collective-permute-start(f32[3,16,512]{2,1,0:T(8,128)S(1)} %slice.69), channel_id=1, source_target_pairs={{32,0},{64,32},{96,64},{0,96},{160,128},{192,160},{224,192},{128,2... | collective-permute-start | bytes 294920 | tf_op jit(solution)/shard_map/ppermute | solution.py:25
  228.8 6.2 %copy-start.34 = (f32[3,16,512]{2,1,0:T(8,128)}, f32[3,16,512]{2,1,0:T(8,128)S(1)}, u32[]{:S(2)}) copy-start(f32[3,16,512]{2,1,0:T(8,128)S(1)} %collective-permute-done.10.refs_4_) | copy-start | bytes 294916
  228.8 19.1 %collective-permute-start.14 = (f32[3,16,512]{2,1,0:T(8,128)S(1)}, f32[3,16,512]{2,1,0:T(8,128)S(1)}, u32[]{:S(2)}, u32[]{:S(2)}) collective-permute-start(f32[3,16,512]{2,1,0:T(8,128)S(1)} %slice.68), channel_id=1, source_target_pairs={{0,32},{32,64},{64,96},{96,0},{128,160},{160,192},{192,224},{224,1... | collective-permute-start | bytes 294920 | tf_op jit(solution)/shard_map/ppermute | solution.py:25
  (17 other events, 24.0 us)

commit v2 on v0

v2 whole, which is shorter than its diff:
```python
import functools

import jax
import jax.numpy as jnp
import numpy as np
from jax import lax
from jax.experimental import pallas as pl
from jax.experimental.pallas import tpu as pltpu
from jax.sharding import PartitionSpec as P

smoothing_rate = 0.15
support_width = 0.3
floor_eps = 1e-06
mark_radius = 3
ROWS = 16
RIM = 2
PAD = 8

UP = [(4 * z + y, 4 * z + (y + 1) % 4) for z in range(2) for y in range(4)]
DOWN = [(j, i) for i, j in UP]
ACROSS = [(4 * z + y, 4 * z + (y + 2) % 4) for z in range(2) for y in range(4)]
SWAP = [(4 * z + y, 4 * (1 - z) + y) for z in range(2) for y in range(4)]


def send(x, pairs):
    return lax.ppermute(x, "source", pairs)


def block_lists(tile_x, tile_y):
    groups = tile_y // ROWS
    every = [(p, g) for p in range(tile_x) for g in range(groups)]
    inner = [(p, g) for p, g in every if 4 <= p < tile_x - 4 and 0 < g < groups - 1]
    outer = [b for b in every if b not in inner]
    cut = len(outer) // 32 * 16
    return [outer[:cut], outer[cut:], inner]


def tables(blocks):
    arr = np.array(blocks, np.int32)
    return jnp.asarray(arr[:, 0]), jnp.asarray(arr[:, 1])


big = pltpu.CompilerParams(vmem_limit_bytes=11 * 2**20)


def hold(*arrays):
    return [pltpu.with_memory_space_constraint(x, pltpu.VMEM) for x in arrays]


def held(shape):
    return pltpu.VMEM(shape, jnp.float32)


def vmem(n):
    return [pl.BlockSpec(memory_space=pltpu.VMEM)] * n


def smem(n):
    return [pl.BlockSpec(memory_space=pltpu.SMEM)] * n


def partials(source_grad, adjoint_grad, planes, groups, starts, count):
    depth = source_grad.shape[-1]
    n = len(starts)
    width = depth // 2 if depth % 256 == 0 else depth

    def body(start_ref, plane_ref, group_ref, f_hbm, b_hbm, *refs):
        outs, (f_ref, b_ref, sems) = refs[: n // 2], refs[n // 2 :]

        def copies(k, i):
            at = start_ref[k] + i
            p = plane_ref[at]
            rows = pl.ds(pl.multiple_of(group_ref[at] * ROWS, ROWS), ROWS)
            j = k * count + i
            return [
                pltpu.make_async_copy(hbm.at[0, :, p, rows], ref.at[j], sems.at[m, j])
                for m, (hbm, ref) in enumerate([(f_hbm, f_ref), (b_hbm, b_ref)])
            ]

        for k in range(n):

            def begin(i, _, k=k):
                for c in copies(k, i):
                    c.start()
                return 0

            lax.fori_loop(0, count, begin, 0)
        for k in range(n):

            def one(i, _, k=k):
                for c in copies(k, i):
                    c.wait()
                j = k * count + i
                for lo in range(0, depth, width):
                    f = f_ref[j, :, :, lo : lo + width].astype(jnp.float32)
                    b = b_ref[j, :, :, lo : lo + width].astype(jnp.float32)
                    outs[k // 2][k % 2, 0, i, :, lo : lo + width] = f[0] * b[0] + f[1] * b[1] + f[2] * b[2]
                    outs[k // 2][k % 2, 1, i, :, lo : lo + width] = (f[0] * f[0] + f[1] * f[1] + f[2] * f[2]) * (
                        b[0] * b[0] + b[1] * b[1] + b[2] * b[2]
                    )
                return 0

            lax.fori_loop(0, count, one, 0)

    return pl.pallas_call(
        body,
        out_shape=[held((2, 2, count, ROWS, depth))] * (n // 2),
        in_specs=smem(3) + [pl.BlockSpec(memory_space=pl.ANY)] * 2,
        out_specs=vmem(n // 2),
        scratch_shapes=[pltpu.VMEM((n * count, 3, ROWS, depth), jnp.bfloat16)] * 2
        + [pltpu.SemaphoreType.DMA((2, n * count))],
        compiler_params=big,
        name="partials",
    )(jnp.stack(starts).astype(jnp.int32), planes, groups, *[pltpu.with_memory_space_constraint(x, pltpu.HBM) for x in (source_grad, adjoint_grad)])


def place(pieces, segments, starts_ref, plane_ref, group_ref, ms_ref, g_ref, rim, pad):
    for k, (piece, offset, count) in enumerate(segments):
        for i in range(count):
            at = starts_ref[k] + i
            p, g = plane_ref[at], group_ref[at]
            rows = pl.multiple_of(g * ROWS, ROWS)
            g_ref[p + rim, pl.ds(pl.multiple_of(pad + rows, 8), ROWS), :] = (
                pieces[piece][offset + i] * ms_ref[p, pl.ds(rows, ROWS), :]
            )


def frame_kernel(n, segments, starts, planes, groups, *refs):
    pieces, (ms, g, low, high) = refs[:n], refs[n:]
    place(pieces, segments, starts, planes, groups, ms, g, 0, 0)
    rows = ms.shape[1]

    def rim(p, _):
        low[p] = g[p, :RIM]
        high[p] = g[p, rows - RIM :]
        return 0

    lax.fori_loop(0, ms.shape[0], rim, 0)


def rim_kernel(tile, before, after, wide, low, high):
    planes, rows, depth = tile.shape
    zero = jnp.zeros((PAD, depth), jnp.float32)

    def fill(p, _):
        at = p + RIM
        wide[at, :PAD] = zero
        wide[at, PAD + rows :] = zero
        wide[at, PAD : PAD + rows] = tile[p]
        wide[at, PAD - RIM : PAD] = before[p]
        wide[at, PAD + rows : PAD + rows + RIM] = after[p]
        return 0

    lax.fori_loop(0, planes, fill, 0)
    low[...] = wide[RIM : 2 * RIM]
    high[...] = wide[planes : planes + RIM]


def neighbours(ref, p, r, n):
    here = ref[p, r : r + n]
    depth = here.shape[1]
    lane = lax.broadcasted_iota(jnp.int32, here.shape, 1)
    total = ref[p + 1, r : r + n] + ref[p - 1, r : r + n]
    total = total + (ref[p, r + 1 : r + n + 1] if r + n < ref.shape[1] else pltpu.roll(here, n - 1, 0))
    total = total + (ref[p, r - 1 : r + n - 1] if r else pltpu.roll(here, 1, 0))
    total = total + jnp.where(lane == depth - 1, 0.0, pltpu.roll(here, depth - 1, 1))
    total = total + jnp.where(lane == 0, 0.0, pltpu.roll(here, 1, 1))
    return here, total


def chunks(rows):
    return [(r, ROWS) for r in range(PAD, PAD + rows, ROWS)]


def assemble(wide, low, high, full):
    count = wide.shape[0] - 2 * RIM

    def copy(p, _):
        full[p + RIM] = wide[p + RIM]
        return 0

    lax.fori_loop(0, count, copy, 0)
    full[:RIM] = low[...]
    full[count + RIM :] = high[...]


def coefficient_kernel(wide, low, high, s, a, t):
    planes, rows = t.shape[:2]
    assemble(wide, low, high, s)

    def one(p, _):
        for r, n in [(0, PAD), *chunks(rows), (PAD + rows, PAD)]:
            here, total = neighbours(s, p, r, n)
            a[p, r : r + n] = 1.0 - smoothing_rate * here * total
        return 0

    lax.fori_loop(1, planes + 2 * RIM - 1, one, 0)

    def two(p, _):
        for r, n in chunks(rows):
            here = s[p + RIM, r : r + n]
            value = a[p + RIM, r : r + n]
            t[p, r - PAD : r - PAD + n] = jnp.where(here > 0.0, value / jnp.where(here > 0.0, here, 1.0), 0.0)
        return 0

    lax.fori_loop(0, planes, two, 0)


GROUPS = 4


def smooth_kernel(n, segments, starts, planes, groups, *refs):
    pieces, refs = refs[:n], refs[n:]
    low, high, wide, ms_hbm, s_hbm, a_hbm, t_hbm, out_hbm, g, g1, ms, s, a, t, out, sems = refs
    count, rows = out.shape[:2]
    framed, step = g.shape[0] // GROUPS, count // GROUPS
    ms_copy = pltpu.make_async_copy(ms_hbm, ms, sems.at[0, 0])
    ms_copy.start()
    arrivals = []
    for k in range(GROUPS):
        part = pl.ds(k * framed, framed)
        arrivals.append(
            [
                pltpu.make_async_copy(s_hbm.at[part], s.at[part], sems.at[1, k]),
                pltpu.make_async_copy(a_hbm.at[part], a.at[part], sems.at[2, k]),
            ]
        )
    t_copies = []
    for k in range(GROUPS):
        part = pl.ds(k * step, step)
        t_copies.append(pltpu.make_async_copy(t_hbm.at[part], t.at[part], sems.at[3, k]))
    for c in arrivals[0]:
        c.start()
    assemble(wide, low, high, g)
    ms_copy.wait()
    for c in sum(arrivals[1:], []) + t_copies:
        c.start()
    place(pieces, segments, starts, planes, groups, ms, g, RIM, PAD)

    def first(p, _):
        for r, m in [(0, PAD), *chunks(rows), (PAD + rows, PAD)]:
            here, total = neighbours(g, p, r, m)
            w = s[p, r : r + m]
            g1[p, r : r + m] = a[p, r : r + m] * here + smoothing_rate * w * w * total
        return 0

    for k in range(GROUPS):
        for c in arrivals[k]:
            c.wait()
        lax.fori_loop(max(1, k * framed), min(g.shape[0] - 1, (k + 1) * framed), first, 0)

    def second(p, _):
        for r, m in chunks(rows):
            here, total = neighbours(g1, p + RIM, r, m)
            out[p, r - PAD : r - PAD + m] = (
                t[p, r - PAD : r - PAD + m] * here + smoothing_rate * s[p + RIM, r : r + m] * total
            )
        return 0

    leaving = []
    for k in range(GROUPS):
        t_copies[k].wait()
        lax.fori_loop(k * step, (k + 1) * step, second, 0)
        part = pl.ds(k * step, step)
        leaving.append(pltpu.make_async_copy(out.at[part], out_hbm.at[part], sems.at[4, k]))
        leaving[-1].start()
    for c in leaving:
        c.wait()


def halo(low, high, axis):
    size = lax.axis_size(axis)
    up = [(i, i + 1) for i in range(size - 1)]
    return lax.ppermute(high, axis, up), lax.ppermute(low, axis, [(j, i) for i, j in up])


def with_rims(tile, before, after):
    planes, rows, depth = tile.shape
    rim = held((RIM, rows + 2 * PAD, depth))
    return pl.pallas_call(
        rim_kernel,
        out_shape=(held((planes + 2 * RIM, rows + 2 * PAD, depth)), rim, rim),
        in_specs=vmem(3),
        out_specs=vmem(3),
        compiler_params=big,
        name="rims",
    )(*hold(tile, before, after))


def shards(source_grad, adjoint_grad, log_model, surface_depth, source_columns, receiver_columns):
    tile_x, tile_y, depth_cells = log_model.shape
    me = lax.axis_index("source")
    y, half = me % 4, me // 4
    lists = block_lists(tile_x, tile_y)
    planes, groups = tables(sum(lists, []))
    parts = [len(blocks) // 8 for blocks in lists]
    after_rest = lax.optimization_barrier

    def start_of(k, offset, z):
        return 8 * sum(parts[:k]) + (2 * ((y + offset) % 4) + z) * parts[k]

    def sums_of(k):
        at = functools.partial(start_of, k)
        starts = [at(2, 1), at(1, 0), at(2, 0), at(-1, 1), at(-1, 0), at(1, 1), at(0, 0), at(0, 1)]
        return partials(source_grad, adjoint_grad, planes, groups, starts, parts[k])

    def first_step(up, down):
        return send(up, UP), send(down, DOWN)

    def second_step(up, down, keep):
        return keep[0] + down[0], keep[1] + up[0]

    def finish(own, up, down, end0, end1):
        own0 = own[0] + up[1] + end0
        own1 = own[1] + down[1] + end1
        return jnp.where(half == 0, own0, own1), jnp.where(half == 0, own1, own0)

    def normalised(own, other):
        total = own + other
        return total[0] * lax.rsqrt(total[1] + floor_eps)

    def ring(piece):
        return [piece, send(piece, UP), send(piece, DOWN), send(piece, ACROSS)]

    ring_offsets = (0, -1, 1, 2)

    up, down, keep, own = sums_of(0)
    log_model, up = after_rest((log_model, up))
    up, down = first_step(up, down)
    depth_index = lax.broadcasted_iota(jnp.int32, (tile_x, tile_y, depth_cells), 2)
    total_y = tile_y * lax.axis_size("line")
    columns = jnp.concatenate([source_columns, receiver_columns])
    electrode_x = columns // total_y
    electrode_y = columns % total_y
    global_x = lax.broadcasted_iota(jnp.int32, (1, tile_x), 1) + lax.axis_index("profile") * tile_x
    global_y = lax.broadcasted_iota(jnp.int32, (1, tile_y), 1) + lax.axis_index("line") * tile_y
    near_x = (jnp.abs(global_x - electrode_x[:, None]) <= mark_radius).astype(jnp.float32)
    near_y = (jnp.abs(global_y - electrode_y[:, None]) <= mark_radius).astype(jnp.float32)
    covered = jnp.einsum("ex,ey->xy", near_x, near_y, precision=lax.Precision.HIGHEST)
    threshold = surface_depth + jnp.where(covered > 0.5, depth_cells // 16, 0)
    root = support_width * lax.rsqrt(log_model * log_model + support_width * support_width)
    root = jnp.where(depth_index >= surface_depth[:, :, None], root, 0.0)
    masked = jnp.where(depth_index >= threshold[:, :, None], root, 0.0)
    up, down, root, masked = after_rest((up, down, root, masked))
    end0, end1 = second_step(up, down, keep)
    source_grad, adjoint_grad, end0, end1 = after_rest((source_grad, adjoint_grad, end0, end1))
    end0, end1 = send(end0, DOWN), send(end1, UP)

    up2, down2, keep2, own2 = sums_of(1)
    before, after = halo(root[:, :RIM], root[:, -RIM:], "line")
    own, leaving = finish(own, up, down, end0, end1)
    up2, down2, leaving, root = after_rest((up2, down2, leaving, root))
    other = send(leaving, SWAP)
    up, down = first_step(up2, down2)
    wide, low, high = with_rims(root, before, after)
    low, high = halo(low, high, "profile")
    up, down, wide, low, high = after_rest((up, down, wide, low, high))
    end0, end1 = second_step(up, down, keep2)
    source_grad, adjoint_grad, end0, end1, other = after_rest((source_grad, adjoint_grad, end0, end1, other))
    end0, end1 = send(end0, DOWN), send(end1, UP)

    up3, down3, keep3, own3 = sums_of(2)
    own2, leaving = finish(own2, up, down, end0, end1)
    up3, down3, leaving, wide = after_rest((up3, down3, leaving, wide))
    other2 = send(leaving, SWAP)
    up, down = first_step(up3, down3)
    s, a, t = pl.pallas_call(
        coefficient_kernel,
        out_shape=(held(wide.shape),) * 2 + (held(log_model.shape),),
        in_specs=vmem(3),
        out_specs=vmem(3),
        compiler_params=big,
        name="coefficients",
    )(*hold(wide, low, high))
    up, down, s, a, t, other2 = after_rest((up, down, s, a, t, other2))
    end0, end1 = second_step(up, down, keep3)
    end0, end1 = send(end0, DOWN), send(end1, UP)
    frame = jnp.concatenate([normalised(own, other), normalised(own2, other2)])
    frame_other = send(frame, SWAP)
    frame_ring = ring(frame)
    own3, leaving = finish(own3, up, down, end0, end1)
    inner = normalised(own3, send(leaving, SWAP))
    inner_other = send(inner, SWAP)
    other_ring = ring(frame_other)
    inner_rings = ring(inner) + ring(inner_other)
    frame_ring, other_ring, inner_other = after_rest((frame_ring, other_ring, inner_other))

    def segments_of(ranges):
        segments = [(i, offset, parts[k]) for i, piece in enumerate(ranges) for k, _, offset, _ in piece]
        starts = jnp.stack([start_of(k, q, z) for piece in ranges for k, z, _, q in piece])
        return segments, starts.astype(jnp.int32)

    pieces = frame_ring + other_ring
    segments, starts = segments_of([[(0, z, 0, q), (1, z, parts[0], q)] for z in (half, 1 - half) for q in ring_offsets])
    rim_y = held((tile_x, RIM, depth_cells))
    g, low, high = pl.pallas_call(
        functools.partial(frame_kernel, len(pieces), segments),
        out_shape=(held(log_model.shape), rim_y, rim_y),
        in_specs=smem(3) + vmem(len(pieces) + 1),
        out_specs=vmem(3),
        compiler_params=big,
        name="frame",
    )(starts, planes, groups, *hold(*pieces, masked))
    before, after = halo(low, high, "line")
    before, after, inner_rings = after_rest((before, after, inner_rings))
    g, low, high = with_rims(g, before, after)
    low, high = halo(low, high, "profile")
    pieces = inner_rings
    segments, starts = segments_of(
        [[(2, z, 0, q)] for z in (half, 1 - half) for q in ring_offsets]
    )
    wide_f32, tile_f32 = pltpu.VMEM(s.shape, jnp.float32), pltpu.VMEM(log_model.shape, jnp.float32)
    anywhere = pl.BlockSpec(memory_space=pl.ANY)
    return pl.pallas_call(
        functools.partial(smooth_kernel, len(pieces), segments),
        out_shape=jax.ShapeDtypeStruct(log_model.shape, jnp.float32),
        in_specs=smem(3) + vmem(len(pieces) + 3) + [anywhere] * 4,
        out_specs=anywhere,
        scratch_shapes=[wide_f32, wide_f32, tile_f32, wide_f32, wide_f32, tile_f32, tile_f32]
        + [pltpu.SemaphoreType.DMA((5, GROUPS))],
        compiler_params=pltpu.CompilerParams(vmem_limit_bytes=40 * 2**20),
        name="smooth",
    )(starts, planes, groups, *hold(*pieces, low, high, g), masked, s, a, t)


def solution(mesh):
    placed = (
        P("source", None, "profile", "line", None),
        P("source", None, "profile", "line", None),
        P("profile", "line", None),
        P("profile", "line"),
        P(),
        P(),
    )
    return jax.shard_map(
        shards, mesh=mesh, in_specs=placed, out_specs=P("profile", "line", None), check_vma=False
    )
```

time: 481 us -> 226 us (0.47)
  waiting for transfers between devices: 370 us -> 62.9 us
  starting transfers between devices: 19.7 us -> 93 us
  other arithmetic: 64.8 us -> 14 us
  Pallas kernels: 0 us -> 34.8 us
  between operations: 13.6 us -> 0.75 us
  local copies, waits for them, and re-layouts: 9.1 us -> 19.3 us
    psum x1 -> x0, waiting for transfers between devices: 353 us -> none  [shards(): correlation, energy = lax.psum((correlation, energy), 'source')]
    ppermute x8 -> x37, starting transfers between devices: 19.7 us -> 93 us  [the longest x29 51.3 us: send(): return lax.ppermute(x, 'source', pairs)]
    ppermute x8 -> x37, waiting for transfers between devices: 16.4 us -> 62.9 us  [the longest x29 48.9 us: send(): return lax.ppermute(x, 'source', pairs)]
    pallas_call x0 -> x8, Pallas kernels: none -> 34.8 us  [the longest x1 14.5 us: shards(): pl.pallas_call(functools.partial(smooth_kernel, len(pieces), segments), o...]
    add x3 -> x6, other arithmetic: 33.4 us -> 5.41 us  [the longest x3 2.86 us: normalised(): total = own + other]
    unnamed x6 -> x66, local copies, waits for them, and re-layouts: 0.63 us -> 18.8 us
    reduce_sum x1 -> x0, other arithmetic: 13.2 us -> none  [shards(): jnp.sum(backward * backward, axis=1)]
    concatenate x1, other arithmetic: 8.61 us -> 0.02 us  [shards(): frame = jnp.concatenate([normalised(own, other), normalised(own2, other2)])]
  transfers between devices with their start and end apart: 9 -> 37, of which waited for: 7 -> 16; matrix products, arithmetic and copies ran while one was open for 0% -> 5% of each run, Pallas kernels for 0% -> 7%
where the time goes in v2:
time: 226 us; the launch traced here: 225 us
  starting transfers between devices  93 us (41%)
  waiting for transfers between devices  62.9 us (28%)
  Pallas kernels  34.8 us (15%)
  local copies, waits for them, and re-layouts  19.3 us (9%)
  other arithmetic  14 us (6%)
    ppermute x29, starting transfers between devices, send(): return lax.ppermute(x, 'source', pairs)  51.3 us
    ppermute x29, waiting for transfers between devices, send(): return lax.ppermute(x, 'source', pairs)  48.9 us
    ppermute x4, starting transfers between devices, halo(): lax.ppermute(high, axis, up)  35.2 us
    unnamed x66, local copies, waits for them, and re-layouts  18.8 us
    pallas_call x1, Pallas kernels, shards(): pl.pallas_call(functools.partial(smooth_kernel, len(pieces), segments), o...  14.5 us
    pallas_call x3, Pallas kernels, partials(): pl.pallas_call(body, out_shape=[held((2, 2, count, ROWS, depth))] * (n //...  11.4 us
    ppermute x4, waiting for transfers between devices, halo(): lax.ppermute(low, axis, [(j, i) for i, j in up])  10.2 us
    pallas_call x1, Pallas kernels, shards(): pl.pallas_call(coefficient_kernel, out_shape=(held(wide.shape),) * 2 + (h...  6.71 us
  transfers between devices with their start and end apart: 37, of which 16 were waited for; matrix products, arithmetic and copies ran while one was open for 5% of the time, Pallas kernels for 7%

profile of v2, /device:TPU:33, one launch (start us, length us, event | category | flops | bytes accessed | tf_op | source)
XLA Modules:
  0.0 225.1 jit_solution(13767916614284717319)
XLA Ops:
  0.1 0.7 copy-done.11
  1.4 3.1 %partials.3 = (f32[2,2,4,16,512]{4,3,2,1,0:T(8,128)S(1)}, f32[2,2,4,16,512]{4,3,2,1,0:T(8,128)S(1)}, f32[2,2,4,16,512]{4,3,2,1,0:T(8,128)S(1)}, f32[2,2,4,16,512]{4,3,2,1,0:T(8,128)S(1)}) custom-call(s32[8]{0:T(128)S(1)} %stack.193.start_ref, s32[128]{0:T(128)S(1)} %copy-done.13, s32[128]{0:T(128)S(1)} %copy-done.11, bf16[1,3,32,64,512]{4,3,2,1,0:T(8,128)(2,1)} %f_hbm.3, ...), custom_call_target="tpu_custom_call" | custom-call | tf_op jit(solution)/shard_map/partials/pallas_call | solution.py:105
  4.5 1.4 collective-permute-start
  5.9 1.5 collective-permute-start.1
  7.8 5.6 %fusion = (f32[32,64,512]{2,1,0:T(8,128)}, f32[32,64,512]{2,1,0:T(8,128)}) fusion(s32[32,64]{1,0:T(8,128)S(1)} %fusion.2, f32[32,64,512]{2,1,0:T(8,128)} %param.10, s32[32,64]{1,0:T(8,128)S(1)} %copy-done.28), kind=kLoop, calls=%fused_computation.3 | loop fusion | flops 7340032 | bytes 12599296 | tf_op jit(solution)/shard_map/jit(_where)/select_n | solution.py:343
  13.4 5.3 %collective-permute-done = f32[2,2,4,16,512]{4,3,2,1,0:T(8,128)S(1)} collective-permute-done((f32[2,2,4,16,512]{4,3,2,1,0:T(8,128)S(1)}, f32[2,2,4,16,512]{4,3,2,1,0:T(8,128)S(1)}, u32[]{:S(2)}, u32[]{:S(2)}) %collective-permute-start) | collective-permute-done | bytes 524320 | tf_op jit(solution)/shard_map/ppermute | solution.py:26
  18.7 1.2 add_bitcast_fusion.4
  19.9 2.5 %collective-permute-start.2 = (f32[2,4,16,512]{3,2,1,0:T(8,128)S(1)}, f32[2,4,16,512]{3,2,1,0:T(8,128)S(1)}, u32[]{:S(2)}, u32[]{:S(2)}) collective-permute-start(f32[2,4,16,512]{3,2,1,0:T(8,128)S(1)} %get-tuple-element.89), channel_id=1, source_target_pairs={{32,0},{64,32},{96,64},{0,96},{160,128},{192,160},{224,192},{128,2... | collective-permute-start | bytes 786440 | tf_op jit(solution)/shard_map/ppermute | solution.py:26
  22.6 4.1 %partials.4 = (f32[2,2,6,16,512]{4,3,2,1,0:T(8,128)S(1)}, f32[2,2,6,16,512]{4,3,2,1,0:T(8,128)S(1)}, f32[2,2,6,16,512]{4,3,2,1,0:T(8,128)S(1)}, f32[2,2,6,16,512]{4,3,2,1,0:T(8,128)S(1)}) custom-call(s32[8]{0:T(128)S(1)} %stack.202.start_ref, s32[128]{0:T(128)S(1)} %copy-done.14, s32[128]{0:T(128)S(1)} %copy-done.12, bf16[1,3,32,64,512]{4,3,2,1,0:T(8,128)(2,1)} %f_hbm.3, ...), custom_call_target="tpu_custom_call" | custom-call | tf_op jit(solution)/shard_map/partials/pallas_call | solution.py:105
  26.8 2.7 %collective-permute-done.3 = f32[2,4,16,512]{3,2,1,0:T(8,128)S(1)} collective-permute-done((f32[2,4,16,512]{3,2,1,0:T(8,128)S(1)}, f32[2,4,16,512]{3,2,1,0:T(8,128)S(1)}, u32[]{:S(2)}, u32[]{:S(2)}) %collective-permute-start.3) | collective-permute-done | bytes 262176 | tf_op jit(solution)/shard_map/ppermute | solution.py:26
  29.5 1.2 broadcast_select_fusion.2
  30.8 2.7 %collective-permute-start.5 = (f32[2,2,6,16,512]{4,3,2,1,0:T(8,128)S(1)}, f32[2,2,6,16,512]{4,3,2,1,0:T(8,128)S(1)}, u32[]{:S(2)}, u32[]{:S(2)}) collective-permute-start(f32[2,2,6,16,512]{4,3,2,1,0:T(8,128)S(1)} %get-tuple-element.98), channel_id=1, source_target_pairs={{32,0},{64,32},{96,64},{0,96},{160,128},{192,160},{224,192},{128,2... | collective-permute-start | bytes 2359304 | tf_op jit(solution)/shard_map/ppermute | solution.py:26
  33.6 1.3 collective-permute-start.7
  34.9 4.0 %collective-permute-start.6 = (f32[32,2,512]{2,1,0:T(2,128)S(1)}, f32[32,2,512]{2,1,0:T(2,128)S(1)}, u32[]{:S(2)}, u32[]{:S(2)}) collective-permute-start(f32[32,2,512]{2,1,0:T(2,128)S(1)} %get-tuple-element.160), channel_id=1, source_target_pairs={{0,1},{1,2},{2,3},{4,5},{5,6},{6,7},{8,9},{9,10},{10,11},{12,13},{... | collective-permute-start | bytes 393224 | tf_op jit(solution)/shard_map/ppermute | solution.py:274
  38.9 0.7 collective-permute-done.7.after
  39.6 1.2 collective-permute-done.6.before
  41.3 2.5 %copy-done.3 = f32[36,80,512]{2,1,0:T(8,128)} copy-done((f32[36,80,512]{2,1,0:T(8,128)}, f32[36,80,512]{2,1,0:T(8,128)S(1)}, u32[]{:S(2)}) %copy-start.3) | copy-done | bytes 5898264
  43.9 8.0 %collective-permute-start.8 = (f32[2,80,512]{2,1,0:T(8,128)S(1)}, f32[2,80,512]{2,1,0:T(8,128)S(1)}, u32[]{:S(2)}, u32[]{:S(2)}) collective-permute-start(f32[2,80,512]{2,1,0:T(8,128)S(1)} %get-tuple-element.101), channel_id=1, source_target_pairs={{0,4},{4,8},{8,12},{12,16},{16,20},{20,24},{24,28},{1,5},{5,9},{9,... | collective-permute-start | bytes 983048 | tf_op jit(solution)/shard_map/ppermute | solution.py:274
  51.9 1.9 collective-permute-start.9
  53.8 5.2 %collective-permute-start.10 = (f32[2,4,16,512]{3,2,1,0:T(8,128)S(1)}, f32[2,4,16,512]{3,2,1,0:T(8,128)S(1)}, u32[]{:S(2)}, u32[]{:S(2)}) collective-permute-start(f32[2,4,16,512]{3,2,1,0:T(8,128)S(1)} %broadcast_select_fusion.2), channel_id=1, source_target_pairs={{0,128},{32,160},{64,192},{96,224},{128,0},{160,32},{192,64},{224,... | collective-permute-start | bytes 786440 | tf_op jit(solution)/shard_map/ppermute | solution.py:26
  59.0 1.3 collective-permute-done.9.high
  60.3 0.8 copy-done.9
  61.1 1.2 add_bitcast_fusion.2
  62.3 5.0 %collective-permute-done.10 = f32[2,4,16,512]{3,2,1,0:T(8,128)S(1)} collective-permute-done((f32[2,4,16,512]{3,2,1,0:T(8,128)S(1)}, f32[2,4,16,512]{3,2,1,0:T(8,128)S(1)}, u32[]{:S(2)}, u32[]{:S(2)}) %collective-permute-start.10) | collective-permute-done | bytes 262176 | tf_op jit(solution)/shard_map/ppermute | solution.py:26
  67.3 1.5 collective-permute-start.12
  68.9 4.2 %partials.5 = (f32[2,2,6,16,512]{4,3,2,1,0:T(8,128)S(1)}, f32[2,2,6,16,512]{4,3,2,1,0:T(8,128)S(1)}, f32[2,2,6,16,512]{4,3,2,1,0:T(8,128)S(1)}, f32[2,2,6,16,512]{4,3,2,1,0:T(8,128)S(1)}) custom-call(s32[8]{0:T(128)S(1)} %stack.211.start_ref, s32[128]{0:T(128)S(1)} %copy-done.14, s32[128]{0:T(128)S(1)} %copy-done.12, bf16[1,3,32,64,512]{4,3,2,1,0:T(8,128)(2,1)} %f_hbm.3, ...), custom_call_target="tpu_custom_call" | custom-call | tf_op jit(solution)/shard_map/partials/pallas_call | solution.py:105
  73.1 1.3 collective-permute-done.11
  74.4 1.1 collective-permute-done.12
  75.5 1.4 broadcast_select_fusion.1
  77.2 2.5 %collective-permute-start.14 = (f32[2,2,6,16,512]{4,3,2,1,0:T(8,128)S(1)}, f32[2,2,6,16,512]{4,3,2,1,0:T(8,128)S(1)}, u32[]{:S(2)}, u32[]{:S(2)}) collective-permute-start(f32[2,2,6,16,512]{4,3,2,1,0:T(8,128)S(1)} %get-tuple-element.116), channel_id=1, source_target_pairs={{32,0},{64,32},{96,64},{0,96},{160,128},{192,160},{224,192},{128,2... | collective-permute-start | bytes 2359304 | tf_op jit(solution)/shard_map/ppermute | solution.py:26
  79.7 9.3 %collective-permute-start.15 = (f32[2,6,16,512]{3,2,1,0:T(8,128)S(1)}, f32[2,6,16,512]{3,2,1,0:T(8,128)S(1)}, u32[]{:S(2)}, u32[]{:S(2)}) collective-permute-start(f32[2,6,16,512]{3,2,1,0:T(8,128)S(1)} %broadcast_select_fusion.1), channel_id=1, source_target_pairs={{0,128},{32,160},{64,192},{96,224},{128,0},{160,32},{192,64},{224,... | collective-permute-start | bytes 1179656 | tf_op jit(solution)/shard_map/ppermute | solution.py:26
  89.0 1.1 select_add_fusion.2
  90.2 6.7 %coefficients.1 = (f32[36,80,512]{2,1,0:T(8,128)S(1)}, f32[36,80,512]{2,1,0:T(8,128)S(1)}, f32[32,64,512]{2,1,0:T(8,128)S(1)}) custom-call(f32[36,80,512]{2,1,0:T(8,128)S(1)} %bitcast.103, f32[2,80,512]{2,1,0:T(8,128)S(1)} %collective-permute-done.8.low, f32[2,80,512]{2,1,0:T(8,128)S(1)} %copy-done.10), custom_call_target="tpu_custom_call" | custom-call | tf_op jit(solution)/shard_map/coefficients/pallas_call | solution.py:367
  96.9 2.5 %copy-done.4 = f32[36,80,512]{2,1,0:T(8,128)} copy-done((f32[36,80,512]{2,1,0:T(8,128)}, f32[36,80,512]{2,1,0:T(8,128)S(1)}, u32[]{:S(2)}) %copy-start.4) | copy-done | bytes 5898264
  99.5 2.0 copy-done.8
  101.7 2.7 %collective-permute-start.23 = (f32[2,6,16,512]{3,2,1,0:T(8,128)S(1)}, f32[2,6,16,512]{3,2,1,0:T(8,128)S(1)}, u32[]{:S(2)}, u32[]{:S(2)}) collective-permute-start(f32[2,6,16,512]{3,2,1,0:T(8,128)S(1)} %get-tuple-element.162), channel_id=1, source_target_pairs={{32,0},{64,32},{96,64},{0,96},{160,128},{192,160},{224,192},{128,2... | collective-permute-start | bytes 1179656 | tf_op jit(solution)/shard_map/ppermute | solution.py:26
  104.4 1.4 select_add_fusion.1
  105.9 3.7 %collective-permute-done.24 = f32[2,6,16,512]{3,2,1,0:T(8,128)S(1)} collective-permute-done((f32[2,6,16,512]{3,2,1,0:T(8,128)S(1)}, f32[2,6,16,512]{3,2,1,0:T(8,128)S(1)}, u32[]{:S(2)}, u32[]{:S(2)}) %collective-permute-start.24) | collective-permute-done | bytes 393248 | tf_op jit(solution)/shard_map/ppermute | solution.py:26
  109.8 4.6 %collective-permute-start.25 = (f32[2,6,16,512]{3,2,1,0:T(8,128)S(1)}, f32[2,6,16,512]{3,2,1,0:T(8,128)S(1)}, u32[]{:S(2)}, u32[]{:S(2)}) collective-permute-start(f32[2,6,16,512]{3,2,1,0:T(8,128)S(1)} %broadcast_select_fusion), channel_id=1, source_target_pairs={{0,128},{32,160},{64,192},{96,224},{128,0},{160,32},{192,64},{224,... | collective-permute-start | bytes 1179656 | tf_op jit(solution)/shard_map/ppermute | solution.py:26
  114.5 0.9 collective-permute-start.19
  115.4 1.2 collective-permute-start.18
  116.6 1.5 collective-permute-start.17
  118.7 18.5 %collective-permute-done.19.refs_4_ = f32[10,16,512]{2,1,0:T(8,128)S(1)} collective-permute-done((f32[10,16,512]{2,1,0:T(8,128)S(1)}, f32[10,16,512]{2,1,0:T(8,128)S(1)}, u32[]{:S(2)}, u32[]{:S(2)}) %collective-permute-start.19) | collective-permute-done | bytes 327712 | tf_op jit(solution)/shard_map/ppermute | solution.py:26
  137.4 2.1 collective-permute-start.21
  140.2 2.1 collective-permute-start.31
  142.2 4.0 %collective-permute-done.22.refs_7_ = f32[10,16,512]{2,1,0:T(8,128)S(1)} collective-permute-done((f32[10,16,512]{2,1,0:T(8,128)S(1)}, f32[10,16,512]{2,1,0:T(8,128)S(1)}, u32[]{:S(2)}, u32[]{:S(2)}) %collective-permute-start.22) | collective-permute-done | bytes 327712 | tf_op jit(solution)/shard_map/ppermute | solution.py:26
  146.2 1.6 collective-permute-start.30
  147.8 7.3 %collective-permute-done.21.refs_6_ = f32[10,16,512]{2,1,0:T(8,128)S(1)} collective-permute-done((f32[10,16,512]{2,1,0:T(8,128)S(1)}, f32[10,16,512]{2,1,0:T(8,128)S(1)}, u32[]{:S(2)}, u32[]{:S(2)}) %collective-permute-start.21) | collective-permute-done | bytes 327712 | tf_op jit(solution)/shard_map/ppermute | solution.py:26
  155.1 2.3 %collective-permute-start.29 = (f32[6,16,512]{2,1,0:T(8,128)S(1)}, f32[6,16,512]{2,1,0:T(8,128)}, u32[]{:S(2)}, u32[]{:S(2)}) collective-permute-start(f32[6,16,512]{2,1,0:T(8,128)S(1)} %fusion.5.refs_0_), channel_id=1, source_target_pairs={{0,32},{32,64},{64,96},{96,0},{128,160},{160,192},{192,224},{224,1... | collective-permute-start | bytes 589832 | tf_op jit(solution)/shard_map/ppermute | solution.py:26
  157.5 2.8 %collective-permute-start.34 = (f32[6,16,512]{2,1,0:T(8,128)S(1)}, f32[6,16,512]{2,1,0:T(8,128)}, u32[]{:S(2)}, u32[]{:S(2)}) collective-permute-start(f32[6,16,512]{2,1,0:T(8,128)S(1)} %collective-permute-done.26.refs_4_), channel_id=1, source_target_pairs={{0,64},{32,96},{64,0},{96,32},{128,192},{160,224},{192,128},{224,1... | collective-permute-start | bytes 589832 | tf_op jit(solution)/shard_map/ppermute | solution.py:26
  160.2 1.5 collective-permute-start.32
  161.8 2.2 copy-done
  164.0 1.1 frame.1
  165.1 4.1 %collective-permute-start.27 = (f32[32,2,512]{2,1,0:T(2,128)S(1)}, f32[32,2,512]{2,1,0:T(2,128)S(1)}, u32[]{:S(2)}, u32[]{:S(2)}) collective-permute-start(f32[32,2,512]{2,1,0:T(2,128)S(1)} %get-tuple-element.138), channel_id=1, source_target_pairs={{0,1},{1,2},{2,3},{4,5},{5,6},{6,7},{8,9},{9,10},{10,11},{12,13},{... | collective-permute-start | bytes 393224 | tf_op jit(solution)/shard_map/ppermute | solution.py:274
  169.2 1.3 collective-permute-start.28
  171.1 3.8 %collective-permute-done.28.after = f32[32,2,512]{2,1,0:T(2,128)S(1)} collective-permute-done((f32[32,2,512]{2,1,0:T(2,128)S(1)}, f32[32,2,512]{2,1,0:T(2,128)S(1)}, u32[]{:S(2)}, u32[]{:S(2)}) %collective-permute-start.28) | collective-permute-done | bytes 131104 | tf_op jit(solution)/shard_map/ppermute | solution.py:274
  175.5 2.5 %copy-done.6 = f32[36,80,512]{2,1,0:T(8,128)} copy-done((f32[36,80,512]{2,1,0:T(8,128)}, f32[36,80,512]{2,1,0:T(8,128)S(1)}, u32[]{:S(2)}) %copy-start.6) | copy-done | bytes 5898264
  177.9 19.2 %collective-permute-start.35 = (f32[2,80,512]{2,1,0:T(8,128)S(1)}, f32[2,80,512]{2,1,0:T(8,128)S(1)}, u32[]{:S(2)}, u32[]{:S(2)}) collective-permute-start(f32[2,80,512]{2,1,0:T(8,128)S(1)} %get-tuple-element.151), channel_id=1, source_target_pairs={{0,4},{4,8},{8,12},{12,16},{16,20},{20,24},{24,28},{1,5},{5,9},{9,... | collective-permute-start | bytes 983048 | tf_op jit(solution)/shard_map/ppermute | solution.py:274
  197.1 1.9 collective-permute-start.36
  199.1 1.9 collective-permute-done.35.refs_8_
  201.1 4.4 %collective-permute-done.36.refs_9_ = f32[2,80,512]{2,1,0:T(8,128)S(1)} collective-permute-done((f32[2,80,512]{2,1,0:T(8,128)S(1)}, f32[2,80,512]{2,1,0:T(8,128)S(1)}, u32[]{:S(2)}, u32[]{:S(2)}) %collective-permute-start.36) | collective-permute-done | bytes 327712 | tf_op jit(solution)/shard_map/ppermute | solution.py:274
  205.5 2.2 copy-done.1
  207.7 2.7 %copy-done.7 = f32[36,80,512]{2,1,0:T(8,128)S(1)} copy-done((f32[36,80,512]{2,1,0:T(8,128)S(1)}, f32[36,80,512]{2,1,0:T(8,128)}, u32[]{:S(2)}) %copy-start.7) | copy-done | bytes 5898264
  210.4 14.5 %smooth.1 = f32[32,64,512]{2,1,0:T(8,128)} custom-call(s32[8]{0:T(128)S(1)} %stack.167.starts, s32[128]{0:T(128)S(1)} %copy-done.14, s32[128]{0:T(128)S(1)} %copy-done.12, f32[6,16,512]{2,1,0:T(8,128)S(1)} %fusion.5.refs_0_, f32[6,16,512]{2,1,0:T(8,128)} %collective-permute-done.29.refs_1_, f32[6,16,512]{2,1,0:T(8,128)S(1)} %collective-permute-done.30.refs_2_, ...), custom_call_target="tpu_custom_call" | custom-call | tf_op jit(solution)/shard_map/smooth/pallas_call | solution.py:414
  (109 shorter events, 5.7 us)
Async XLA Ops:
  1.4 6.0 %copy-start.29 = (s32[256]{0:T(256)S(1)}, s32[256]{0:T(256)}, u32[]{:S(2)}) copy-start(s32[256]{0:T(256)} %param.13) | copy-start | bytes 3076
  1.4 6.0 %copy-start.30 = (s32[8]{0:T(128)S(1)}, s32[8]{0:T(128)}, u32[]{:S(2)}) copy-start(s32[8]{0:T(128)} %param.12) | copy-start | bytes 100
  1.4 6.1 %copy-start.28 = (s32[32,64]{1,0:T(8,128)S(1)}, s32[32,64]{1,0:T(8,128)}, u32[]{:S(2)}) copy-start(s32[32,64]{1,0:T(8,128)} %param.11) | copy-start | bytes 24580
  4.5 14.2 %collective-permute-start = (f32[2,2,4,16,512]{4,3,2,1,0:T(8,128)S(1)}, f32[2,2,4,16,512]{4,3,2,1,0:T(8,128)S(1)}, u32[]{:S(2)}, u32[]{:S(2)}) collective-permute-start(f32[2,2,4,16,512]{4,3,2,1,0:T(8,128)S(1)} %get-tuple-element.83), channel_id=1, source_target_pairs={{0,32},{32,64},{64,96},{96,0},{128,160},{160,192},{192,224},{224,1... | collective-permute-start | bytes 1572872 | tf_op jit(solution)/shard_map/ppermute | solution.py:26
  5.9 12.8 %collective-permute-start.1 = (f32[2,2,4,16,512]{4,3,2,1,0:T(8,128)S(1)}, f32[2,2,4,16,512]{4,3,2,1,0:T(8,128)}, u32[]{:S(2)}, u32[]{:S(2)}) collective-permute-start(f32[2,2,4,16,512]{4,3,2,1,0:T(8,128)S(1)} %get-tuple-element.84), channel_id=1, source_target_pairs={{32,0},{64,32},{96,64},{0,96},{160,128},{192,160},{224,192},{128,2... | collective-permute-start | bytes 1572872 | tf_op jit(solution)/shard_map/ppermute | solution.py:26
  7.8 14.8 %copy-start.12 = (s32[128]{0:T(128)S(1)}, s32[128]{0:T(128)}, u32[]{:S(2)}) copy-start(s32[128]{0:T(128)} %constant.207.clone.group_ref.groups) | copy-start | bytes 1540
  7.8 14.7 %copy-start.14 = (s32[128]{0:T(128)S(1)}, s32[128]{0:T(128)}, u32[]{:S(2)}) copy-start(s32[128]{0:T(128)} %constant.206.clone.plane_ref.planes) | copy-start | bytes 1540
  18.7 3.8 %copy-start.19 = (f32[2,2,4,16,512]{4,3,2,1,0:T(8,128)}, f32[2,2,4,16,512]{4,3,2,1,0:T(8,128)S(1)}, u32[]{:S(2)}) copy-start(f32[2,2,4,16,512]{4,3,2,1,0:T(8,128)S(1)} %collective-permute-done) | copy-start | bytes 1572868
  19.9 6.8 %collective-permute-start.2 = (f32[2,4,16,512]{3,2,1,0:T(8,128)S(1)}, f32[2,4,16,512]{3,2,1,0:T(8,128)S(1)}, u32[]{:S(2)}, u32[]{:S(2)}) collective-permute-start(f32[2,4,16,512]{3,2,1,0:T(8,128)S(1)} %get-tuple-element.89), channel_id=1, source_target_pairs={{32,0},{64,32},{96,64},{0,96},{160,128},{192,160},{224,192},{128,2... | collective-permute-start | bytes 786440 | tf_op jit(solution)/shard_map/ppermute | solution.py:26
  22.5 7.0 %collective-permute-start.3 = (f32[2,4,16,512]{3,2,1,0:T(8,128)S(1)}, f32[2,4,16,512]{3,2,1,0:T(8,128)S(1)}, u32[]{:S(2)}, u32[]{:S(2)}) collective-permute-start(f32[2,4,16,512]{3,2,1,0:T(8,128)S(1)} %get-tuple-element.90), channel_id=1, source_target_pairs={{0,32},{32,64},{64,96},{96,0},{128,160},{160,192},{192,224},{224,1... | collective-permute-start | bytes 786440 | tf_op jit(solution)/shard_map/ppermute | solution.py:26
  22.6 6.9 %copy-start.20 = (f32[2,2,4,16,512]{4,3,2,1,0:T(8,128)S(1)}, f32[2,2,4,16,512]{4,3,2,1,0:T(8,128)}, u32[]{:S(2)}) copy-start(f32[2,2,4,16,512]{4,3,2,1,0:T(8,128)} %copy-done.19) | copy-start | bytes 1572868
  22.6 10.9 %copy-start.2 = (f32[32,64,512]{2,1,0:T(8,128)S(1)}, f32[32,64,512]{2,1,0:T(8,128)}, u32[]{:S(2)}) copy-start(f32[32,64,512]{2,1,0:T(8,128)} %get-tuple-element.99.tile) | copy-start | bytes 12582916
  26.7 14.6 %copy-start.22 = (f32[2,4,16,512]{3,2,1,0:T(8,128)}, f32[2,4,16,512]{3,2,1,0:T(8,128)S(1)}, u32[]{:S(2)}) copy-start(f32[2,4,16,512]{3,2,1,0:T(8,128)S(1)} %collective-permute-done.2) | copy-start | bytes 786436
  29.5 32.8 %copy-start.24 = (f32[2,4,16,512]{3,2,1,0:T(8,128)}, f32[2,4,16,512]{3,2,1,0:T(8,128)S(1)}, u32[]{:S(2)}) copy-start(f32[2,4,16,512]{3,2,1,0:T(8,128)S(1)} %collective-permute-done.3) | copy-start | bytes 786436
  30.7 30.4 %collective-permute-start.4 = (f32[2,2,6,16,512]{4,3,2,1,0:T(8,128)S(1)}, f32[2,2,6,16,512]{4,3,2,1,0:T(8,128)S(1)}, u32[]{:S(2)}, u32[]{:S(2)}) collective-permute-start(f32[2,2,6,16,512]{4,3,2,1,0:T(8,128)S(1)} %get-tuple-element.97), channel_id=1, source_target_pairs={{0,32},{32,64},{64,96},{96,0},{128,160},{160,192},{192,224},{224,1... | collective-permute-start | bytes 2359304 | tf_op jit(solution)/shard_map/ppermute | solution.py:26
  30.8 30.3 %collective-permute-start.5 = (f32[2,2,6,16,512]{4,3,2,1,0:T(8,128)S(1)}, f32[2,2,6,16,512]{4,3,2,1,0:T(8,128)S(1)}, u32[]{:S(2)}, u32[]{:S(2)}) collective-permute-start(f32[2,2,6,16,512]{4,3,2,1,0:T(8,128)S(1)} %get-tuple-element.98), channel_id=1, source_target_pairs={{32,0},{64,32},{96,64},{0,96},{160,128},{192,160},{224,192},{128,2... | collective-permute-start | bytes 2359304 | tf_op jit(solution)/shard_map/ppermute | solution.py:26
  33.6 6.0 %collective-permute-start.7 = (f32[32,2,512]{2,1,0:T(2,128)S(1)}, f32[32,2,512]{2,1,0:T(2,128)S(1)}, u32[]{:S(2)}, u32[]{:S(2)}) collective-permute-start(f32[32,2,512]{2,1,0:T(2,128)S(1)} %get-tuple-element.159), channel_id=1, source_target_pairs={{1,0},{2,1},{3,2},{5,4},{6,5},{7,6},{9,8},{10,9},{11,10},{13,12},{... | collective-permute-start | bytes 393224 | tf_op jit(solution)/shard_map/ppermute | solution.py:274
  34.9 5.9 %collective-permute-start.6 = (f32[32,2,512]{2,1,0:T(2,128)S(1)}, f32[32,2,512]{2,1,0:T(2,128)S(1)}, u32[]{:S(2)}, u32[]{:S(2)}) collective-permute-start(f32[32,2,512]{2,1,0:T(2,128)S(1)} %get-tuple-element.160), channel_id=1, source_target_pairs={{0,1},{1,2},{2,3},{4,5},{5,6},{6,7},{8,9},{9,10},{10,11},{12,13},{... | collective-permute-start | bytes 393224 | tf_op jit(solution)/shard_map/ppermute | solution.py:274
  41.3 2.6 %copy-start.3 = (f32[36,80,512]{2,1,0:T(8,128)}, f32[36,80,512]{2,1,0:T(8,128)S(1)}, u32[]{:S(2)}) copy-start(f32[36,80,512]{2,1,0:T(8,128)S(1)} %get-tuple-element.117.wide) | copy-start | bytes 17694724
  43.9 15.2 %collective-permute-start.8 = (f32[2,80,512]{2,1,0:T(8,128)S(1)}, f32[2,80,512]{2,1,0:T(8,128)S(1)}, u32[]{:S(2)}, u32[]{:S(2)}) collective-permute-start(f32[2,80,512]{2,1,0:T(8,128)S(1)} %get-tuple-element.101), channel_id=1, source_target_pairs={{0,4},{4,8},{8,12},{12,16},{16,20},{20,24},{24,28},{1,5},{5,9},{9,... | collective-permute-start | bytes 983048 | tf_op jit(solution)/shard_map/ppermute | solution.py:274
  51.9 8.4 %collective-permute-start.9 = (f32[2,80,512]{2,1,0:T(8,128)S(1)}, f32[2,80,512]{2,1,0:T(8,128)S(1)}, u32[]{:S(2)}, u32[]{:S(2)}) collective-permute-start(f32[2,80,512]{2,1,0:T(8,128)S(1)} %get-tuple-element.102), channel_id=1, source_target_pairs={{4,0},{8,4},{12,8},{16,12},{20,16},{24,20},{28,24},{5,1},{9,5},{13... | collective-permute-start | bytes 983048 | tf_op jit(solution)/shard_map/ppermute | solution.py:274
  53.8 13.4 %collective-permute-start.10 = (f32[2,4,16,512]{3,2,1,0:T(8,128)S(1)}, f32[2,4,16,512]{3,2,1,0:T(8,128)S(1)}, u32[]{:S(2)}, u32[]{:S(2)}) collective-permute-start(f32[2,4,16,512]{3,2,1,0:T(8,128)S(1)} %broadcast_select_fusion.2), channel_id=1, source_target_pairs={{0,128},{32,160},{64,192},{96,224},{128,0},{160,32},{192,64},{224,... | collective-permute-start | bytes 786440 | tf_op jit(solution)/shard_map/ppermute | solution.py:26
  61.1 6.2 %copy-start.17 = (f32[2,2,6,16,512]{4,3,2,1,0:T(8,128)}, f32[2,2,6,16,512]{4,3,2,1,0:T(8,128)S(1)}, u32[]{:S(2)}) copy-start(f32[2,2,6,16,512]{4,3,2,1,0:T(8,128)S(1)} %collective-permute-done.5) | copy-start | bytes 2359300
  67.3 7.1 %collective-permute-start.11 = (f32[2,6,16,512]{3,2,1,0:T(8,128)}, f32[2,6,16,512]{3,2,1,0:T(8,128)}, u32[]{:S(2)}, u32[]{:S(2)}) collective-permute-start(f32[2,6,16,512]{3,2,1,0:T(8,128)} %get-tuple-element.108), channel_id=1, source_target_pairs={{32,0},{64,32},{96,64},{0,96},{160,128},{192,160},{224,192},{128,2... | collective-permute-start | bytes 1179656 | tf_op jit(solution)/shard_map/ppermute | solution.py:26
  67.3 8.2 %collective-permute-start.12 = (f32[2,6,16,512]{3,2,1,0:T(8,128)}, f32[2,6,16,512]{3,2,1,0:T(8,128)}, u32[]{:S(2)}, u32[]{:S(2)}) collective-permute-start(f32[2,6,16,512]{3,2,1,0:T(8,128)} %get-tuple-element.109), channel_id=1, source_target_pairs={{0,32},{32,64},{64,96},{96,0},{128,160},{160,192},{192,224},{224,1... | collective-permute-start | bytes 1179656 | tf_op jit(solution)/shard_map/ppermute | solution.py:26
  68.8 21.4 %slice-start = ((s8[5898240]{0:T(1024)(128)(4,1)}), s8[1703936]{0:T(1024)(128)(4,1)S(1)}, s32[]{:S(2)}) async-start(s8[5898240]{0:T(1024)(128)(4,1)} %bitcast.102), calls=%async_computation | async-start | bytes 3407872
  68.8 6.7 %copy-start.16 = (f32[2,2,6,16,512]{4,3,2,1,0:T(8,128)S(1)}, f32[2,2,6,16,512]{4,3,2,1,0:T(8,128)}, u32[]{:S(2)}) copy-start(f32[2,2,6,16,512]{4,3,2,1,0:T(8,128)} %copy-done.15) | copy-start | bytes 2359300
  68.8 6.7 %copy-start.18 = (f32[2,2,6,16,512]{4,3,2,1,0:T(8,128)S(1)}, f32[2,2,6,16,512]{4,3,2,1,0:T(8,128)}, u32[]{:S(2)}) copy-start(f32[2,2,6,16,512]{4,3,2,1,0:T(8,128)} %copy-done.17) | copy-start | bytes 2359300
  68.9 20.1 %copy-start.21 = (f32[2,2,4,16,512]{4,3,2,1,0:T(8,128)S(1)}, f32[2,2,4,16,512]{4,3,2,1,0:T(8,128)}, u32[]{:S(2)}) copy-start(f32[2,2,4,16,512]{4,3,2,1,0:T(8,128)} %copy-done.19) | copy-start | bytes 1572868
  68.9 20.1 %copy-start.23 = (f32[2,4,16,512]{3,2,1,0:T(8,128)S(1)}, f32[2,4,16,512]{3,2,1,0:T(8,128)}, u32[]{:S(2)}) copy-start(f32[2,4,16,512]{3,2,1,0:T(8,128)} %copy-done.22) | copy-start | bytes 786436
  68.9 20.1 %copy-start.25 = (f32[2,4,16,512]{3,2,1,0:T(8,128)S(1)}, f32[2,4,16,512]{3,2,1,0:T(8,128)}, u32[]{:S(2)}) copy-start(f32[2,4,16,512]{3,2,1,0:T(8,128)} %copy-done.24) | copy-start | bytes 786436
  68.9 20.1 %copy-start.27 = (f32[2,4,16,512]{3,2,1,0:T(8,128)S(1)}, f32[2,4,16,512]{3,2,1,0:T(8,128)}, u32[]{:S(2)}) copy-start(f32[2,4,16,512]{3,2,1,0:T(8,128)} %copy-done.26) | copy-start | bytes 786436
  68.9 21.3 %slice-start.1 = ((s8[5898240]{0:T(1024)(128)(4,1)}), s8[4194304]{0:T(1024)(128)(4,1)S(1)}, s32[]{:S(2)}) async-start(s8[5898240]{0:T(1024)(128)(4,1)} %bitcast.102), calls=%async_computation.1 | async-start | bytes 8388608
  73.1 17.1 %copy-start.10 = (f32[2,80,512]{2,1,0:T(8,128)S(1)}, f32[2,80,512]{2,1,0:T(8,128)}, u32[]{:S(2)}) copy-start(f32[2,80,512]{2,1,0:T(8,128)} %copy-done.9) | copy-start | bytes 983044
  76.9 24.6 %collective-permute-start.13 = (f32[2,2,6,16,512]{4,3,2,1,0:T(8,128)S(1)}, f32[2,2,6,16,512]{4,3,2,1,0:T(8,128)S(1)}, u32[]{:S(2)}, u32[]{:S(2)}) collective-permute-start(f32[2,2,6,16,512]{4,3,2,1,0:T(8,128)S(1)} %get-tuple-element.115), channel_id=1, source_target_pairs={{0,32},{32,64},{64,96},{96,0},{128,160},{160,192},{192,224},{224,1... | collective-permute-start | bytes 2359304 | tf_op jit(solution)/shard_map/ppermute | solution.py:26
  77.2 24.3 %collective-permute-start.14 = (f32[2,2,6,16,512]{4,3,2,1,0:T(8,128)S(1)}, f32[2,2,6,16,512]{4,3,2,1,0:T(8,128)S(1)}, u32[]{:S(2)}, u32[]{:S(2)}) collective-permute-start(f32[2,2,6,16,512]{4,3,2,1,0:T(8,128)S(1)} %get-tuple-element.116), channel_id=1, source_target_pairs={{32,0},{64,32},{96,64},{0,96},{160,128},{192,160},{224,192},{128,2... | collective-permute-start | bytes 2359304 | tf_op jit(solution)/shard_map/ppermute | solution.py:26
  79.7 21.8 %collective-permute-start.15 = (f32[2,6,16,512]{3,2,1,0:T(8,128)S(1)}, f32[2,6,16,512]{3,2,1,0:T(8,128)S(1)}, u32[]{:S(2)}, u32[]{:S(2)}) collective-permute-start(f32[2,6,16,512]{3,2,1,0:T(8,128)S(1)} %broadcast_select_fusion.1), channel_id=1, source_target_pairs={{0,128},{32,160},{64,192},{96,224},{128,0},{160,32},{192,64},{224,... | collective-permute-start | bytes 1179656 | tf_op jit(solution)/shard_map/ppermute | solution.py:26
  96.9 2.6 %copy-start.4 = (f32[36,80,512]{2,1,0:T(8,128)}, f32[36,80,512]{2,1,0:T(8,128)S(1)}, u32[]{:S(2)}) copy-start(f32[36,80,512]{2,1,0:T(8,128)S(1)} %get-tuple-element.154.refs_12_) | copy-start | bytes 17694724
  101.5 8.4 %copy-start.5 = (f32[36,80,512]{2,1,0:T(8,128)}, f32[36,80,512]{2,1,0:T(8,128)S(1)}, u32[]{:S(2)}) copy-start(f32[36,80,512]{2,1,0:T(8,128)S(1)} %get-tuple-element.155.refs_13_) | copy-start | bytes 17694724
  101.7 7.9 %collective-permute-start.24 = (f32[2,6,16,512]{3,2,1,0:T(8,128)S(1)}, f32[2,6,16,512]{3,2,1,0:T(8,128)S(1)}, u32[]{:S(2)}, u32[]{:S(2)}) collective-permute-start(f32[2,6,16,512]{3,2,1,0:T(8,128)S(1)} %get-tuple-element.161), channel_id=1, source_target_pairs={{0,32},{32,64},{64,96},{96,0},{128,160},{160,192},{192,224},{224,1... | collective-permute-start | bytes 1179656 | tf_op jit(solution)/shard_map/ppermute | solution.py:26
  101.7 7.8 %collective-permute-start.23 = (f32[2,6,16,512]{3,2,1,0:T(8,128)S(1)}, f32[2,6,16,512]{3,2,1,0:T(8,128)S(1)}, u32[]{:S(2)}, u32[]{:S(2)}) collective-permute-start(f32[2,6,16,512]{3,2,1,0:T(8,128)S(1)} %get-tuple-element.162), channel_id=1, source_target_pairs={{32,0},{64,32},{96,64},{0,96},{160,128},{192,160},{224,192},{128,2... | collective-permute-start | bytes 1179656 | tf_op jit(solution)/shard_map/ppermute | solution.py:26
  109.8 27.6 %collective-permute-start.25 = (f32[2,6,16,512]{3,2,1,0:T(8,128)S(1)}, f32[2,6,16,512]{3,2,1,0:T(8,128)S(1)}, u32[]{:S(2)}, u32[]{:S(2)}) collective-permute-start(f32[2,6,16,512]{3,2,1,0:T(8,128)S(1)} %broadcast_select_fusion), channel_id=1, source_target_pairs={{0,128},{32,160},{64,192},{96,224},{128,0},{160,32},{192,64},{224,... | collective-permute-start | bytes 1179656 | tf_op jit(solution)/shard_map/ppermute | solution.py:26
  114.5 22.6 %collective-permute-start.19 = (f32[10,16,512]{2,1,0:T(8,128)S(1)}, f32[10,16,512]{2,1,0:T(8,128)S(1)}, u32[]{:S(2)}, u32[]{:S(2)}) collective-permute-start(f32[10,16,512]{2,1,0:T(8,128)S(1)} %pad_maximum_fusion.refs_0_), channel_id=1, source_target_pairs={{0,128},{32,160},{64,192},{96,224},{128,0},{160,32},{192,64},{224,... | collective-permute-start | bytes 983048 | tf_op jit(solution)/shard_map/ppermute | solution.py:26
  115.4 24.5 %collective-permute-start.18 = (f32[10,16,512]{2,1,0:T(8,128)S(1)}, f32[10,16,512]{2,1,0:T(8,128)S(1)}, u32[]{:S(2)}, u32[]{:S(2)}) collective-permute-start(f32[10,16,512]{2,1,0:T(8,128)S(1)} %pad_maximum_fusion.refs_0_), channel_id=1, source_target_pairs={{0,64},{32,96},{64,0},{96,32},{128,192},{160,224},{192,128},{224,1... | collective-permute-start | bytes 983048 | tf_op jit(solution)/shard_map/ppermute | solution.py:26
  116.6 23.4 %collective-permute-start.17 = (f32[10,16,512]{2,1,0:T(8,128)S(1)}, f32[10,16,512]{2,1,0:T(8,128)S(1)}, u32[]{:S(2)}, u32[]{:S(2)}) collective-permute-start(f32[10,16,512]{2,1,0:T(8,128)S(1)} %pad_maximum_fusion.refs_0_), channel_id=1, source_target_pairs={{32,0},{64,32},{96,64},{0,96},{160,128},{192,160},{224,192},{128,2... | collective-permute-start | bytes 983048 | tf_op jit(solution)/shard_map/ppermute | solution.py:26
  118.1 22.1 %collective-permute-start.16 = (f32[10,16,512]{2,1,0:T(8,128)S(1)}, f32[10,16,512]{2,1,0:T(8,128)S(1)}, u32[]{:S(2)}, u32[]{:S(2)}) collective-permute-start(f32[10,16,512]{2,1,0:T(8,128)S(1)} %pad_maximum_fusion.refs_0_), channel_id=1, source_target_pairs={{0,32},{32,64},{64,96},{96,0},{128,160},{160,192},{192,224},{224,1... | collective-permute-start | bytes 983048 | tf_op jit(solution)/shard_map/ppermute | solution.py:26
  137.1 9.0 %collective-permute-start.22 = (f32[10,16,512]{2,1,0:T(8,128)S(1)}, f32[10,16,512]{2,1,0:T(8,128)S(1)}, u32[]{:S(2)}, u32[]{:S(2)}) collective-permute-start(f32[10,16,512]{2,1,0:T(8,128)S(1)} %collective-permute-done.19.refs_4_), channel_id=1, source_target_pairs={{0,64},{32,96},{64,0},{96,32},{128,192},{160,224},{192,128},{224,1... | collective-permute-start | bytes 983048 | tf_op jit(solution)/shard_map/ppermute | solution.py:26
  137.4 17.7 %collective-permute-start.21 = (f32[10,16,512]{2,1,0:T(8,128)S(1)}, f32[10,16,512]{2,1,0:T(8,128)S(1)}, u32[]{:S(2)}, u32[]{:S(2)}) collective-permute-start(f32[10,16,512]{2,1,0:T(8,128)S(1)} %collective-permute-done.19.refs_4_), channel_id=1, source_target_pairs={{32,0},{64,32},{96,64},{0,96},{160,128},{192,160},{224,192},{128,2... | collective-permute-start | bytes 983048 | tf_op jit(solution)/shard_map/ppermute | solution.py:26
  139.9 20.3 %collective-permute-start.20 = (f32[10,16,512]{2,1,0:T(8,128)S(1)}, f32[10,16,512]{2,1,0:T(8,128)S(1)}, u32[]{:S(2)}, u32[]{:S(2)}) collective-permute-start(f32[10,16,512]{2,1,0:T(8,128)S(1)} %collective-permute-done.19.refs_4_), channel_id=1, source_target_pairs={{0,32},{32,64},{64,96},{96,0},{128,160},{160,192},{192,224},{224,1... | collective-permute-start | bytes 983048 | tf_op jit(solution)/shard_map/ppermute | solution.py:26
  140.0 17.4 %collective-permute-start.26 = (f32[6,16,512]{2,1,0:T(8,128)S(1)}, f32[6,16,512]{2,1,0:T(8,128)S(1)}, u32[]{:S(2)}, u32[]{:S(2)}) collective-permute-start(f32[6,16,512]{2,1,0:T(8,128)S(1)} %fusion.5.refs_0_), channel_id=1, source_target_pairs={{0,128},{32,160},{64,192},{96,224},{128,0},{160,32},{192,64},{224,... | collective-permute-start | bytes 589832 | tf_op jit(solution)/shard_map/ppermute | solution.py:26
  140.2 20.1 %collective-permute-start.31 = (f32[6,16,512]{2,1,0:T(8,128)S(1)}, f32[6,16,512]{2,1,0:T(8,128)S(1)}, u32[]{:S(2)}, u32[]{:S(2)}) collective-permute-start(f32[6,16,512]{2,1,0:T(8,128)S(1)} %fusion.5.refs_0_), channel_id=1, source_target_pairs={{0,64},{32,96},{64,0},{96,32},{128,192},{160,224},{192,128},{224,1... | collective-permute-start | bytes 589832 | tf_op jit(solution)/shard_map/ppermute | solution.py:26
  146.2 18.9 %collective-permute-start.30 = (f32[6,16,512]{2,1,0:T(8,128)S(1)}, f32[6,16,512]{2,1,0:T(8,128)S(1)}, u32[]{:S(2)}, u32[]{:S(2)}) collective-permute-start(f32[6,16,512]{2,1,0:T(8,128)S(1)} %fusion.5.refs_0_), channel_id=1, source_target_pairs={{32,0},{64,32},{96,64},{0,96},{160,128},{192,160},{224,192},{128,2... | collective-permute-start | bytes 589832 | tf_op jit(solution)/shard_map/ppermute | solution.py:26
  155.1 14.1 %collective-permute-start.29 = (f32[6,16,512]{2,1,0:T(8,128)S(1)}, f32[6,16,512]{2,1,0:T(8,128)}, u32[]{:S(2)}, u32[]{:S(2)}) collective-permute-start(f32[6,16,512]{2,1,0:T(8,128)S(1)} %fusion.5.refs_0_), channel_id=1, source_target_pairs={{0,32},{32,64},{64,96},{96,0},{128,160},{160,192},{192,224},{224,1... | collective-permute-start | bytes 589832 | tf_op jit(solution)/shard_map/ppermute | solution.py:26
  157.5 17.5 %collective-permute-start.34 = (f32[6,16,512]{2,1,0:T(8,128)S(1)}, f32[6,16,512]{2,1,0:T(8,128)}, u32[]{:S(2)}, u32[]{:S(2)}) collective-permute-start(f32[6,16,512]{2,1,0:T(8,128)S(1)} %collective-permute-done.26.refs_4_), channel_id=1, source_target_pairs={{0,64},{32,96},{64,0},{96,32},{128,192},{160,224},{192,128},{224,1... | collective-permute-start | bytes 589832 | tf_op jit(solution)/shard_map/ppermute | solution.py:26
  160.2 14.7 %collective-permute-start.33 = (f32[6,16,512]{2,1,0:T(8,128)S(1)}, f32[6,16,512]{2,1,0:T(8,128)}, u32[]{:S(2)}, u32[]{:S(2)}) collective-permute-start(f32[6,16,512]{2,1,0:T(8,128)S(1)} %collective-permute-done.26.refs_4_), channel_id=1, source_target_pairs={{32,0},{64,32},{96,64},{0,96},{160,128},{192,160},{224,192},{128,2... | collective-permute-start | bytes 589832 | tf_op jit(solution)/shard_map/ppermute | solution.py:26
  160.2 14.7 %collective-permute-start.32 = (f32[6,16,512]{2,1,0:T(8,128)S(1)}, f32[6,16,512]{2,1,0:T(8,128)}, u32[]{:S(2)}, u32[]{:S(2)}) collective-permute-start(f32[6,16,512]{2,1,0:T(8,128)S(1)} %collective-permute-done.26.refs_4_), channel_id=1, source_target_pairs={{0,32},{32,64},{64,96},{96,0},{128,160},{160,192},{192,224},{224,1... | collective-permute-start | bytes 589832 | tf_op jit(solution)/shard_map/ppermute | solution.py:26
  161.8 2.2 copy-start
  165.1 6.0 %collective-permute-start.27 = (f32[32,2,512]{2,1,0:T(2,128)S(1)}, f32[32,2,512]{2,1,0:T(2,128)S(1)}, u32[]{:S(2)}, u32[]{:S(2)}) collective-permute-start(f32[32,2,512]{2,1,0:T(2,128)S(1)} %get-tuple-element.138), channel_id=1, source_target_pairs={{0,1},{1,2},{2,3},{4,5},{5,6},{6,7},{8,9},{9,10},{10,11},{12,13},{... | collective-permute-start | bytes 393224 | tf_op jit(solution)/shard_map/ppermute | solution.py:274
  169.2 5.7 %collective-permute-start.28 = (f32[32,2,512]{2,1,0:T(2,128)S(1)}, f32[32,2,512]{2,1,0:T(2,128)S(1)}, u32[]{:S(2)}, u32[]{:S(2)}) collective-permute-start(f32[32,2,512]{2,1,0:T(2,128)S(1)} %get-tuple-element.139), channel_id=1, source_target_pairs={{1,0},{2,1},{3,2},{5,4},{6,5},{7,6},{9,8},{10,9},{11,10},{13,12},{... | collective-permute-start | bytes 393224 | tf_op jit(solution)/shard_map/ppermute | solution.py:274
  175.5 2.5 %copy-start.6 = (f32[36,80,512]{2,1,0:T(8,128)}, f32[36,80,512]{2,1,0:T(8,128)S(1)}, u32[]{:S(2)}) copy-start(f32[36,80,512]{2,1,0:T(8,128)S(1)} %get-tuple-element.153.refs_10_) | copy-start | bytes 17694724
  177.9 23.2 %collective-permute-start.35 = (f32[2,80,512]{2,1,0:T(8,128)S(1)}, f32[2,80,512]{2,1,0:T(8,128)S(1)}, u32[]{:S(2)}, u32[]{:S(2)}) collective-permute-start(f32[2,80,512]{2,1,0:T(8,128)S(1)} %get-tuple-element.151), channel_id=1, source_target_pairs={{0,4},{4,8},{8,12},{12,16},{16,20},{20,24},{24,28},{1,5},{5,9},{9,... | collective-permute-start | bytes 983048 | tf_op jit(solution)/shard_map/ppermute | solution.py:274
  197.1 8.4 %collective-permute-start.36 = (f32[2,80,512]{2,1,0:T(8,128)S(1)}, f32[2,80,512]{2,1,0:T(8,128)S(1)}, u32[]{:S(2)}, u32[]{:S(2)}) collective-permute-start(f32[2,80,512]{2,1,0:T(8,128)S(1)} %get-tuple-element.152), channel_id=1, source_target_pairs={{4,0},{8,4},{12,8},{16,12},{20,16},{24,20},{28,24},{5,1},{9,5},{13... | collective-permute-start | bytes 983048 | tf_op jit(solution)/shard_map/ppermute | solution.py:274
  205.5 2.2 copy-start.1
  207.7 2.7 %copy-start.7 = (f32[36,80,512]{2,1,0:T(8,128)S(1)}, f32[36,80,512]{2,1,0:T(8,128)}, u32[]{:S(2)}) copy-start(f32[36,80,512]{2,1,0:T(8,128)} %copy-done.6) | copy-start | bytes 17694724
  (6 other events, 6.8 us)

commit v3 on v2

--- a/solution.py
+++ b/solution.py
@@ -45,6 +45,10 @@
 
 def hold(*arrays):
     return [pltpu.with_memory_space_constraint(x, pltpu.VMEM) for x in arrays]
+
+
+def in_hbm(*arrays):
+    return [pltpu.with_memory_space_constraint(x, pltpu.HBM) for x in arrays]
 
 
 def held(shape):
@@ -111,7 +115,7 @@
         + [pltpu.SemaphoreType.DMA((2, n * count))],
         compiler_params=big,
         name="partials",
-    )(jnp.stack(starts).astype(jnp.int32), planes, groups, *[pltpu.with_memory_space_constraint(x, pltpu.HBM) for x in (source_grad, adjoint_grad)])
+    )(jnp.stack(starts).astype(jnp.int32), planes, groups, *in_hbm(source_grad, adjoint_grad))
 
 
 def place(pieces, segments, starts_ref, plane_ref, group_ref, ms_ref, g_ref, rim, pad):
@@ -126,7 +130,7 @@
 
 
 def frame_kernel(n, segments, starts, planes, groups, *refs):
-    pieces, (ms, g, low, high) = refs[:n], refs[n:]
+    pieces, (ms, g, low, high, first, last) = refs[:n], refs[n:]
     place(pieces, segments, starts, planes, groups, ms, g, 0, 0)
     rows = ms.shape[1]
 
@@ -136,6 +140,20 @@
         return 0
 
     lax.fori_loop(0, ms.shape[0], rim, 0)
+    first[...] = g[:RIM]
+    last[...] = g[ms.shape[0] - RIM :]
+
+
+def corner_kernel(first, last, before, after, low, high):
+    planes, rows, depth = first.shape
+    zero = jnp.zeros((PAD, depth), jnp.float32)
+    for tile, out, at in ((first, low, 0), (last, high, before.shape[0] - RIM)):
+        for p in range(planes):
+            out[p, :PAD] = zero
+            out[p, PAD + rows :] = zero
+            out[p, PAD : PAD + rows] = tile[p]
+            out[p, PAD - RIM : PAD] = before[at + p]
+            out[p, PAD + rows : PAD + rows + RIM] = after[at + p]
 
 
 def rim_kernel(tile, before, after, wide, low, high):
@@ -211,11 +229,15 @@
 
 def smooth_kernel(n, segments, starts, planes, groups, *refs):
     pieces, refs = refs[:n], refs[n:]
-    low, high, wide, ms_hbm, s_hbm, a_hbm, t_hbm, out_hbm, g, g1, ms, s, a, t, out, sems = refs
-    count, rows = out.shape[:2]
+    low, high, before, after, ms_hbm, tile_hbm, s_hbm, a_hbm, t_hbm, out_hbm, g, g1, s, a, t, sems = refs
+    count, rows = t.shape[:2]
+    ms = g1.at[pl.ds(0, count), pl.ds(0, rows)]
     framed, step = g.shape[0] // GROUPS, count // GROUPS
     ms_copy = pltpu.make_async_copy(ms_hbm, ms, sems.at[0, 0])
+    inside = g.at[pl.ds(RIM, count), pl.ds(PAD, rows)]
+    g_copy = pltpu.make_async_copy(tile_hbm, inside, sems.at[0, 1])
     ms_copy.start()
+    g_copy.start()
     arrivals = []
     for k in range(GROUPS):
         part = pl.ds(k * framed, framed)
@@ -231,8 +253,21 @@
         t_copies.append(pltpu.make_async_copy(t_hbm.at[part], t.at[part], sems.at[3, k]))
     for c in arrivals[0]:
         c.start()
-    assemble(wide, low, high, g)
+    g[:RIM] = low[...]
+    g[count + RIM :] = high[...]
+    zero = jnp.zeros((PAD, g.shape[2]), jnp.float32)
+
+    def rims(p, _):
+        at = p + RIM
+        g[at, :PAD] = zero
+        g[at, PAD + rows :] = zero
+        g[at, PAD - RIM : PAD] = before[p]
+        g[at, PAD + rows : PAD + rows + RIM] = after[p]
+        return 0
+
+    lax.fori_loop(0, count, rims, 0)
     ms_copy.wait()
+    g_copy.wait()
     for c in sum(arrivals[1:], []) + t_copies:
         c.start()
     place(pieces, segments, starts, planes, groups, ms, g, RIM, PAD)
@@ -252,7 +287,7 @@
     def second(p, _):
         for r, m in chunks(rows):
             here, total = neighbours(g1, p + RIM, r, m)
-            out[p, r - PAD : r - PAD + m] = (
+            t[p, r - PAD : r - PAD + m] = (
                 t[p, r - PAD : r - PAD + m] * here + smoothing_rate * s[p + RIM, r : r + m] * total
             )
         return 0
@@ -262,7 +297,7 @@
         t_copies[k].wait()
         lax.fori_loop(k * step, (k + 1) * step, second, 0)
         part = pl.ds(k * step, step)
-        leaving.append(pltpu.make_async_copy(out.at[part], out_hbm.at[part], sems.at[4, k]))
+        leaving.append(pltpu.make_async_copy(t.at[part], out_hbm.at[part], sems.at[4, k]))
         leaving[-1].start()
     for c in leaving:
         c.wait()
@@ -347,23 +382,22 @@
     end0, end1 = send(end0, DOWN), send(end1, UP)
 
     up2, down2, keep2, own2 = sums_of(1)
-    before, after = halo(root[:, :RIM], root[:, -RIM:], "line")
     own, leaving = finish(own, up, down, end0, end1)
-    up2, down2, leaving, root = after_rest((up2, down2, leaving, root))
+    up2, down2, leaving = after_rest((up2, down2, leaving))
     other = send(leaving, SWAP)
     up, down = first_step(up2, down2)
-    wide, low, high = with_rims(root, before, after)
-    low, high = halo(low, high, "profile")
-    up, down, wide, low, high = after_rest((up, down, wide, low, high))
     end0, end1 = second_step(up, down, keep2)
     source_grad, adjoint_grad, end0, end1, other = after_rest((source_grad, adjoint_grad, end0, end1, other))
     end0, end1 = send(end0, DOWN), send(end1, UP)
 
     up3, down3, keep3, own3 = sums_of(2)
     own2, leaving = finish(own2, up, down, end0, end1)
-    up3, down3, leaving, wide = after_rest((up3, down3, leaving, wide))
+    up3, down3, leaving, root = after_rest((up3, down3, leaving, root))
     other2 = send(leaving, SWAP)
     up, down = first_step(up3, down3)
+    before, after = halo(root[:, :RIM], root[:, -RIM:], "line")
+    wide, low, high = with_rims(root, before, after)
+    low, high = halo(low, high, "profile")
     s, a, t = pl.pallas_call(
         coefficient_kernel,
         out_shape=(held(wide.shape),) * 2 + (held(log_model.shape),),
@@ -372,18 +406,18 @@
         compiler_params=big,
         name="coefficients",
     )(*hold(wide, low, high))
-    up, down, s, a, t, other2 = after_rest((up, down, s, a, t, other2))
+    up, down, wide, other2 = after_rest((up, down, wide, other2))
     end0, end1 = second_step(up, down, keep3)
     end0, end1 = send(end0, DOWN), send(end1, UP)
     frame = jnp.concatenate([normalised(own, other), normalised(own2, other2)])
     frame_other = send(frame, SWAP)
     frame_ring = ring(frame)
+    end0, end1, frame_other, s, a, t = after_rest((end0, end1, frame_other, s, a, t))
     own3, leaving = finish(own3, up, down, end0, end1)
     inner = normalised(own3, send(leaving, SWAP))
     inner_other = send(inner, SWAP)
     other_ring = ring(frame_other)
     inner_rings = ring(inner) + ring(inner_other)
-    frame_ring, other_ring, inner_other = after_rest((frame_ring, other_ring, inner_other))
 
     def segments_of(ranges):
         segments = [(i, offset, parts[k]) for i, piece in enumerate(ranges) for k, _, offset, _ in piece]
@@ -392,18 +426,25 @@
 
     pieces = frame_ring + other_ring
     segments, starts = segments_of([[(0, z, 0, q), (1, z, parts[0], q)] for z in (half, 1 - half) for q in ring_offsets])
-    rim_y = held((tile_x, RIM, depth_cells))
-    g, low, high = pl.pallas_call(
+    rim_y, rim_x = held((tile_x, RIM, depth_cells)), held((RIM, tile_y, depth_cells))
+    g, low, high, first, last = pl.pallas_call(
         functools.partial(frame_kernel, len(pieces), segments),
-        out_shape=(held(log_model.shape), rim_y, rim_y),
+        out_shape=(jax.ShapeDtypeStruct(log_model.shape, jnp.float32), rim_y, rim_y, rim_x, rim_x),
         in_specs=smem(3) + vmem(len(pieces) + 1),
-        out_specs=vmem(3),
+        out_specs=vmem(5),
         compiler_params=big,
         name="frame",
     )(starts, planes, groups, *hold(*pieces, masked))
     before, after = halo(low, high, "line")
     before, after, inner_rings = after_rest((before, after, inner_rings))
-    g, low, high = with_rims(g, before, after)
+    low, high = pl.pallas_call(
+        corner_kernel,
+        out_shape=(held((RIM, tile_y + 2 * PAD, depth_cells)),) * 2,
+        in_specs=vmem(4),
+        out_specs=vmem(2),
+        compiler_params=big,
+        name="corners",
+    )(*hold(first, last, before, after))
     low, high = halo(low, high, "profile")
     pieces = inner_rings
     segments, starts = segments_of(
@@ -414,13 +455,13 @@
     return pl.pallas_call(
         functools.partial(smooth_kernel, len(pieces), segments),
         out_shape=jax.ShapeDtypeStruct(log_model.shape, jnp.float32),
-        in_specs=smem(3) + vmem(len(pieces) + 3) + [anywhere] * 4,
+        in_specs=smem(3) + vmem(len(pieces) + 4) + [anywhere] * 5,
         out_specs=anywhere,
-        scratch_shapes=[wide_f32, wide_f32, tile_f32, wide_f32, wide_f32, tile_f32, tile_f32]
+        scratch_shapes=[wide_f32, wide_f32, wide_f32, wide_f32, tile_f32]
         + [pltpu.SemaphoreType.DMA((5, GROUPS))],
-        compiler_params=pltpu.CompilerParams(vmem_limit_bytes=40 * 2**20),
+        compiler_params=pltpu.CompilerParams(vmem_limit_bytes=30 * 2**20),
         name="smooth",
-    )(starts, planes, groups, *hold(*pieces, low, high, g), masked, s, a, t)
+    )(starts, planes, groups, *hold(*pieces, low, high, before, after), *in_hbm(masked, g, s, a, t))
 
 
 def solution(mesh):

time: 226 us -> 206 us (0.912)
  starting transfers between devices: 93 us -> 68.5 us
  waiting for transfers between devices: 62.9 us -> 72.6 us
  local copies, waits for them, and re-layouts: 19.3 us -> 14.3 us
  other arithmetic: 14 us -> 11.4 us
    ppermute x4, starting transfers between devices: 35.2 us -> 21.9 us  [halo(): lax.ppermute(high, axis, up)]
    ppermute x29, starting transfers between devices: 51.3 us -> 40.2 us  [send(): return lax.ppermute(x, 'source', pairs)]
    ppermute x29, waiting for transfers between devices: 48.9 us -> 58.9 us  [send(): return lax.ppermute(x, 'source', pairs)]
    unnamed x66 -> x42, local copies, waits for them, and re-layouts: 18.8 us -> 13.7 us
  transfers between devices with their start and end apart: 37 -> 37, of which waited for: 16 -> 23; matrix products, arithmetic and copies ran while one was open for 5% -> 5% of each run, Pallas kernels for 7% -> 8%
where the time goes in v3:
time: 206 us; the launch traced here: 203 us
  waiting for transfers between devices  72.6 us (35%)
  starting transfers between devices  68.5 us (33%)
  Pallas kernels  35.6 us (17%)
  local copies, waits for them, and re-layouts  14.3 us (7%)
  other arithmetic  11.4 us (6%)
    ppermute x29, waiting for transfers between devices, send(): return lax.ppermute(x, 'source', pairs)  58.9 us
    ppermute x29, starting transfers between devices, send(): return lax.ppermute(x, 'source', pairs)  40.2 us
    ppermute x4, starting transfers between devices, halo(): lax.ppermute(high, axis, up)  21.9 us
    pallas_call x1, Pallas kernels, shards(): pl.pallas_call(functools.partial(smooth_kernel, len(pieces), segments), o...  16.3 us
    unnamed x42, local copies, waits for them, and re-layouts  13.7 us
    pallas_call x3, Pallas kernels, partials(): pl.pallas_call(body, out_shape=[held((2, 2, count, ROWS, depth))] * (n //...  10.9 us
    ppermute x4, waiting for transfers between devices, halo(): lax.ppermute(low, axis, [(j, i) for i, j in up])  9.65 us
    pallas_call x1, Pallas kernels, shards(): pl.pallas_call(coefficient_kernel, out_shape=(held(wide.shape),) * 2 + (h...  6.72 us
  transfers between devices with their start and end apart: 37, of which 23 were waited for; matrix products, arithmetic and copies ran while one was open for 5% of the time, Pallas kernels for 8%

profile of v3, /device:TPU:33, one launch (start us, length us, event | category | flops | bytes accessed | tf_op | source)
XLA Modules:
  0.0 203.3 jit_solution(10344132947711990824)
XLA Ops:
  0.1 0.7 copy-done.6
  0.7 0.7 copy-done.8
  1.4 3.1 %partials.3 = (f32[2,2,4,16,512]{4,3,2,1,0:T(8,128)S(1)}, f32[2,2,4,16,512]{4,3,2,1,0:T(8,128)S(1)}, f32[2,2,4,16,512]{4,3,2,1,0:T(8,128)S(1)}, f32[2,2,4,16,512]{4,3,2,1,0:T(8,128)S(1)}) custom-call(s32[8]{0:T(128)S(1)} %stack.193.start_ref, s32[128]{0:T(128)S(1)} %copy-done.8, s32[128]{0:T(128)S(1)} %copy-done.6, bf16[1,3,32,64,512]{4,3,2,1,0:T(8,128)(2,1)} %f_hbm.3, ...), custom_call_target="tpu_custom_call" | custom-call | tf_op jit(solution)/shard_map/partials/pallas_call | solution.py:109
  4.5 1.4 collective-permute-start
  5.9 1.5 collective-permute-start.1
  7.8 5.6 %fusion = (f32[32,64,512]{2,1,0:T(8,128)}, f32[32,64,512]{2,1,0:T(8,128)}) fusion(s32[32,64]{1,0:T(8,128)S(1)} %fusion.2, f32[32,64,512]{2,1,0:T(8,128)} %param.10, s32[32,64]{1,0:T(8,128)S(1)} %copy-done.18), kind=kLoop, calls=%fused_computation.3 | loop fusion | flops 7340032 | bytes 12599296 | tf_op jit(solution)/shard_map/jit(_where)/select_n | solution.py:378
  13.4 5.3 %collective-permute-done = f32[2,2,4,16,512]{4,3,2,1,0:T(8,128)S(1)} collective-permute-done((f32[2,2,4,16,512]{4,3,2,1,0:T(8,128)S(1)}, f32[2,2,4,16,512]{4,3,2,1,0:T(8,128)S(1)}, u32[]{:S(2)}, u32[]{:S(2)}) %collective-permute-start) | collective-permute-done | bytes 524320 | tf_op jit(solution)/shard_map/ppermute | solution.py:26
  18.7 0.9 add_bitcast_fusion.2
  19.6 2.5 %collective-permute-start.2 = (f32[2,4,16,512]{3,2,1,0:T(8,128)}, f32[2,4,16,512]{3,2,1,0:T(8,128)S(1)}, u32[]{:S(2)}, u32[]{:S(2)}) collective-permute-start(f32[2,4,16,512]{3,2,1,0:T(8,128)} %get-tuple-element.79), channel_id=1, source_target_pairs={{32,0},{64,32},{96,64},{0,96},{160,128},{192,160},{224,192},{128,2... | collective-permute-start | bytes 786440 | tf_op jit(solution)/shard_map/ppermute | solution.py:26
  22.2 3.9 %partials.4 = (f32[2,2,6,16,512]{4,3,2,1,0:T(8,128)S(1)}, f32[2,2,6,16,512]{4,3,2,1,0:T(8,128)S(1)}, f32[2,2,6,16,512]{4,3,2,1,0:T(8,128)S(1)}, f32[2,2,6,16,512]{4,3,2,1,0:T(8,128)S(1)}) custom-call(s32[8]{0:T(128)S(1)} %stack.202.start_ref, s32[128]{0:T(128)S(1)} %copy-done.9, s32[128]{0:T(128)S(1)} %copy-done.7, bf16[1,3,32,64,512]{4,3,2,1,0:T(8,128)(2,1)} %f_hbm.3, ...), custom_call_target="tpu_custom_call" | custom-call | tf_op jit(solution)/shard_map/partials/pallas_call | solution.py:109
  26.4 2.8 %collective-permute-done.3 = f32[2,4,16,512]{3,2,1,0:T(8,128)S(1)} collective-permute-done((f32[2,4,16,512]{3,2,1,0:T(8,128)S(1)}, f32[2,4,16,512]{3,2,1,0:T(8,128)S(1)}, u32[]{:S(2)}, u32[]{:S(2)}) %collective-permute-start.3) | collective-permute-done | bytes 262176 | tf_op jit(solution)/shard_map/ppermute | solution.py:26
  30.4 1.0 collective-permute-start.5
  31.3 6.0 %collective-permute-start.6 = (f32[2,4,16,512]{3,2,1,0:T(8,128)S(1)}, f32[2,4,16,512]{3,2,1,0:T(8,128)S(1)}, u32[]{:S(2)}, u32[]{:S(2)}) collective-permute-start(f32[2,4,16,512]{3,2,1,0:T(8,128)S(1)} %broadcast_select_fusion.2), channel_id=1, source_target_pairs={{0,128},{32,160},{64,192},{96,224},{128,0},{160,32},{192,64},{224,... | collective-permute-start | bytes 786440 | tf_op jit(solution)/shard_map/ppermute | solution.py:26
  37.4 8.7 %collective-permute-done.4 = f32[2,2,6,16,512]{4,3,2,1,0:T(8,128)S(1)} collective-permute-done((f32[2,2,6,16,512]{4,3,2,1,0:T(8,128)S(1)}, f32[2,2,6,16,512]{4,3,2,1,0:T(8,128)S(1)}, u32[]{:S(2)}, u32[]{:S(2)}) %collective-permute-start.4) | collective-permute-done | bytes 786464 | tf_op jit(solution)/shard_map/ppermute | solution.py:26
  46.0 1.7 collective-permute-done.5
  47.7 1.0 fusion.7
  48.8 0.7 copy-done.16
  49.8 1.2 collective-permute-start.8
  51.1 3.9 %partials.5 = (f32[2,2,6,16,512]{4,3,2,1,0:T(8,128)S(1)}, f32[2,2,6,16,512]{4,3,2,1,0:T(8,128)S(1)}, f32[2,2,6,16,512]{4,3,2,1,0:T(8,128)S(1)}, f32[2,2,6,16,512]{4,3,2,1,0:T(8,128)S(1)}) custom-call(s32[8]{0:T(128)S(1)} %stack.211.start_ref, s32[128]{0:T(128)S(1)} %copy-done.9, s32[128]{0:T(128)S(1)} %copy-done.7, bf16[1,3,32,64,512]{4,3,2,1,0:T(8,128)(2,1)} %f_hbm.3, ...), custom_call_target="tpu_custom_call" | custom-call | tf_op jit(solution)/shard_map/partials/pallas_call | solution.py:109
  55.0 1.3 collective-permute-done.7
  56.3 1.6 collective-permute-done.8
  57.9 1.2 broadcast_select_fusion.1
  59.4 2.5 %collective-permute-start.10 = (f32[2,2,6,16,512]{4,3,2,1,0:T(8,128)S(1)}, f32[2,2,6,16,512]{4,3,2,1,0:T(8,128)S(1)}, u32[]{:S(2)}, u32[]{:S(2)}) collective-permute-start(f32[2,2,6,16,512]{4,3,2,1,0:T(8,128)S(1)} %get-tuple-element.99), channel_id=1, source_target_pairs={{32,0},{64,32},{96,64},{0,96},{160,128},{192,160},{224,192},{128,2... | collective-permute-start | bytes 2359304 | tf_op jit(solution)/shard_map/ppermute | solution.py:26
  62.1 6.3 %collective-permute-start.13 = (f32[2,6,16,512]{3,2,1,0:T(8,128)S(1)}, f32[2,6,16,512]{3,2,1,0:T(8,128)S(1)}, u32[]{:S(2)}, u32[]{:S(2)}) collective-permute-start(f32[2,6,16,512]{3,2,1,0:T(8,128)S(1)} %broadcast_select_fusion.1), channel_id=1, source_target_pairs={{0,128},{32,160},{64,192},{96,224},{128,0},{160,32},{192,64},{224,... | collective-permute-start | bytes 1179656 | tf_op jit(solution)/shard_map/ppermute | solution.py:26
  68.5 1.3 collective-permute-start.12
  69.8 4.0 %collective-permute-start.11 = (f32[32,2,512]{2,1,0:T(2,128)S(1)}, f32[32,2,512]{2,1,0:T(2,128)S(1)}, u32[]{:S(2)}, u32[]{:S(2)}) collective-permute-start(f32[32,2,512]{2,1,0:T(2,128)S(1)} %get-tuple-element.140), channel_id=1, source_target_pairs={{0,1},{1,2},{2,3},{4,5},{5,6},{6,7},{8,9},{9,10},{10,11},{12,13},{... | collective-permute-start | bytes 393224 | tf_op jit(solution)/shard_map/ppermute | solution.py:309
  73.8 0.7 collective-permute-done.12.after
  74.5 1.2 collective-permute-done.11.before
  76.2 9.8 %collective-permute-start.20 = (f32[2,80,512]{2,1,0:T(8,128)S(1)}, f32[2,80,512]{2,1,0:T(8,128)S(1)}, u32[]{:S(2)}, u32[]{:S(2)}) collective-permute-start(f32[2,80,512]{2,1,0:T(8,128)S(1)} %get-tuple-element.107), channel_id=1, source_target_pairs={{0,4},{4,8},{8,12},{12,16},{16,20},{20,24},{24,28},{1,5},{5,9},{9,... | collective-permute-start | bytes 983048 | tf_op jit(solution)/shard_map/ppermute | solution.py:309
  86.1 1.9 collective-permute-start.21
  88.1 1.3 select_add_fusion.1
  89.7 2.7 %collective-permute-start.17 = (f32[2,6,16,512]{3,2,1,0:T(8,128)S(1)}, f32[2,6,16,512]{3,2,1,0:T(8,128)S(1)}, u32[]{:S(2)}, u32[]{:S(2)}) collective-permute-start(f32[2,6,16,512]{3,2,1,0:T(8,128)S(1)} %get-tuple-element.142), channel_id=1, source_target_pairs={{32,0},{64,32},{96,64},{0,96},{160,128},{192,160},{224,192},{128,2... | collective-permute-start | bytes 1179656 | tf_op jit(solution)/shard_map/ppermute | solution.py:26
  92.3 0.9 collective-permute-start.19
  93.2 1.6 collective-permute-done.21.high
  94.8 6.7 %coefficients.1 = (f32[36,80,512]{2,1,0:T(8,128)S(1)}, f32[36,80,512]{2,1,0:T(8,128)S(1)}, f32[32,64,512]{2,1,0:T(8,128)S(1)}) custom-call(f32[36,80,512]{2,1,0:T(8,128)S(1)} %get-tuple-element.101.wide, f32[2,80,512]{2,1,0:T(8,128)S(1)} %collective-permute-done.20.low, f32[2,80,512]{2,1,0:T(8,128)S(1)} %collective-permute-done.21.high), custom_call_target="tpu_custom_call" | custom-call | tf_op jit(solution)/shard_map/coefficients/pallas_call | solution.py:401
  101.5 2.6 %copy-done.2 = f32[36,80,512]{2,1,0:T(8,128)} copy-done((f32[36,80,512]{2,1,0:T(8,128)}, f32[36,80,512]{2,1,0:T(8,128)S(1)}, u32[]{:S(2)}) %copy-start.2) | copy-done | bytes 5898264
  104.1 2.5 %copy-done.3 = f32[36,80,512]{2,1,0:T(8,128)} copy-done((f32[36,80,512]{2,1,0:T(8,128)}, f32[36,80,512]{2,1,0:T(8,128)S(1)}, u32[]{:S(2)}) %copy-start.3) | copy-done | bytes 5898264
  106.6 1.9 copy-done.4
  108.5 4.1 %collective-permute-done.19.refs_4_ = f32[10,16,512]{2,1,0:T(8,128)S(1)} collective-permute-done((f32[10,16,512]{2,1,0:T(8,128)S(1)}, f32[10,16,512]{2,1,0:T(8,128)S(1)}, u32[]{:S(2)}, u32[]{:S(2)}) %collective-permute-start.19) | collective-permute-done | bytes 327712 | tf_op jit(solution)/shard_map/ppermute | solution.py:26
  112.8 0.9 collective-permute-start.27
  113.7 0.8 collective-permute-start.15
  115.2 3.0 %collective-permute-start.24 = (f32[10,16,512]{2,1,0:T(8,128)S(1)}, f32[10,16,512]{2,1,0:T(8,128)S(1)}, u32[]{:S(2)}, u32[]{:S(2)}) collective-permute-start(f32[10,16,512]{2,1,0:T(8,128)S(1)} %collective-permute-done.19.refs_4_), channel_id=1, source_target_pairs={{0,64},{32,96},{64,0},{96,32},{128,192},{160,224},{192,128},{224,1... | collective-permute-start | bytes 983048 | tf_op jit(solution)/shard_map/ppermute | solution.py:26
  118.2 5.2 %collective-permute-done.16.refs_3_ = f32[10,16,512]{2,1,0:T(8,128)S(1)} collective-permute-done((f32[10,16,512]{2,1,0:T(8,128)S(1)}, f32[10,16,512]{2,1,0:T(8,128)S(1)}, u32[]{:S(2)}, u32[]{:S(2)}) %collective-permute-start.16) | collective-permute-done | bytes 327712 | tf_op jit(solution)/shard_map/ppermute | solution.py:26
  123.3 7.6 %collective-permute-done.27 = f32[2,6,16,512]{3,2,1,0:T(8,128)S(1)} collective-permute-done((f32[2,6,16,512]{3,2,1,0:T(8,128)S(1)}, f32[2,6,16,512]{3,2,1,0:T(8,128)S(1)}, u32[]{:S(2)}, u32[]{:S(2)}) %collective-permute-start.27) | collective-permute-done | bytes 393248 | tf_op jit(solution)/shard_map/ppermute | solution.py:26
  131.4 4.3 %collective-permute-start.31 = (f32[6,16,512]{2,1,0:T(8,128)S(1)}, f32[6,16,512]{2,1,0:T(8,128)S(1)}, u32[]{:S(2)}, u32[]{:S(2)}) collective-permute-start(f32[6,16,512]{2,1,0:T(8,128)S(1)} %fusion.11.refs_0_), channel_id=1, source_target_pairs={{0,128},{32,160},{64,192},{96,224},{128,0},{160,32},{192,64},{224,... | collective-permute-start | bytes 589832 | tf_op jit(solution)/shard_map/ppermute | solution.py:26
  135.7 1.2 collective-permute-start.30
  137.4 6.1 %collective-permute-done.23.refs_6_ = f32[10,16,512]{2,1,0:T(8,128)S(1)} collective-permute-done((f32[10,16,512]{2,1,0:T(8,128)S(1)}, f32[10,16,512]{2,1,0:T(8,128)S(1)}, u32[]{:S(2)}, u32[]{:S(2)}) %collective-permute-start.23) | collective-permute-done | bytes 327712 | tf_op jit(solution)/shard_map/ppermute | solution.py:26
  143.5 4.0 %collective-permute-done.22.refs_5_ = f32[10,16,512]{2,1,0:T(8,128)S(1)} collective-permute-done((f32[10,16,512]{2,1,0:T(8,128)S(1)}, f32[10,16,512]{2,1,0:T(8,128)S(1)}, u32[]{:S(2)}, u32[]{:S(2)}) %collective-permute-start.22) | collective-permute-done | bytes 327712 | tf_op jit(solution)/shard_map/ppermute | solution.py:26
  147.5 2.2 %copy-done = f32[32,64,512]{2,1,0:T(8,128)S(1)} copy-done((f32[32,64,512]{2,1,0:T(8,128)S(1)}, f32[32,64,512]{2,1,0:T(8,128)}, u32[]{:S(2)}) %copy-start) | copy-done | bytes 4194328
  149.7 1.1 frame.1
  150.9 2.0 copy-done.5
  152.9 4.1 %collective-permute-start.25 = (f32[32,2,512]{2,1,0:T(2,128)S(1)}, f32[32,2,512]{2,1,0:T(2,128)S(1)}, u32[]{:S(2)}, u32[]{:S(2)}) collective-permute-start(f32[32,2,512]{2,1,0:T(2,128)S(1)} %get-tuple-element.114), channel_id=1, source_target_pairs={{0,1},{1,2},{2,3},{4,5},{5,6},{6,7},{8,9},{9,10},{10,11},{12,13},{... | collective-permute-start | bytes 393224 | tf_op jit(solution)/shard_map/ppermute | solution.py:309
  156.9 1.3 collective-permute-start.26
  158.3 0.9 collective-permute-done.25.before.refs_10_
  160.0 3.0 %collective-permute-done.26.after.refs_11_ = f32[32,2,512]{2,1,0:T(2,128)S(1)} collective-permute-done((f32[32,2,512]{2,1,0:T(2,128)S(1)}, f32[32,2,512]{2,1,0:T(2,128)S(1)}, u32[]{:S(2)}, u32[]{:S(2)}) %collective-permute-start.26) | collective-permute-done | bytes 131104 | tf_op jit(solution)/shard_map/ppermute | solution.py:309
  163.0 1.5 collective-permute-start.32
  164.5 4.1 %collective-permute-done.28.refs_1_ = f32[6,16,512]{2,1,0:T(8,128)S(1)} collective-permute-done((f32[6,16,512]{2,1,0:T(8,128)S(1)}, f32[6,16,512]{2,1,0:T(8,128)S(1)}, u32[]{:S(2)}, u32[]{:S(2)}) %collective-permute-start.28) | collective-permute-done | bytes 196640 | tf_op jit(solution)/shard_map/ppermute | solution.py:26
  168.6 3.8 %collective-permute-done.33.refs_6_ = f32[6,16,512]{2,1,0:T(8,128)S(1)} collective-permute-done((f32[6,16,512]{2,1,0:T(8,128)S(1)}, f32[6,16,512]{2,1,0:T(8,128)S(1)}, u32[]{:S(2)}, u32[]{:S(2)}) %collective-permute-start.33) | collective-permute-done | bytes 196640 | tf_op jit(solution)/shard_map/ppermute | solution.py:26
  172.3 2.0 collective-permute-done.32.refs_5_
  174.4 4.0 %collective-permute-start.35 = (f32[2,80,512]{2,1,0:T(8,128)S(1)}, f32[2,80,512]{2,1,0:T(8,128)S(1)}, u32[]{:S(2)}, u32[]{:S(2)}) collective-permute-start(f32[2,80,512]{2,1,0:T(8,128)S(1)} %get-tuple-element.131), channel_id=1, source_target_pairs={{0,4},{4,8},{8,12},{12,16},{16,20},{20,24},{24,28},{1,5},{5,9},{9,... | collective-permute-start | bytes 983048 | tf_op jit(solution)/shard_map/ppermute | solution.py:309
  178.4 1.9 collective-permute-start.36
  180.4 1.9 collective-permute-done.35.refs_8_
  182.4 4.4 %collective-permute-done.36.refs_9_ = f32[2,80,512]{2,1,0:T(8,128)S(1)} collective-permute-done((f32[2,80,512]{2,1,0:T(8,128)S(1)}, f32[2,80,512]{2,1,0:T(8,128)S(1)}, u32[]{:S(2)}, u32[]{:S(2)}) %collective-permute-start.36) | collective-permute-done | bytes 327712 | tf_op jit(solution)/shard_map/ppermute | solution.py:309
  186.8 16.3 %smooth.1 = f32[32,64,512]{2,1,0:T(8,128)} custom-call(s32[8]{0:T(128)S(1)} %stack.167.starts, s32[128]{0:T(128)S(1)} %copy-done.9, s32[128]{0:T(128)S(1)} %copy-done.7, f32[6,16,512]{2,1,0:T(8,128)S(1)} %fusion.11.refs_0_, f32[6,16,512]{2,1,0:T(8,128)S(1)} %collective-permute-done.28.refs_1_, f32[6,16,512]{2,1,0:T(8,128)S(1)} %collective-permute-done.29.refs_2_, ...), custom_call_target="tpu_custom_call" | custom-call | tf_op jit(solution)/shard_map/smooth/pallas_call | solution.py:455
  (84 shorter events, 6.6 us)
Async XLA Ops:
  0.1 0.7 copy-start.6
  0.7 0.7 copy-start.8
  1.4 6.0 %copy-start.19 = (s32[256]{0:T(256)S(1)}, s32[256]{0:T(256)}, u32[]{:S(2)}) copy-start(s32[256]{0:T(256)} %param.13) | copy-start | bytes 3076
  1.4 6.0 %copy-start.20 = (s32[8]{0:T(128)S(1)}, s32[8]{0:T(128)}, u32[]{:S(2)}) copy-start(s32[8]{0:T(128)} %param.12) | copy-start | bytes 100
  1.4 6.1 %copy-start.18 = (s32[32,64]{1,0:T(8,128)S(1)}, s32[32,64]{1,0:T(8,128)}, u32[]{:S(2)}) copy-start(s32[32,64]{1,0:T(8,128)} %param.11) | copy-start | bytes 24580
  4.5 14.2 %collective-permute-start = (f32[2,2,4,16,512]{4,3,2,1,0:T(8,128)S(1)}, f32[2,2,4,16,512]{4,3,2,1,0:T(8,128)S(1)}, u32[]{:S(2)}, u32[]{:S(2)}) collective-permute-start(f32[2,2,4,16,512]{4,3,2,1,0:T(8,128)S(1)} %get-tuple-element.73), channel_id=1, source_target_pairs={{0,32},{32,64},{64,96},{96,0},{128,160},{160,192},{192,224},{224,1... | collective-permute-start | bytes 1572872 | tf_op jit(solution)/shard_map/ppermute | solution.py:26
  5.9 12.8 %collective-permute-start.1 = (f32[2,2,4,16,512]{4,3,2,1,0:T(8,128)S(1)}, f32[2,2,4,16,512]{4,3,2,1,0:T(8,128)S(1)}, u32[]{:S(2)}, u32[]{:S(2)}) collective-permute-start(f32[2,2,4,16,512]{4,3,2,1,0:T(8,128)S(1)} %get-tuple-element.74), channel_id=1, source_target_pairs={{32,0},{64,32},{96,64},{0,96},{160,128},{192,160},{224,192},{128,2... | collective-permute-start | bytes 1572872 | tf_op jit(solution)/shard_map/ppermute | solution.py:26
  7.8 14.4 %copy-start.7 = (s32[128]{0:T(128)S(1)}, s32[128]{0:T(128)}, u32[]{:S(2)}) copy-start(s32[128]{0:T(128)} %constant.207.clone.group_ref.groups) | copy-start | bytes 1540
  7.8 14.4 %copy-start.9 = (s32[128]{0:T(128)S(1)}, s32[128]{0:T(128)}, u32[]{:S(2)}) copy-start(s32[128]{0:T(128)} %constant.206.clone.plane_ref.planes) | copy-start | bytes 1540
  18.7 10.5 %copy-start.10 = (f32[2,2,4,16,512]{4,3,2,1,0:T(8,128)}, f32[2,2,4,16,512]{4,3,2,1,0:T(8,128)S(1)}, u32[]{:S(2)}) copy-start(f32[2,2,4,16,512]{4,3,2,1,0:T(8,128)S(1)} %collective-permute-done) | copy-start | bytes 1572868
  18.7 10.5 %copy-start.12 = (f32[2,2,4,16,512]{4,3,2,1,0:T(8,128)}, f32[2,2,4,16,512]{4,3,2,1,0:T(8,128)S(1)}, u32[]{:S(2)}) copy-start(f32[2,2,4,16,512]{4,3,2,1,0:T(8,128)S(1)} %collective-permute-done.1) | copy-start | bytes 1572868
  19.6 6.7 %collective-permute-start.2 = (f32[2,4,16,512]{3,2,1,0:T(8,128)}, f32[2,4,16,512]{3,2,1,0:T(8,128)S(1)}, u32[]{:S(2)}, u32[]{:S(2)}) collective-permute-start(f32[2,4,16,512]{3,2,1,0:T(8,128)} %get-tuple-element.79), channel_id=1, source_target_pairs={{32,0},{64,32},{96,64},{0,96},{160,128},{192,160},{224,192},{128,2... | collective-permute-start | bytes 786440 | tf_op jit(solution)/shard_map/ppermute | solution.py:26
  22.2 7.0 %collective-permute-start.3 = (f32[2,4,16,512]{3,2,1,0:T(8,128)S(1)}, f32[2,4,16,512]{3,2,1,0:T(8,128)S(1)}, u32[]{:S(2)}, u32[]{:S(2)}) collective-permute-start(f32[2,4,16,512]{3,2,1,0:T(8,128)S(1)} %get-tuple-element.80), channel_id=1, source_target_pairs={{0,32},{32,64},{64,96},{96,0},{128,160},{160,192},{192,224},{224,1... | collective-permute-start | bytes 786440 | tf_op jit(solution)/shard_map/ppermute | solution.py:26
  29.2 0.7 copy-start.14
  29.9 16.1 %collective-permute-start.4 = (f32[2,2,6,16,512]{4,3,2,1,0:T(8,128)S(1)}, f32[2,2,6,16,512]{4,3,2,1,0:T(8,128)S(1)}, u32[]{:S(2)}, u32[]{:S(2)}) collective-permute-start(f32[2,2,6,16,512]{4,3,2,1,0:T(8,128)S(1)} %get-tuple-element.86), channel_id=1, source_target_pairs={{32,0},{64,32},{96,64},{0,96},{160,128},{192,160},{224,192},{128,2... | collective-permute-start | bytes 2359304 | tf_op jit(solution)/shard_map/ppermute | solution.py:26
  30.4 17.3 %collective-permute-start.5 = (f32[2,2,6,16,512]{4,3,2,1,0:T(8,128)S(1)}, f32[2,2,6,16,512]{4,3,2,1,0:T(8,128)S(1)}, u32[]{:S(2)}, u32[]{:S(2)}) collective-permute-start(f32[2,2,6,16,512]{4,3,2,1,0:T(8,128)S(1)} %get-tuple-element.87), channel_id=1, source_target_pairs={{0,32},{32,64},{64,96},{96,0},{128,160},{160,192},{192,224},{224,1... | collective-permute-start | bytes 2359304 | tf_op jit(solution)/shard_map/ppermute | solution.py:26
  31.3 17.4 %collective-permute-start.6 = (f32[2,4,16,512]{3,2,1,0:T(8,128)S(1)}, f32[2,4,16,512]{3,2,1,0:T(8,128)S(1)}, u32[]{:S(2)}, u32[]{:S(2)}) collective-permute-start(f32[2,4,16,512]{3,2,1,0:T(8,128)S(1)} %broadcast_select_fusion.2), channel_id=1, source_target_pairs={{0,128},{32,160},{64,192},{96,224},{128,0},{160,32},{192,64},{224,... | collective-permute-start | bytes 786440 | tf_op jit(solution)/shard_map/ppermute | solution.py:26
  48.8 0.7 copy-start.16
  49.5 6.8 %collective-permute-start.7 = (f32[2,6,16,512]{3,2,1,0:T(8,128)}, f32[2,6,16,512]{3,2,1,0:T(8,128)S(1)}, u32[]{:S(2)}, u32[]{:S(2)}) collective-permute-start(f32[2,6,16,512]{3,2,1,0:T(8,128)} %get-tuple-element.91), channel_id=1, source_target_pairs={{32,0},{64,32},{96,64},{0,96},{160,128},{192,160},{224,192},{128,2... | collective-permute-start | bytes 1179656 | tf_op jit(solution)/shard_map/ppermute | solution.py:26
  49.8 8.2 %collective-permute-start.8 = (f32[2,6,16,512]{3,2,1,0:T(8,128)}, f32[2,6,16,512]{3,2,1,0:T(8,128)}, u32[]{:S(2)}, u32[]{:S(2)}) collective-permute-start(f32[2,6,16,512]{3,2,1,0:T(8,128)} %get-tuple-element.92), channel_id=1, source_target_pairs={{0,32},{32,64},{64,96},{96,0},{128,160},{160,192},{192,224},{224,1... | collective-permute-start | bytes 1179656 | tf_op jit(solution)/shard_map/ppermute | solution.py:26
  51.0 10.9 %copy-start.11 = (f32[2,2,4,16,512]{4,3,2,1,0:T(8,128)S(1)}, f32[2,2,4,16,512]{4,3,2,1,0:T(8,128)}, u32[]{:S(2)}) copy-start(f32[2,2,4,16,512]{4,3,2,1,0:T(8,128)} %copy-done.10) | copy-start | bytes 1572868
  51.0 10.9 %copy-start.13 = (f32[2,2,4,16,512]{4,3,2,1,0:T(8,128)S(1)}, f32[2,2,4,16,512]{4,3,2,1,0:T(8,128)}, u32[]{:S(2)}) copy-start(f32[2,2,4,16,512]{4,3,2,1,0:T(8,128)} %copy-done.12) | copy-start | bytes 1572868
  51.0 10.9 %copy-start.15 = (f32[2,4,16,512]{3,2,1,0:T(8,128)S(1)}, f32[2,4,16,512]{3,2,1,0:T(8,128)}, u32[]{:S(2)}) copy-start(f32[2,4,16,512]{3,2,1,0:T(8,128)} %copy-done.14) | copy-start | bytes 786436
  51.0 10.9 %copy-start.17 = (f32[2,4,16,512]{3,2,1,0:T(8,128)S(1)}, f32[2,4,16,512]{3,2,1,0:T(8,128)}, u32[]{:S(2)}) copy-start(f32[2,4,16,512]{3,2,1,0:T(8,128)} %copy-done.16) | copy-start | bytes 786436
  55.0 13.4 %copy-start.1 = (f32[32,64,512]{2,1,0:T(8,128)S(1)}, f32[32,64,512]{2,1,0:T(8,128)}, u32[]{:S(2)}) copy-start(f32[32,64,512]{2,1,0:T(8,128)} %get-tuple-element.100.tile) | copy-start | bytes 12582916
  59.2 28.9 %collective-permute-start.9 = (f32[2,2,6,16,512]{4,3,2,1,0:T(8,128)S(1)}, f32[2,2,6,16,512]{4,3,2,1,0:T(8,128)S(1)}, u32[]{:S(2)}, u32[]{:S(2)}) collective-permute-start(f32[2,2,6,16,512]{4,3,2,1,0:T(8,128)S(1)} %get-tuple-element.98), channel_id=1, source_target_pairs={{0,32},{32,64},{64,96},{96,0},{128,160},{160,192},{192,224},{224,1... | collective-permute-start | bytes 2359304 | tf_op jit(solution)/shard_map/ppermute | solution.py:26
  59.4 28.7 %collective-permute-start.10 = (f32[2,2,6,16,512]{4,3,2,1,0:T(8,128)S(1)}, f32[2,2,6,16,512]{4,3,2,1,0:T(8,128)S(1)}, u32[]{:S(2)}, u32[]{:S(2)}) collective-permute-start(f32[2,2,6,16,512]{4,3,2,1,0:T(8,128)S(1)} %get-tuple-element.99), channel_id=1, source_target_pairs={{32,0},{64,32},{96,64},{0,96},{160,128},{192,160},{224,192},{128,2... | collective-permute-start | bytes 2359304 | tf_op jit(solution)/shard_map/ppermute | solution.py:26
  62.1 25.9 %collective-permute-start.13 = (f32[2,6,16,512]{3,2,1,0:T(8,128)S(1)}, f32[2,6,16,512]{3,2,1,0:T(8,128)S(1)}, u32[]{:S(2)}, u32[]{:S(2)}) collective-permute-start(f32[2,6,16,512]{3,2,1,0:T(8,128)S(1)} %broadcast_select_fusion.1), channel_id=1, source_target_pairs={{0,128},{32,160},{64,192},{96,224},{128,0},{160,32},{192,64},{224,... | collective-permute-start | bytes 1179656 | tf_op jit(solution)/shard_map/ppermute | solution.py:26
  68.5 6.0 %collective-permute-start.12 = (f32[32,2,512]{2,1,0:T(2,128)S(1)}, f32[32,2,512]{2,1,0:T(2,128)S(1)}, u32[]{:S(2)}, u32[]{:S(2)}) collective-permute-start(f32[32,2,512]{2,1,0:T(2,128)S(1)} %get-tuple-element.139), channel_id=1, source_target_pairs={{1,0},{2,1},{3,2},{5,4},{6,5},{7,6},{9,8},{10,9},{11,10},{13,12},{... | collective-permute-start | bytes 393224 | tf_op jit(solution)/shard_map/ppermute | solution.py:309
  69.8 5.9 %collective-permute-start.11 = (f32[32,2,512]{2,1,0:T(2,128)S(1)}, f32[32,2,512]{2,1,0:T(2,128)S(1)}, u32[]{:S(2)}, u32[]{:S(2)}) collective-permute-start(f32[32,2,512]{2,1,0:T(2,128)S(1)} %get-tuple-element.140), channel_id=1, source_target_pairs={{0,1},{1,2},{2,3},{4,5},{5,6},{6,7},{8,9},{9,10},{10,11},{12,13},{... | collective-permute-start | bytes 393224 | tf_op jit(solution)/shard_map/ppermute | solution.py:309
  76.2 17.0 %collective-permute-start.20 = (f32[2,80,512]{2,1,0:T(8,128)S(1)}, f32[2,80,512]{2,1,0:T(8,128)S(1)}, u32[]{:S(2)}, u32[]{:S(2)}) collective-permute-start(f32[2,80,512]{2,1,0:T(8,128)S(1)} %get-tuple-element.107), channel_id=1, source_target_pairs={{0,4},{4,8},{8,12},{12,16},{16,20},{20,24},{24,28},{1,5},{5,9},{9,... | collective-permute-start | bytes 983048 | tf_op jit(solution)/shard_map/ppermute | solution.py:309
  86.1 8.7 %collective-permute-start.21 = (f32[2,80,512]{2,1,0:T(8,128)S(1)}, f32[2,80,512]{2,1,0:T(8,128)S(1)}, u32[]{:S(2)}, u32[]{:S(2)}) collective-permute-start(f32[2,80,512]{2,1,0:T(8,128)S(1)} %get-tuple-element.108), channel_id=1, source_target_pairs={{4,0},{8,4},{12,8},{16,12},{20,16},{24,20},{28,24},{5,1},{9,5},{13... | collective-permute-start | bytes 983048 | tf_op jit(solution)/shard_map/ppermute | solution.py:309
  89.6 23.0 %collective-permute-start.18 = (f32[2,6,16,512]{3,2,1,0:T(8,128)S(1)}, f32[2,6,16,512]{3,2,1,0:T(8,128)S(1)}, u32[]{:S(2)}, u32[]{:S(2)}) collective-permute-start(f32[2,6,16,512]{3,2,1,0:T(8,128)S(1)} %get-tuple-element.141), channel_id=1, source_target_pairs={{0,32},{32,64},{64,96},{96,0},{128,160},{160,192},{192,224},{224,1... | collective-permute-start | bytes 1179656 | tf_op jit(solution)/shard_map/ppermute | solution.py:26
  89.7 22.9 %collective-permute-start.17 = (f32[2,6,16,512]{3,2,1,0:T(8,128)S(1)}, f32[2,6,16,512]{3,2,1,0:T(8,128)S(1)}, u32[]{:S(2)}, u32[]{:S(2)}) collective-permute-start(f32[2,6,16,512]{3,2,1,0:T(8,128)S(1)} %get-tuple-element.142), channel_id=1, source_target_pairs={{32,0},{64,32},{96,64},{0,96},{160,128},{192,160},{224,192},{128,2... | collective-permute-start | bytes 1179656 | tf_op jit(solution)/shard_map/ppermute | solution.py:26
  92.3 20.2 %collective-permute-start.19 = (f32[10,16,512]{2,1,0:T(8,128)S(1)}, f32[10,16,512]{2,1,0:T(8,128)S(1)}, u32[]{:S(2)}, u32[]{:S(2)}) collective-permute-start(f32[10,16,512]{2,1,0:T(8,128)S(1)} %pad_maximum_fusion.refs_0_), channel_id=1, source_target_pairs={{0,128},{32,160},{64,192},{96,224},{128,0},{160,32},{192,64},{224,... | collective-permute-start | bytes 983048 | tf_op jit(solution)/shard_map/ppermute | solution.py:26
  101.5 2.6 %copy-start.2 = (f32[36,80,512]{2,1,0:T(8,128)}, f32[36,80,512]{2,1,0:T(8,128)S(1)}, u32[]{:S(2)}) copy-start(f32[36,80,512]{2,1,0:T(8,128)S(1)} %get-tuple-element.134.refs_14_) | copy-start | bytes 17694724
  104.1 2.5 %copy-start.3 = (f32[36,80,512]{2,1,0:T(8,128)}, f32[36,80,512]{2,1,0:T(8,128)S(1)}, u32[]{:S(2)}) copy-start(f32[36,80,512]{2,1,0:T(8,128)S(1)} %get-tuple-element.135.refs_15_) | copy-start | bytes 17694724
  106.6 1.9 copy-start.4
  112.8 18.2 %collective-permute-start.27 = (f32[2,6,16,512]{3,2,1,0:T(8,128)S(1)}, f32[2,6,16,512]{3,2,1,0:T(8,128)S(1)}, u32[]{:S(2)}, u32[]{:S(2)}) collective-permute-start(f32[2,6,16,512]{3,2,1,0:T(8,128)S(1)} %broadcast_select_fusion), channel_id=1, source_target_pairs={{0,128},{32,160},{64,192},{96,224},{128,0},{160,32},{192,64},{224,... | collective-permute-start | bytes 1179656 | tf_op jit(solution)/shard_map/ppermute | solution.py:26
  113.7 9.6 %collective-permute-start.16 = (f32[10,16,512]{2,1,0:T(8,128)S(1)}, f32[10,16,512]{2,1,0:T(8,128)S(1)}, u32[]{:S(2)}, u32[]{:S(2)}) collective-permute-start(f32[10,16,512]{2,1,0:T(8,128)S(1)} %pad_maximum_fusion.refs_0_), channel_id=1, source_target_pairs={{0,64},{32,96},{64,0},{96,32},{128,192},{160,224},{192,128},{224,1... | collective-permute-start | bytes 983048 | tf_op jit(solution)/shard_map/ppermute | solution.py:26
  113.7 17.6 %collective-permute-start.15 = (f32[10,16,512]{2,1,0:T(8,128)S(1)}, f32[10,16,512]{2,1,0:T(8,128)S(1)}, u32[]{:S(2)}, u32[]{:S(2)}) collective-permute-start(f32[10,16,512]{2,1,0:T(8,128)S(1)} %pad_maximum_fusion.refs_0_), channel_id=1, source_target_pairs={{32,0},{64,32},{96,64},{0,96},{160,128},{192,160},{224,192},{128,2... | collective-permute-start | bytes 983048 | tf_op jit(solution)/shard_map/ppermute | solution.py:26
  114.6 21.1 %collective-permute-start.14 = (f32[10,16,512]{2,1,0:T(8,128)S(1)}, f32[10,16,512]{2,1,0:T(8,128)S(1)}, u32[]{:S(2)}, u32[]{:S(2)}) collective-permute-start(f32[10,16,512]{2,1,0:T(8,128)S(1)} %pad_maximum_fusion.refs_0_), channel_id=1, source_target_pairs={{0,32},{32,64},{64,96},{96,0},{128,160},{160,192},{192,224},{224,1... | collective-permute-start | bytes 983048 | tf_op jit(solution)/shard_map/ppermute | solution.py:26
  115.2 22.2 %collective-permute-start.24 = (f32[10,16,512]{2,1,0:T(8,128)S(1)}, f32[10,16,512]{2,1,0:T(8,128)S(1)}, u32[]{:S(2)}, u32[]{:S(2)}) collective-permute-start(f32[10,16,512]{2,1,0:T(8,128)S(1)} %collective-permute-done.19.refs_4_), channel_id=1, source_target_pairs={{0,64},{32,96},{64,0},{96,32},{128,192},{160,224},{192,128},{224,1... | collective-permute-start | bytes 983048 | tf_op jit(solution)/shard_map/ppermute | solution.py:26
  123.3 20.2 %collective-permute-start.23 = (f32[10,16,512]{2,1,0:T(8,128)S(1)}, f32[10,16,512]{2,1,0:T(8,128)S(1)}, u32[]{:S(2)}, u32[]{:S(2)}) collective-permute-start(f32[10,16,512]{2,1,0:T(8,128)S(1)} %collective-permute-done.19.refs_4_), channel_id=1, source_target_pairs={{32,0},{64,32},{96,64},{0,96},{160,128},{192,160},{224,192},{128,2... | collective-permute-start | bytes 983048 | tf_op jit(solution)/shard_map/ppermute | solution.py:26
  131.0 16.6 %collective-permute-start.22 = (f32[10,16,512]{2,1,0:T(8,128)S(1)}, f32[10,16,512]{2,1,0:T(8,128)S(1)}, u32[]{:S(2)}, u32[]{:S(2)}) collective-permute-start(f32[10,16,512]{2,1,0:T(8,128)S(1)} %collective-permute-done.19.refs_4_), channel_id=1, source_target_pairs={{0,32},{32,64},{64,96},{96,0},{128,160},{160,192},{192,224},{224,1... | collective-permute-start | bytes 983048 | tf_op jit(solution)/shard_map/ppermute | solution.py:26
  131.4 28.4 %collective-permute-start.31 = (f32[6,16,512]{2,1,0:T(8,128)S(1)}, f32[6,16,512]{2,1,0:T(8,128)S(1)}, u32[]{:S(2)}, u32[]{:S(2)}) collective-permute-start(f32[6,16,512]{2,1,0:T(8,128)S(1)} %fusion.11.refs_0_), channel_id=1, source_target_pairs={{0,128},{32,160},{64,192},{96,224},{128,0},{160,32},{192,64},{224,... | collective-permute-start | bytes 589832 | tf_op jit(solution)/shard_map/ppermute | solution.py:26
  135.7 27.3 %collective-permute-start.30 = (f32[6,16,512]{2,1,0:T(8,128)S(1)}, f32[6,16,512]{2,1,0:T(8,128)S(1)}, u32[]{:S(2)}, u32[]{:S(2)}) collective-permute-start(f32[6,16,512]{2,1,0:T(8,128)S(1)} %fusion.11.refs_0_), channel_id=1, source_target_pairs={{0,64},{32,96},{64,0},{96,32},{128,192},{160,224},{192,128},{224,1... | collective-permute-start | bytes 589832 | tf_op jit(solution)/shard_map/ppermute | solution.py:26
  147.5 2.2 %copy-start = (f32[32,64,512]{2,1,0:T(8,128)S(1)}, f32[32,64,512]{2,1,0:T(8,128)}, u32[]{:S(2)}) copy-start(f32[32,64,512]{2,1,0:T(8,128)} %get-tuple-element.113.refs_8_.refs_12_) | copy-start | bytes 12582916
  150.9 2.0 copy-start.5
  152.9 6.3 %collective-permute-start.25 = (f32[32,2,512]{2,1,0:T(2,128)S(1)}, f32[32,2,512]{2,1,0:T(2,128)S(1)}, u32[]{:S(2)}, u32[]{:S(2)}) collective-permute-start(f32[32,2,512]{2,1,0:T(2,128)S(1)} %get-tuple-element.114), channel_id=1, source_target_pairs={{0,1},{1,2},{2,3},{4,5},{5,6},{6,7},{8,9},{9,10},{10,11},{12,13},{... | collective-permute-start | bytes 393224 | tf_op jit(solution)/shard_map/ppermute | solution.py:309
  156.9 6.0 %collective-permute-start.26 = (f32[32,2,512]{2,1,0:T(2,128)S(1)}, f32[32,2,512]{2,1,0:T(2,128)S(1)}, u32[]{:S(2)}, u32[]{:S(2)}) collective-permute-start(f32[32,2,512]{2,1,0:T(2,128)S(1)} %get-tuple-element.115), channel_id=1, source_target_pairs={{1,0},{2,1},{3,2},{5,4},{6,5},{7,6},{9,8},{10,9},{11,10},{13,12},{... | collective-permute-start | bytes 393224 | tf_op jit(solution)/shard_map/ppermute | solution.py:309
  158.2 6.2 %collective-permute-start.29 = (f32[6,16,512]{2,1,0:T(8,128)S(1)}, f32[6,16,512]{2,1,0:T(8,128)S(1)}, u32[]{:S(2)}, u32[]{:S(2)}) collective-permute-start(f32[6,16,512]{2,1,0:T(8,128)S(1)} %fusion.11.refs_0_), channel_id=1, source_target_pairs={{32,0},{64,32},{96,64},{0,96},{160,128},{192,160},{224,192},{128,2... | collective-permute-start | bytes 589832 | tf_op jit(solution)/shard_map/ppermute | solution.py:26
  159.2 9.4 %collective-permute-start.28 = (f32[6,16,512]{2,1,0:T(8,128)S(1)}, f32[6,16,512]{2,1,0:T(8,128)S(1)}, u32[]{:S(2)}, u32[]{:S(2)}) collective-permute-start(f32[6,16,512]{2,1,0:T(8,128)S(1)} %fusion.11.refs_0_), channel_id=1, source_target_pairs={{0,32},{32,64},{64,96},{96,0},{128,160},{160,192},{192,224},{224,1... | collective-permute-start | bytes 589832 | tf_op jit(solution)/shard_map/ppermute | solution.py:26
  159.8 8.8 %collective-permute-start.34 = (f32[6,16,512]{2,1,0:T(8,128)S(1)}, f32[6,16,512]{2,1,0:T(8,128)S(1)}, u32[]{:S(2)}, u32[]{:S(2)}) collective-permute-start(f32[6,16,512]{2,1,0:T(8,128)S(1)} %collective-permute-done.31.refs_4_), channel_id=1, source_target_pairs={{0,64},{32,96},{64,0},{96,32},{128,192},{160,224},{192,128},{224,1... | collective-permute-start | bytes 589832 | tf_op jit(solution)/shard_map/ppermute | solution.py:26
  163.0 9.4 %collective-permute-start.33 = (f32[6,16,512]{2,1,0:T(8,128)S(1)}, f32[6,16,512]{2,1,0:T(8,128)S(1)}, u32[]{:S(2)}, u32[]{:S(2)}) collective-permute-start(f32[6,16,512]{2,1,0:T(8,128)S(1)} %collective-permute-done.31.refs_4_), channel_id=1, source_target_pairs={{32,0},{64,32},{96,64},{0,96},{160,128},{192,160},{224,192},{128,2... | collective-permute-start | bytes 589832 | tf_op jit(solution)/shard_map/ppermute | solution.py:26
  163.0 11.3 %collective-permute-start.32 = (f32[6,16,512]{2,1,0:T(8,128)S(1)}, f32[6,16,512]{2,1,0:T(8,128)S(1)}, u32[]{:S(2)}, u32[]{:S(2)}) collective-permute-start(f32[6,16,512]{2,1,0:T(8,128)S(1)} %collective-permute-done.31.refs_4_), channel_id=1, source_target_pairs={{0,32},{32,64},{64,96},{96,0},{128,160},{160,192},{192,224},{224,1... | collective-permute-start | bytes 589832 | tf_op jit(solution)/shard_map/ppermute | solution.py:26
  174.4 8.0 %collective-permute-start.35 = (f32[2,80,512]{2,1,0:T(8,128)S(1)}, f32[2,80,512]{2,1,0:T(8,128)S(1)}, u32[]{:S(2)}, u32[]{:S(2)}) collective-permute-start(f32[2,80,512]{2,1,0:T(8,128)S(1)} %get-tuple-element.131), channel_id=1, source_target_pairs={{0,4},{4,8},{8,12},{12,16},{16,20},{20,24},{24,28},{1,5},{5,9},{9,... | collective-permute-start | bytes 983048 | tf_op jit(solution)/shard_map/ppermute | solution.py:309
  178.4 8.4 %collective-permute-start.36 = (f32[2,80,512]{2,1,0:T(8,128)S(1)}, f32[2,80,512]{2,1,0:T(8,128)S(1)}, u32[]{:S(2)}, u32[]{:S(2)}) collective-permute-start(f32[2,80,512]{2,1,0:T(8,128)S(1)} %get-tuple-element.132), channel_id=1, source_target_pairs={{4,0},{8,4},{12,8},{16,12},{20,16},{24,20},{28,24},{5,1},{9,5},{13... | collective-permute-start | bytes 983048 | tf_op jit(solution)/shard_map/ppermute | solution.py:309

commit v4 on v3

--- a/solution.py
+++ b/solution.py
@@ -436,7 +436,6 @@
         name="frame",
     )(starts, planes, groups, *hold(*pieces, masked))
     before, after = halo(low, high, "line")
-    before, after, inner_rings = after_rest((before, after, inner_rings))
     low, high = pl.pallas_call(
         corner_kernel,
         out_shape=(held((RIM, tile_y + 2 * PAD, depth_cells)),) * 2,

time: 206 us -> 198 us (0.961)
  the two profiles are of different devices: /device:TPU:33 before, /device:TPU:2 now
where the time goes in v4:
time: 198 us
  starting transfers between devices  71.4 us (36%)
  waiting for transfers between devices  62.6 us (32%)
  Pallas kernels  35.7 us (18%)
  local copies, waits for them, and re-layouts  13.7 us (7%)
  other arithmetic  13.3 us (7%)
    ppermute x29, waiting for transfers between devices, send(): return lax.ppermute(x, 'source', pairs)  57.7 us
    ppermute x29, starting transfers between devices, send(): return lax.ppermute(x, 'source', pairs)  53.9 us
    pallas_call x1, Pallas kernels, shards(): pl.pallas_call(functools.partial(smooth_kernel, len(pieces), segments), o...  16.3 us
    unnamed x62, local copies, waits for them, and re-layouts  13.2 us
    pallas_call x3, Pallas kernels, partials(): pl.pallas_call(body, out_shape=[held((2, 2, count, ROWS, depth))] * (n //...  11 us
    ppermute x4, starting transfers between devices, halo(): lax.ppermute(high, axis, up)  9.11 us
    ppermute x4, starting transfers between devices, halo(): lax.ppermute(low, axis, [(j, i) for i, j in up])  8.38 us
    pallas_call x1, Pallas kernels, shards(): pl.pallas_call(coefficient_kernel, out_shape=(held(wide.shape),) * 2 + (h...  6.72 us
  transfers between devices with their start and end apart: 37, of which 13 were waited for; matrix products, arithmetic and copies ran while one was open for 6% of the time, Pallas kernels for 8%

profile of v4, /device:TPU:2, one launch (start us, length us, event | category | flops | bytes accessed | tf_op | source)
XLA Modules:
  0.0 197.7 jit_solution(1717676148216471135)
XLA Ops:
  0.1 0.7 copy-done.6
  0.7 0.7 copy-done.8
  1.4 3.1 %partials.3 = (f32[2,2,4,16,512]{4,3,2,1,0:T(8,128)S(1)}, f32[2,2,4,16,512]{4,3,2,1,0:T(8,128)S(1)}, f32[2,2,4,16,512]{4,3,2,1,0:T(8,128)S(1)}, f32[2,2,4,16,512]{4,3,2,1,0:T(8,128)S(1)}) custom-call(s32[8]{0:T(128)S(1)} %stack.185.start_ref, s32[128]{0:T(128)S(1)} %copy-done.6, s32[128]{0:T(128)S(1)} %copy-done.8, bf16[1,3,32,64,512]{4,3,2,1,0:T(8,128)(2,1)} %f_hbm.3, ...), custom_call_target="tpu_custom_call" | custom-call | tf_op jit(solution)/shard_map/partials/pallas_call | solution.py:109
  4.5 1.7 collective-permute-start
  6.2 1.7 collective-permute-start.1
  8.3 5.6 %fusion = (f32[32,64,512]{2,1,0:T(8,128)}, f32[32,64,512]{2,1,0:T(8,128)}) fusion(s32[32,64]{1,0:T(8,128)S(1)} %fusion.2, f32[32,64,512]{2,1,0:T(8,128)} %param.10, s32[32,64]{1,0:T(8,128)S(1)} %copy-done.28), kind=kLoop, calls=%fused_computation.3 | loop fusion | flops 7340032 | bytes 12599296 | tf_op jit(solution)/shard_map/jit(_where)/select_n | solution.py:378
  13.8 5.7 %collective-permute-done = f32[2,2,4,16,512]{4,3,2,1,0:T(8,128)S(1)} collective-permute-done((f32[2,2,4,16,512]{4,3,2,1,0:T(8,128)S(1)}, f32[2,2,4,16,512]{4,3,2,1,0:T(8,128)S(1)}, u32[]{:S(2)}, u32[]{:S(2)}) %collective-permute-start) | collective-permute-done | bytes 524320 | tf_op jit(solution)/shard_map/ppermute | solution.py:26
  19.5 0.9 add_bitcast_fusion.2
  20.5 1.6 collective-permute-start.2
  22.0 1.7 collective-permute-start.3
  23.8 3.9 %partials.4 = (f32[2,2,6,16,512]{4,3,2,1,0:T(8,128)S(1)}, f32[2,2,6,16,512]{4,3,2,1,0:T(8,128)S(1)}, f32[2,2,6,16,512]{4,3,2,1,0:T(8,128)S(1)}, f32[2,2,6,16,512]{4,3,2,1,0:T(8,128)S(1)}) custom-call(s32[8]{0:T(128)S(1)} %stack.194.start_ref, s32[128]{0:T(128)S(1)} %copy-done.7, s32[128]{0:T(128)S(1)} %copy-done.9, bf16[1,3,32,64,512]{4,3,2,1,0:T(8,128)(2,1)} %f_hbm.3, ...), custom_call_target="tpu_custom_call" | custom-call | tf_op jit(solution)/shard_map/partials/pallas_call | solution.py:109
  27.7 1.4 collective-permute-done.2
  29.3 0.5 copy-done.24
  29.8 0.4 collective-permute-start.5
  30.2 2.9 %collective-permute-start.4 = (f32[2,2,6,16,512]{4,3,2,1,0:T(8,128)S(1)}, f32[2,2,6,16,512]{4,3,2,1,0:T(8,128)S(1)}, u32[]{:S(2)}, u32[]{:S(2)}) collective-permute-start(f32[2,2,6,16,512]{4,3,2,1,0:T(8,128)S(1)} %get-tuple-element.76), channel_id=1, source_target_pairs={{32,0},{64,32},{96,64},{0,96},{160,128},{192,160},{224,192},{128,2... | collective-permute-start | bytes 2359304 | tf_op jit(solution)/shard_map/ppermute | solution.py:26
  33.1 7.2 %collective-permute-start.6 = (f32[2,4,16,512]{3,2,1,0:T(8,128)S(1)}, f32[2,4,16,512]{3,2,1,0:T(8,128)S(1)}, u32[]{:S(2)}, u32[]{:S(2)}) collective-permute-start(f32[2,4,16,512]{3,2,1,0:T(8,128)S(1)} %broadcast_select_fusion.2), channel_id=1, source_target_pairs={{0,128},{32,160},{64,192},{96,224},{128,0},{160,32},{192,64},{224,... | collective-permute-start | bytes 786440 | tf_op jit(solution)/shard_map/ppermute | solution.py:26
  40.2 8.3 %collective-permute-done.5 = f32[2,2,6,16,512]{4,3,2,1,0:T(8,128)S(1)} collective-permute-done((f32[2,2,6,16,512]{4,3,2,1,0:T(8,128)S(1)}, f32[2,2,6,16,512]{4,3,2,1,0:T(8,128)S(1)}, u32[]{:S(2)}, u32[]{:S(2)}) %collective-permute-start.5) | collective-permute-done | bytes 786464 | tf_op jit(solution)/shard_map/ppermute | solution.py:26
  48.6 1.1 fusion.7
  49.9 3.0 %collective-permute-start.8 = (f32[2,6,16,512]{3,2,1,0:T(8,128)}, f32[2,6,16,512]{3,2,1,0:T(8,128)}, u32[]{:S(2)}, u32[]{:S(2)}) collective-permute-start(f32[2,6,16,512]{3,2,1,0:T(8,128)} %get-tuple-element.86), channel_id=1, source_target_pairs={{32,0},{64,32},{96,64},{0,96},{160,128},{192,160},{224,192},{128,2... | collective-permute-start | bytes 1179656 | tf_op jit(solution)/shard_map/ppermute | solution.py:26
  53.1 4.0 %partials.5 = (f32[2,2,6,16,512]{4,3,2,1,0:T(8,128)S(1)}, f32[2,2,6,16,512]{4,3,2,1,0:T(8,128)S(1)}, f32[2,2,6,16,512]{4,3,2,1,0:T(8,128)S(1)}, f32[2,2,6,16,512]{4,3,2,1,0:T(8,128)S(1)}) custom-call(s32[8]{0:T(128)S(1)} %stack.176.start_ref, s32[128]{0:T(128)S(1)} %copy-done.7, s32[128]{0:T(128)S(1)} %copy-done.9, bf16[1,3,32,64,512]{4,3,2,1,0:T(8,128)(2,1)} %f_hbm.3, ...), custom_call_target="tpu_custom_call" | custom-call | tf_op jit(solution)/shard_map/partials/pallas_call | solution.py:109
  57.1 2.2 %collective-permute-done.7 = f32[2,6,16,512]{3,2,1,0:T(8,128)S(1)} collective-permute-done((f32[2,6,16,512]{3,2,1,0:T(8,128)}, f32[2,6,16,512]{3,2,1,0:T(8,128)S(1)}, u32[]{:S(2)}, u32[]{:S(2)}) %collective-permute-start.7) | collective-permute-done | bytes 393248 | tf_op jit(solution)/shard_map/ppermute | solution.py:26
  59.3 1.2 broadcast_select_fusion.1
  60.5 1.0 collective-permute-start.9
  61.6 2.3 %collective-permute-start.10 = (f32[2,2,6,16,512]{4,3,2,1,0:T(8,128)S(1)}, f32[2,2,6,16,512]{4,3,2,1,0:T(8,128)S(1)}, u32[]{:S(2)}, u32[]{:S(2)}) collective-permute-start(f32[2,2,6,16,512]{4,3,2,1,0:T(8,128)S(1)} %get-tuple-element.89), channel_id=1, source_target_pairs={{32,0},{64,32},{96,64},{0,96},{160,128},{192,160},{224,192},{128,2... | collective-permute-start | bytes 2359304 | tf_op jit(solution)/shard_map/ppermute | solution.py:26
  64.1 7.5 %collective-permute-start.13 = (f32[2,6,16,512]{3,2,1,0:T(8,128)S(1)}, f32[2,6,16,512]{3,2,1,0:T(8,128)S(1)}, u32[]{:S(2)}, u32[]{:S(2)}) collective-permute-start(f32[2,6,16,512]{3,2,1,0:T(8,128)S(1)} %broadcast_select_fusion.1), channel_id=1, source_target_pairs={{0,128},{32,160},{64,192},{96,224},{128,0},{160,32},{192,64},{224,... | collective-permute-start | bytes 1179656 | tf_op jit(solution)/shard_map/ppermute | solution.py:26
  71.7 3.4 %collective-permute-start.11 = (f32[32,2,512]{2,1,0:T(2,128)S(1)}, f32[32,2,512]{2,1,0:T(2,128)S(1)}, u32[]{:S(2)}, u32[]{:S(2)}) collective-permute-start(f32[32,2,512]{2,1,0:T(2,128)S(1)} %get-tuple-element.120), channel_id=1, source_target_pairs={{0,1},{1,2},{2,3},{4,5},{5,6},{6,7},{8,9},{9,10},{10,11},{12,13},{... | collective-permute-start | bytes 393224 | tf_op jit(solution)/shard_map/ppermute | solution.py:309
  75.1 2.4 %collective-permute-start.12 = (f32[32,2,512]{2,1,0:T(2,128)S(1)}, f32[32,2,512]{2,1,0:T(2,128)S(1)}, u32[]{:S(2)}, u32[]{:S(2)}) collective-permute-start(f32[32,2,512]{2,1,0:T(2,128)S(1)} %get-tuple-element.119), channel_id=1, source_target_pairs={{1,0},{2,1},{3,2},{5,4},{6,5},{7,6},{9,8},{10,9},{11,10},{13,12},{... | collective-permute-start | bytes 393224 | tf_op jit(solution)/shard_map/ppermute | solution.py:309
  77.5 1.0 collective-permute-done.11.before
  78.5 3.4 %collective-permute-done.12.after = f32[32,2,512]{2,1,0:T(2,128)S(1)} collective-permute-done((f32[32,2,512]{2,1,0:T(2,128)S(1)}, f32[32,2,512]{2,1,0:T(2,128)S(1)}, u32[]{:S(2)}, u32[]{:S(2)}) %collective-permute-start.12) | collective-permute-done | bytes 131104 | tf_op jit(solution)/shard_map/ppermute | solution.py:309
  81.9 0.5 rims.1
  82.4 1.3 collective-permute-start.17
  83.7 1.3 collective-permute-start.18
  85.3 1.9 collective-permute-start.14
  87.4 1.3 select_add_fusion.1
  88.7 5.6 %collective-permute-start.16 = (f32[10,16,512]{2,1,0:T(8,128)S(1)}, f32[10,16,512]{2,1,0:T(8,128)S(1)}, u32[]{:S(2)}, u32[]{:S(2)}) collective-permute-start(f32[10,16,512]{2,1,0:T(8,128)S(1)} %pad_maximum_fusion.refs_0_), channel_id=1, source_target_pairs={{0,128},{32,160},{64,192},{96,224},{128,0},{160,32},{192,64},{224,... | collective-permute-start | bytes 983048 | tf_op jit(solution)/shard_map/ppermute | solution.py:26
  94.4 6.7 %coefficients.1 = (f32[36,80,512]{2,1,0:T(8,128)S(1)}, f32[36,80,512]{2,1,0:T(8,128)S(1)}, f32[32,64,512]{2,1,0:T(8,128)S(1)}) custom-call(f32[36,80,512]{2,1,0:T(8,128)S(1)} %get-tuple-element.91.wide, f32[2,80,512]{2,1,0:T(8,128)S(1)} %collective-permute-done.17.low, f32[2,80,512]{2,1,0:T(8,128)S(1)} %collective-permute-done.18.high), custom_call_target="tpu_custom_call" | custom-call | tf_op jit(solution)/shard_map/coefficients/pallas_call | solution.py:401
  101.1 2.6 %copy-done.2 = f32[36,80,512]{2,1,0:T(8,128)} copy-done((f32[36,80,512]{2,1,0:T(8,128)}, f32[36,80,512]{2,1,0:T(8,128)S(1)}, u32[]{:S(2)}) %copy-start.2) | copy-done | bytes 5898264
  103.7 2.5 %copy-done.3 = f32[36,80,512]{2,1,0:T(8,128)} copy-done((f32[36,80,512]{2,1,0:T(8,128)}, f32[36,80,512]{2,1,0:T(8,128)S(1)}, u32[]{:S(2)}) %copy-start.3) | copy-done | bytes 5898264
  106.2 2.0 copy-done.4
  108.2 3.2 %collective-permute-start.28 = (f32[10,16,512]{2,1,0:T(8,128)S(1)}, f32[10,16,512]{2,1,0:T(8,128)S(1)}, u32[]{:S(2)}, u32[]{:S(2)}) collective-permute-start(f32[10,16,512]{2,1,0:T(8,128)S(1)} %pad_maximum_fusion.refs_0_), channel_id=1, source_target_pairs={{32,0},{64,32},{96,64},{0,96},{160,128},{192,160},{224,192},{128,2... | collective-permute-start | bytes 983048 | tf_op jit(solution)/shard_map/ppermute | solution.py:26
  111.5 1.0 broadcast_select_fusion
  112.5 0.4 collective-permute-start.19
  112.9 1.3 collective-permute-start.29
  114.1 1.4 collective-permute-start.30
  115.6 11.4 %collective-permute-done.27.refs_1_ = f32[10,16,512]{2,1,0:T(8,128)S(1)} collective-permute-done((f32[10,16,512]{2,1,0:T(8,128)S(1)}, f32[10,16,512]{2,1,0:T(8,128)S(1)}, u32[]{:S(2)}, u32[]{:S(2)}) %collective-permute-start.27) | collective-permute-done | bytes 327712 | tf_op jit(solution)/shard_map/ppermute | solution.py:26
  127.2 13.2 %collective-permute-done.30.refs_5_ = f32[10,16,512]{2,1,0:T(8,128)S(1)} collective-permute-done((f32[10,16,512]{2,1,0:T(8,128)S(1)}, f32[10,16,512]{2,1,0:T(8,128)S(1)}, u32[]{:S(2)}, u32[]{:S(2)}) %collective-permute-start.30) | collective-permute-done | bytes 327712 | tf_op jit(solution)/shard_map/ppermute | solution.py:26
  140.4 2.2 %copy-done = f32[32,64,512]{2,1,0:T(8,128)S(1)} copy-done((f32[32,64,512]{2,1,0:T(8,128)S(1)}, f32[32,64,512]{2,1,0:T(8,128)}, u32[]{:S(2)}) %copy-start) | copy-done | bytes 4194328
  142.6 1.1 frame.1
  143.8 2.0 %copy-done.5 = f32[32,64,512]{2,1,0:T(8,128)} copy-done((f32[32,64,512]{2,1,0:T(8,128)}, f32[32,64,512]{2,1,0:T(8,128)S(1)}, u32[]{:S(2)}) %copy-start.5) | copy-done | bytes 4194328
  145.8 3.1 %collective-permute-start.33 = (f32[32,2,512]{2,1,0:T(2,128)S(1)}, f32[32,2,512]{2,1,0:T(2,128)S(1)}, u32[]{:S(2)}, u32[]{:S(2)}) collective-permute-start(f32[32,2,512]{2,1,0:T(2,128)S(1)} %get-tuple-element.109), channel_id=1, source_target_pairs={{0,1},{1,2},{2,3},{4,5},{5,6},{6,7},{8,9},{9,10},{10,11},{12,13},{... | collective-permute-start | bytes 393224 | tf_op jit(solution)/shard_map/ppermute | solution.py:309
  148.9 1.3 select_add_fusion
  150.3 2.5 %collective-permute-start.20 = (f32[6,16,512]{2,1,0:T(8,128)S(1)}, f32[6,16,512]{2,1,0:T(8,128)S(1)}, u32[]{:S(2)}, u32[]{:S(2)}) collective-permute-start(f32[6,16,512]{2,1,0:T(8,128)S(1)} %fusion.11.refs_0_), channel_id=1, source_target_pairs={{0,32},{32,64},{64,96},{96,0},{128,160},{160,192},{192,224},{224,1... | collective-permute-start | bytes 589832 | tf_op jit(solution)/shard_map/ppermute | solution.py:26
  152.8 3.3 %collective-permute-start.34 = (f32[32,2,512]{2,1,0:T(2,128)S(1)}, f32[32,2,512]{2,1,0:T(2,128)S(1)}, u32[]{:S(2)}, u32[]{:S(2)}) collective-permute-start(f32[32,2,512]{2,1,0:T(2,128)S(1)} %get-tuple-element.110), channel_id=1, source_target_pairs={{1,0},{2,1},{3,2},{5,4},{6,5},{7,6},{9,8},{10,9},{11,10},{13,12},{... | collective-permute-start | bytes 393224 | tf_op jit(solution)/shard_map/ppermute | solution.py:309
  156.2 0.5 collective-permute-start.23
  156.7 2.5 %collective-permute-start.21 = (f32[6,16,512]{2,1,0:T(8,128)S(1)}, f32[6,16,512]{2,1,0:T(8,128)S(1)}, u32[]{:S(2)}, u32[]{:S(2)}) collective-permute-start(f32[6,16,512]{2,1,0:T(8,128)S(1)} %fusion.11.refs_0_), channel_id=1, source_target_pairs={{32,0},{64,32},{96,64},{0,96},{160,128},{192,160},{224,192},{128,2... | collective-permute-start | bytes 589832 | tf_op jit(solution)/shard_map/ppermute | solution.py:26
  159.2 0.5 collective-permute-done.34.after.refs_11_
  159.7 1.3 collective-permute-start.35
  161.0 1.3 collective-permute-start.36
  162.3 8.4 %collective-permute-done.23.refs_4_ = f32[6,16,512]{2,1,0:T(8,128)S(1)} collective-permute-done((f32[6,16,512]{2,1,0:T(8,128)S(1)}, f32[6,16,512]{2,1,0:T(8,128)S(1)}, u32[]{:S(2)}, u32[]{:S(2)}) %collective-permute-start.23) | collective-permute-done | bytes 196640 | tf_op jit(solution)/shard_map/ppermute | solution.py:26
  170.8 3.2 %collective-permute-start.25 = (f32[6,16,512]{2,1,0:T(8,128)S(1)}, f32[6,16,512]{2,1,0:T(8,128)S(1)}, u32[]{:S(2)}, u32[]{:S(2)}) collective-permute-start(f32[6,16,512]{2,1,0:T(8,128)S(1)} %collective-permute-done.23.refs_4_), channel_id=1, source_target_pairs={{32,0},{64,32},{96,64},{0,96},{160,128},{192,160},{224,192},{128,2... | collective-permute-start | bytes 589832 | tf_op jit(solution)/shard_map/ppermute | solution.py:26
  174.1 4.8 %collective-permute-done.24.refs_5_ = f32[6,16,512]{2,1,0:T(8,128)S(1)} collective-permute-done((f32[6,16,512]{2,1,0:T(8,128)S(1)}, f32[6,16,512]{2,1,0:T(8,128)S(1)}, u32[]{:S(2)}, u32[]{:S(2)}) %collective-permute-start.24) | collective-permute-done | bytes 196640 | tf_op jit(solution)/shard_map/ppermute | solution.py:26
  178.9 0.8 collective-permute-done.25.refs_6_
  179.7 1.5 collective-permute-done.26.refs_7_
  181.2 16.3 %smooth.1 = f32[32,64,512]{2,1,0:T(8,128)} custom-call(s32[8]{0:T(128)S(1)} %stack.167.starts, s32[128]{0:T(128)S(1)} %copy-done.7, s32[128]{0:T(128)S(1)} %copy-done.9, f32[6,16,512]{2,1,0:T(8,128)S(1)} %fusion.11.refs_0_, f32[6,16,512]{2,1,0:T(8,128)S(1)} %collective-permute-done.20.refs_1_, f32[6,16,512]{2,1,0:T(8,128)S(1)} %collective-permute-done.21.refs_2_, ...), custom_call_target="tpu_custom_call" | custom-call | tf_op jit(solution)/shard_map/smooth/pallas_call | solution.py:454
  (104 shorter events, 2.3 us)
Async XLA Ops:
  1.4 6.4 %copy-start.29 = (s32[256]{0:T(256)S(1)}, s32[256]{0:T(256)}, u32[]{:S(2)}) copy-start(s32[256]{0:T(256)} %param.13) | copy-start | bytes 3076
  1.4 6.4 %copy-start.30 = (s32[8]{0:T(128)S(1)}, s32[8]{0:T(128)}, u32[]{:S(2)}) copy-start(s32[8]{0:T(128)} %param.12) | copy-start | bytes 100
  1.4 6.5 %copy-start.28 = (s32[32,64]{1,0:T(8,128)S(1)}, s32[32,64]{1,0:T(8,128)}, u32[]{:S(2)}) copy-start(s32[32,64]{1,0:T(8,128)} %param.11) | copy-start | bytes 24580
  4.5 15.0 %collective-permute-start = (f32[2,2,4,16,512]{4,3,2,1,0:T(8,128)S(1)}, f32[2,2,4,16,512]{4,3,2,1,0:T(8,128)S(1)}, u32[]{:S(2)}, u32[]{:S(2)}) collective-permute-start(f32[2,2,4,16,512]{4,3,2,1,0:T(8,128)S(1)} %get-tuple-element.63), channel_id=1, source_target_pairs={{0,32},{32,64},{64,96},{96,0},{128,160},{160,192},{192,224},{224,1... | collective-permute-start | bytes 1572872 | tf_op jit(solution)/shard_map/ppermute | solution.py:26
  6.2 13.4 %collective-permute-start.1 = (f32[2,2,4,16,512]{4,3,2,1,0:T(8,128)S(1)}, f32[2,2,4,16,512]{4,3,2,1,0:T(8,128)S(1)}, u32[]{:S(2)}, u32[]{:S(2)}) collective-permute-start(f32[2,2,4,16,512]{4,3,2,1,0:T(8,128)S(1)} %get-tuple-element.64), channel_id=1, source_target_pairs={{32,0},{64,32},{96,64},{0,96},{160,128},{192,160},{224,192},{128,2... | collective-permute-start | bytes 1572872 | tf_op jit(solution)/shard_map/ppermute | solution.py:26
  8.2 15.6 %copy-start.7 = (s32[128]{0:T(128)S(1)}, s32[128]{0:T(128)}, u32[]{:S(2)}) copy-start(s32[128]{0:T(128)} %constant.206.clone.plane_ref.planes) | copy-start | bytes 1540
  8.2 15.6 %copy-start.9 = (s32[128]{0:T(128)S(1)}, s32[128]{0:T(128)}, u32[]{:S(2)}) copy-start(s32[128]{0:T(128)} %constant.207.clone.group_ref.groups) | copy-start | bytes 1540
  19.5 9.6 %copy-start.20 = (f32[2,2,4,16,512]{4,3,2,1,0:T(8,128)}, f32[2,2,4,16,512]{4,3,2,1,0:T(8,128)S(1)}, u32[]{:S(2)}) copy-start(f32[2,2,4,16,512]{4,3,2,1,0:T(8,128)S(1)} %collective-permute-done) | copy-start | bytes 1572868
  19.5 9.6 %copy-start.22 = (f32[2,2,4,16,512]{4,3,2,1,0:T(8,128)}, f32[2,2,4,16,512]{4,3,2,1,0:T(8,128)S(1)}, u32[]{:S(2)}) copy-start(f32[2,2,4,16,512]{4,3,2,1,0:T(8,128)S(1)} %collective-permute-done.1) | copy-start | bytes 1572868
  20.5 8.6 %collective-permute-start.2 = (f32[2,4,16,512]{3,2,1,0:T(8,128)}, f32[2,4,16,512]{3,2,1,0:T(8,128)S(1)}, u32[]{:S(2)}, u32[]{:S(2)}) collective-permute-start(f32[2,4,16,512]{3,2,1,0:T(8,128)} %get-tuple-element.74), channel_id=1, source_target_pairs={{0,32},{32,64},{64,96},{96,0},{128,160},{160,192},{192,224},{224,1... | collective-permute-start | bytes 786440 | tf_op jit(solution)/shard_map/ppermute | solution.py:26
  22.0 7.1 %collective-permute-start.3 = (f32[2,4,16,512]{3,2,1,0:T(8,128)S(1)}, f32[2,4,16,512]{3,2,1,0:T(8,128)S(1)}, u32[]{:S(2)}, u32[]{:S(2)}) collective-permute-start(f32[2,4,16,512]{3,2,1,0:T(8,128)S(1)} %get-tuple-element.75), channel_id=1, source_target_pairs={{32,0},{64,32},{96,64},{0,96},{160,128},{192,160},{224,192},{128,2... | collective-permute-start | bytes 786440 | tf_op jit(solution)/shard_map/ppermute | solution.py:26
  29.1 23.8 %copy-start.26 = (f32[2,4,16,512]{3,2,1,0:T(8,128)}, f32[2,4,16,512]{3,2,1,0:T(8,128)S(1)}, u32[]{:S(2)}) copy-start(f32[2,4,16,512]{3,2,1,0:T(8,128)S(1)} %collective-permute-done.3) | copy-start | bytes 786436
  29.8 18.7 %collective-permute-start.5 = (f32[2,2,6,16,512]{4,3,2,1,0:T(8,128)S(1)}, f32[2,2,6,16,512]{4,3,2,1,0:T(8,128)S(1)}, u32[]{:S(2)}, u32[]{:S(2)}) collective-permute-start(f32[2,2,6,16,512]{4,3,2,1,0:T(8,128)S(1)} %get-tuple-element.77), channel_id=1, source_target_pairs={{0,32},{32,64},{64,96},{96,0},{128,160},{160,192},{192,224},{224,1... | collective-permute-start | bytes 2359304 | tf_op jit(solution)/shard_map/ppermute | solution.py:26
  30.2 18.4 %collective-permute-start.4 = (f32[2,2,6,16,512]{4,3,2,1,0:T(8,128)S(1)}, f32[2,2,6,16,512]{4,3,2,1,0:T(8,128)S(1)}, u32[]{:S(2)}, u32[]{:S(2)}) collective-permute-start(f32[2,2,6,16,512]{4,3,2,1,0:T(8,128)S(1)} %get-tuple-element.76), channel_id=1, source_target_pairs={{32,0},{64,32},{96,64},{0,96},{160,128},{192,160},{224,192},{128,2... | collective-permute-start | bytes 2359304 | tf_op jit(solution)/shard_map/ppermute | solution.py:26
  33.1 16.6 %collective-permute-start.6 = (f32[2,4,16,512]{3,2,1,0:T(8,128)S(1)}, f32[2,4,16,512]{3,2,1,0:T(8,128)S(1)}, u32[]{:S(2)}, u32[]{:S(2)}) collective-permute-start(f32[2,4,16,512]{3,2,1,0:T(8,128)S(1)} %broadcast_select_fusion.2), channel_id=1, source_target_pairs={{0,128},{32,160},{64,192},{96,224},{128,0},{160,32},{192,64},{224,... | collective-permute-start | bytes 786440 | tf_op jit(solution)/shard_map/ppermute | solution.py:26
  49.7 9.6 %collective-permute-start.7 = (f32[2,6,16,512]{3,2,1,0:T(8,128)}, f32[2,6,16,512]{3,2,1,0:T(8,128)S(1)}, u32[]{:S(2)}, u32[]{:S(2)}) collective-permute-start(f32[2,6,16,512]{3,2,1,0:T(8,128)} %get-tuple-element.85), channel_id=1, source_target_pairs={{0,32},{32,64},{64,96},{96,0},{128,160},{160,192},{192,224},{224,1... | collective-permute-start | bytes 1179656 | tf_op jit(solution)/shard_map/ppermute | solution.py:26
  49.9 9.4 %collective-permute-start.8 = (f32[2,6,16,512]{3,2,1,0:T(8,128)}, f32[2,6,16,512]{3,2,1,0:T(8,128)}, u32[]{:S(2)}, u32[]{:S(2)}) collective-permute-start(f32[2,6,16,512]{3,2,1,0:T(8,128)} %get-tuple-element.86), channel_id=1, source_target_pairs={{32,0},{64,32},{96,64},{0,96},{160,128},{192,160},{224,192},{128,2... | collective-permute-start | bytes 1179656 | tf_op jit(solution)/shard_map/ppermute | solution.py:26
  53.0 6.3 %copy-start.15 = (f32[2,2,6,16,512]{4,3,2,1,0:T(8,128)S(1)}, f32[2,2,6,16,512]{4,3,2,1,0:T(8,128)}, u32[]{:S(2)}) copy-start(f32[2,2,6,16,512]{4,3,2,1,0:T(8,128)} %copy-done.14) | copy-start | bytes 2359300
  53.0 10.8 %copy-start.21 = (f32[2,2,4,16,512]{4,3,2,1,0:T(8,128)S(1)}, f32[2,2,4,16,512]{4,3,2,1,0:T(8,128)}, u32[]{:S(2)}) copy-start(f32[2,2,4,16,512]{4,3,2,1,0:T(8,128)} %copy-done.20) | copy-start | bytes 1572868
  53.0 10.8 %copy-start.23 = (f32[2,2,4,16,512]{4,3,2,1,0:T(8,128)S(1)}, f32[2,2,4,16,512]{4,3,2,1,0:T(8,128)}, u32[]{:S(2)}) copy-start(f32[2,2,4,16,512]{4,3,2,1,0:T(8,128)} %copy-done.22) | copy-start | bytes 1572868
  53.0 10.8 %copy-start.25 = (f32[2,4,16,512]{3,2,1,0:T(8,128)S(1)}, f32[2,4,16,512]{3,2,1,0:T(8,128)}, u32[]{:S(2)}) copy-start(f32[2,4,16,512]{3,2,1,0:T(8,128)} %copy-done.24) | copy-start | bytes 786436
  53.1 10.8 %copy-start.27 = (f32[2,4,16,512]{3,2,1,0:T(8,128)S(1)}, f32[2,4,16,512]{3,2,1,0:T(8,128)}, u32[]{:S(2)}) copy-start(f32[2,4,16,512]{3,2,1,0:T(8,128)} %copy-done.26) | copy-start | bytes 786436
  57.1 14.5 %copy-start.1 = (f32[32,64,512]{2,1,0:T(8,128)S(1)}, f32[32,64,512]{2,1,0:T(8,128)}, u32[]{:S(2)}) copy-start(f32[32,64,512]{2,1,0:T(8,128)} %get-tuple-element.90.tile) | copy-start | bytes 12582916
  60.5 24.5 %collective-permute-start.9 = (f32[2,2,6,16,512]{4,3,2,1,0:T(8,128)S(1)}, f32[2,2,6,16,512]{4,3,2,1,0:T(8,128)S(1)}, u32[]{:S(2)}, u32[]{:S(2)}) collective-permute-start(f32[2,2,6,16,512]{4,3,2,1,0:T(8,128)S(1)} %get-tuple-element.88), channel_id=1, source_target_pairs={{0,32},{32,64},{64,96},{96,0},{128,160},{160,192},{192,224},{224,1... | collective-permute-start | bytes 2359304 | tf_op jit(solution)/shard_map/ppermute | solution.py:26
  61.6 23.5 %collective-permute-start.10 = (f32[2,2,6,16,512]{4,3,2,1,0:T(8,128)S(1)}, f32[2,2,6,16,512]{4,3,2,1,0:T(8,128)S(1)}, u32[]{:S(2)}, u32[]{:S(2)}) collective-permute-start(f32[2,2,6,16,512]{4,3,2,1,0:T(8,128)S(1)} %get-tuple-element.89), channel_id=1, source_target_pairs={{32,0},{64,32},{96,64},{0,96},{160,128},{192,160},{224,192},{128,2... | collective-permute-start | bytes 2359304 | tf_op jit(solution)/shard_map/ppermute | solution.py:26
  64.1 21.0 %collective-permute-start.13 = (f32[2,6,16,512]{3,2,1,0:T(8,128)S(1)}, f32[2,6,16,512]{3,2,1,0:T(8,128)S(1)}, u32[]{:S(2)}, u32[]{:S(2)}) collective-permute-start(f32[2,6,16,512]{3,2,1,0:T(8,128)S(1)} %broadcast_select_fusion.1), channel_id=1, source_target_pairs={{0,128},{32,160},{64,192},{96,224},{128,0},{160,32},{192,64},{224,... | collective-permute-start | bytes 1179656 | tf_op jit(solution)/shard_map/ppermute | solution.py:26
  71.7 6.9 %collective-permute-start.11 = (f32[32,2,512]{2,1,0:T(2,128)S(1)}, f32[32,2,512]{2,1,0:T(2,128)S(1)}, u32[]{:S(2)}, u32[]{:S(2)}) collective-permute-start(f32[32,2,512]{2,1,0:T(2,128)S(1)} %get-tuple-element.120), channel_id=1, source_target_pairs={{0,1},{1,2},{2,3},{4,5},{5,6},{6,7},{8,9},{9,10},{10,11},{12,13},{... | collective-permute-start | bytes 393224 | tf_op jit(solution)/shard_map/ppermute | solution.py:309
  75.1 6.9 %collective-permute-start.12 = (f32[32,2,512]{2,1,0:T(2,128)S(1)}, f32[32,2,512]{2,1,0:T(2,128)S(1)}, u32[]{:S(2)}, u32[]{:S(2)}) collective-permute-start(f32[32,2,512]{2,1,0:T(2,128)S(1)} %get-tuple-element.119), channel_id=1, source_target_pairs={{1,0},{2,1},{3,2},{5,4},{6,5},{7,6},{9,8},{10,9},{11,10},{13,12},{... | collective-permute-start | bytes 393224 | tf_op jit(solution)/shard_map/ppermute | solution.py:309
  82.4 11.9 %collective-permute-start.17 = (f32[2,80,512]{2,1,0:T(8,128)S(1)}, f32[2,80,512]{2,1,0:T(8,128)S(1)}, u32[]{:S(2)}, u32[]{:S(2)}) collective-permute-start(f32[2,80,512]{2,1,0:T(8,128)S(1)} %get-tuple-element.98), channel_id=1, source_target_pairs={{0,4},{4,8},{8,12},{12,16},{16,20},{20,24},{24,28},{1,5},{5,9},{9,... | collective-permute-start | bytes 983048 | tf_op jit(solution)/shard_map/ppermute | solution.py:309
  83.7 10.6 %collective-permute-start.18 = (f32[2,80,512]{2,1,0:T(8,128)S(1)}, f32[2,80,512]{2,1,0:T(8,128)S(1)}, u32[]{:S(2)}, u32[]{:S(2)}) collective-permute-start(f32[2,80,512]{2,1,0:T(8,128)S(1)} %get-tuple-element.99), channel_id=1, source_target_pairs={{4,0},{8,4},{12,8},{16,12},{20,16},{24,20},{28,24},{5,1},{9,5},{13... | collective-permute-start | bytes 983048 | tf_op jit(solution)/shard_map/ppermute | solution.py:309
  85.1 26.4 %copy-start.10 = (f32[2,2,6,16,512]{4,3,2,1,0:T(8,128)}, f32[2,2,6,16,512]{4,3,2,1,0:T(8,128)S(1)}, u32[]{:S(2)}) copy-start(f32[2,2,6,16,512]{4,3,2,1,0:T(8,128)S(1)} %collective-permute-done.9) | copy-start | bytes 2359300
  85.1 26.4 %copy-start.12 = (f32[2,2,6,16,512]{4,3,2,1,0:T(8,128)}, f32[2,2,6,16,512]{4,3,2,1,0:T(8,128)S(1)}, u32[]{:S(2)}) copy-start(f32[2,2,6,16,512]{4,3,2,1,0:T(8,128)S(1)} %collective-permute-done.10) | copy-start | bytes 2359300
  85.3 26.1 %collective-permute-start.14 = (f32[2,6,16,512]{3,2,1,0:T(8,128)S(1)}, f32[2,6,16,512]{3,2,1,0:T(8,128)S(1)}, u32[]{:S(2)}, u32[]{:S(2)}) collective-permute-start(f32[2,6,16,512]{3,2,1,0:T(8,128)S(1)} %get-tuple-element.122), channel_id=1, source_target_pairs={{32,0},{64,32},{96,64},{0,96},{160,128},{192,160},{224,192},{128,2... | collective-permute-start | bytes 1179656 | tf_op jit(solution)/shard_map/ppermute | solution.py:26
  87.2 24.2 %collective-permute-start.15 = (f32[2,6,16,512]{3,2,1,0:T(8,128)S(1)}, f32[2,6,16,512]{3,2,1,0:T(8,128)S(1)}, u32[]{:S(2)}, u32[]{:S(2)}) collective-permute-start(f32[2,6,16,512]{3,2,1,0:T(8,128)S(1)} %get-tuple-element.121), channel_id=1, source_target_pairs={{0,32},{32,64},{64,96},{96,0},{128,160},{160,192},{192,224},{224,1... | collective-permute-start | bytes 1179656 | tf_op jit(solution)/shard_map/ppermute | solution.py:26
  88.7 22.7 %collective-permute-start.16 = (f32[10,16,512]{2,1,0:T(8,128)S(1)}, f32[10,16,512]{2,1,0:T(8,128)S(1)}, u32[]{:S(2)}, u32[]{:S(2)}) collective-permute-start(f32[10,16,512]{2,1,0:T(8,128)S(1)} %pad_maximum_fusion.refs_0_), channel_id=1, source_target_pairs={{0,128},{32,160},{64,192},{96,224},{128,0},{160,32},{192,64},{224,... | collective-permute-start | bytes 983048 | tf_op jit(solution)/shard_map/ppermute | solution.py:26
  101.1 2.6 %copy-start.2 = (f32[36,80,512]{2,1,0:T(8,128)}, f32[36,80,512]{2,1,0:T(8,128)S(1)}, u32[]{:S(2)}) copy-start(f32[36,80,512]{2,1,0:T(8,128)S(1)} %get-tuple-element.114.refs_14_) | copy-start | bytes 17694724
  103.7 2.5 %copy-start.3 = (f32[36,80,512]{2,1,0:T(8,128)}, f32[36,80,512]{2,1,0:T(8,128)S(1)}, u32[]{:S(2)}) copy-start(f32[36,80,512]{2,1,0:T(8,128)S(1)} %get-tuple-element.115.refs_15_) | copy-start | bytes 17694724
  106.2 2.0 copy-start.4
  108.2 18.8 %collective-permute-start.27 = (f32[10,16,512]{2,1,0:T(8,128)S(1)}, f32[10,16,512]{2,1,0:T(8,128)S(1)}, u32[]{:S(2)}, u32[]{:S(2)}) collective-permute-start(f32[10,16,512]{2,1,0:T(8,128)S(1)} %pad_maximum_fusion.refs_0_), channel_id=1, source_target_pairs={{0,32},{32,64},{64,96},{96,0},{128,160},{160,192},{192,224},{224,1... | collective-permute-start | bytes 983048 | tf_op jit(solution)/shard_map/ppermute | solution.py:26
  108.2 18.8 %collective-permute-start.28 = (f32[10,16,512]{2,1,0:T(8,128)S(1)}, f32[10,16,512]{2,1,0:T(8,128)S(1)}, u32[]{:S(2)}, u32[]{:S(2)}) collective-permute-start(f32[10,16,512]{2,1,0:T(8,128)S(1)} %pad_maximum_fusion.refs_0_), channel_id=1, source_target_pairs={{32,0},{64,32},{96,64},{0,96},{160,128},{192,160},{224,192},{128,2... | collective-permute-start | bytes 983048 | tf_op jit(solution)/shard_map/ppermute | solution.py:26
  111.4 15.5 %copy-start.16 = (f32[2,6,16,512]{3,2,1,0:T(8,128)}, f32[2,6,16,512]{3,2,1,0:T(8,128)S(1)}, u32[]{:S(2)}) copy-start(f32[2,6,16,512]{3,2,1,0:T(8,128)S(1)} %collective-permute-done.14) | copy-start | bytes 1179652
  111.4 15.5 %copy-start.18 = (f32[2,6,16,512]{3,2,1,0:T(8,128)}, f32[2,6,16,512]{3,2,1,0:T(8,128)S(1)}, u32[]{:S(2)}) copy-start(f32[2,6,16,512]{3,2,1,0:T(8,128)S(1)} %collective-permute-done.15) | copy-start | bytes 1179652
  112.5 36.4 %collective-permute-start.19 = (f32[2,6,16,512]{3,2,1,0:T(8,128)}, f32[2,6,16,512]{3,2,1,0:T(8,128)}, u32[]{:S(2)}, u32[]{:S(2)}) collective-permute-start(f32[2,6,16,512]{3,2,1,0:T(8,128)} %broadcast_select_fusion), channel_id=1, source_target_pairs={{0,128},{32,160},{64,192},{96,224},{128,0},{160,32},{192,64},{224,... | collective-permute-start | bytes 1179656 | tf_op jit(solution)/shard_map/ppermute | solution.py:26
  112.9 14.3 %collective-permute-start.29 = (f32[10,16,512]{2,1,0:T(8,128)S(1)}, f32[10,16,512]{2,1,0:T(8,128)S(1)}, u32[]{:S(2)}, u32[]{:S(2)}) collective-permute-start(f32[10,16,512]{2,1,0:T(8,128)S(1)} %pad_maximum_fusion.refs_0_), channel_id=1, source_target_pairs={{0,64},{32,96},{64,0},{96,32},{128,192},{160,224},{192,128},{224,1... | collective-permute-start | bytes 983048 | tf_op jit(solution)/shard_map/ppermute | solution.py:26
  114.1 26.3 %collective-permute-start.30 = (f32[10,16,512]{2,1,0:T(8,128)S(1)}, f32[10,16,512]{2,1,0:T(8,128)S(1)}, u32[]{:S(2)}, u32[]{:S(2)}) collective-permute-start(f32[10,16,512]{2,1,0:T(8,128)S(1)} %collective-permute-done.16.refs_4_), channel_id=1, source_target_pairs={{0,32},{32,64},{64,96},{96,0},{128,160},{160,192},{192,224},{224,1... | collective-permute-start | bytes 983048 | tf_op jit(solution)/shard_map/ppermute | solution.py:26
  126.9 13.5 %collective-permute-start.31 = (f32[10,16,512]{2,1,0:T(8,128)S(1)}, f32[10,16,512]{2,1,0:T(8,128)S(1)}, u32[]{:S(2)}, u32[]{:S(2)}) collective-permute-start(f32[10,16,512]{2,1,0:T(8,128)S(1)} %collective-permute-done.16.refs_4_), channel_id=1, source_target_pairs={{32,0},{64,32},{96,64},{0,96},{160,128},{192,160},{224,192},{128,2... | collective-permute-start | bytes 983048 | tf_op jit(solution)/shard_map/ppermute | solution.py:26
  126.9 13.5 %collective-permute-start.32 = (f32[10,16,512]{2,1,0:T(8,128)S(1)}, f32[10,16,512]{2,1,0:T(8,128)S(1)}, u32[]{:S(2)}, u32[]{:S(2)}) collective-permute-start(f32[10,16,512]{2,1,0:T(8,128)S(1)} %collective-permute-done.16.refs_4_), channel_id=1, source_target_pairs={{0,64},{32,96},{64,0},{96,32},{128,192},{160,224},{192,128},{224,1... | collective-permute-start | bytes 983048 | tf_op jit(solution)/shard_map/ppermute | solution.py:26
  140.4 2.2 %copy-start = (f32[32,64,512]{2,1,0:T(8,128)S(1)}, f32[32,64,512]{2,1,0:T(8,128)}, u32[]{:S(2)}) copy-start(f32[32,64,512]{2,1,0:T(8,128)} %get-tuple-element.106.refs_8_.refs_12_) | copy-start | bytes 12582916
  142.6 6.3 %copy-start.11 = (f32[2,2,6,16,512]{4,3,2,1,0:T(8,128)S(1)}, f32[2,2,6,16,512]{4,3,2,1,0:T(8,128)}, u32[]{:S(2)}) copy-start(f32[2,2,6,16,512]{4,3,2,1,0:T(8,128)} %copy-done.10) | copy-start | bytes 2359300
  142.6 6.3 %copy-start.13 = (f32[2,2,6,16,512]{4,3,2,1,0:T(8,128)S(1)}, f32[2,2,6,16,512]{4,3,2,1,0:T(8,128)}, u32[]{:S(2)}) copy-start(f32[2,2,6,16,512]{4,3,2,1,0:T(8,128)} %copy-done.12) | copy-start | bytes 2359300
  142.6 6.3 %copy-start.17 = (f32[2,6,16,512]{3,2,1,0:T(8,128)S(1)}, f32[2,6,16,512]{3,2,1,0:T(8,128)}, u32[]{:S(2)}) copy-start(f32[2,6,16,512]{3,2,1,0:T(8,128)} %copy-done.16) | copy-start | bytes 1179652
  142.6 6.3 %copy-start.19 = (f32[2,6,16,512]{3,2,1,0:T(8,128)S(1)}, f32[2,6,16,512]{3,2,1,0:T(8,128)}, u32[]{:S(2)}) copy-start(f32[2,6,16,512]{3,2,1,0:T(8,128)} %copy-done.18) | copy-start | bytes 1179652
  143.8 2.0 %copy-start.5 = (f32[32,64,512]{2,1,0:T(8,128)}, f32[32,64,512]{2,1,0:T(8,128)S(1)}, u32[]{:S(2)}) copy-start(f32[32,64,512]{2,1,0:T(8,128)S(1)} %get-tuple-element.113.refs_13_) | copy-start | bytes 12582916
  145.8 13.4 %collective-permute-start.33 = (f32[32,2,512]{2,1,0:T(2,128)S(1)}, f32[32,2,512]{2,1,0:T(2,128)S(1)}, u32[]{:S(2)}, u32[]{:S(2)}) collective-permute-start(f32[32,2,512]{2,1,0:T(2,128)S(1)} %get-tuple-element.109), channel_id=1, source_target_pairs={{0,1},{1,2},{2,3},{4,5},{5,6},{6,7},{8,9},{9,10},{10,11},{12,13},{... | collective-permute-start | bytes 393224 | tf_op jit(solution)/shard_map/ppermute | solution.py:309
  150.3 10.7 %collective-permute-start.20 = (f32[6,16,512]{2,1,0:T(8,128)S(1)}, f32[6,16,512]{2,1,0:T(8,128)S(1)}, u32[]{:S(2)}, u32[]{:S(2)}) collective-permute-start(f32[6,16,512]{2,1,0:T(8,128)S(1)} %fusion.11.refs_0_), channel_id=1, source_target_pairs={{0,32},{32,64},{64,96},{96,0},{128,160},{160,192},{192,224},{224,1... | collective-permute-start | bytes 589832 | tf_op jit(solution)/shard_map/ppermute | solution.py:26
  152.8 6.8 %collective-permute-start.34 = (f32[32,2,512]{2,1,0:T(2,128)S(1)}, f32[32,2,512]{2,1,0:T(2,128)S(1)}, u32[]{:S(2)}, u32[]{:S(2)}) collective-permute-start(f32[32,2,512]{2,1,0:T(2,128)S(1)} %get-tuple-element.110), channel_id=1, source_target_pairs={{1,0},{2,1},{3,2},{5,4},{6,5},{7,6},{9,8},{10,9},{11,10},{13,12},{... | collective-permute-start | bytes 393224 | tf_op jit(solution)/shard_map/ppermute | solution.py:309
  156.2 14.6 %collective-permute-start.23 = (f32[6,16,512]{2,1,0:T(8,128)S(1)}, f32[6,16,512]{2,1,0:T(8,128)S(1)}, u32[]{:S(2)}, u32[]{:S(2)}) collective-permute-start(f32[6,16,512]{2,1,0:T(8,128)S(1)} %fusion.11.refs_0_), channel_id=1, source_target_pairs={{0,128},{32,160},{64,192},{96,224},{128,0},{160,32},{192,64},{224,... | collective-permute-start | bytes 589832 | tf_op jit(solution)/shard_map/ppermute | solution.py:26
  156.7 14.1 %collective-permute-start.21 = (f32[6,16,512]{2,1,0:T(8,128)S(1)}, f32[6,16,512]{2,1,0:T(8,128)S(1)}, u32[]{:S(2)}, u32[]{:S(2)}) collective-permute-start(f32[6,16,512]{2,1,0:T(8,128)S(1)} %fusion.11.refs_0_), channel_id=1, source_target_pairs={{32,0},{64,32},{96,64},{0,96},{160,128},{192,160},{224,192},{128,2... | collective-permute-start | bytes 589832 | tf_op jit(solution)/shard_map/ppermute | solution.py:26
  159.2 14.9 %collective-permute-start.22 = (f32[6,16,512]{2,1,0:T(8,128)S(1)}, f32[6,16,512]{2,1,0:T(8,128)S(1)}, u32[]{:S(2)}, u32[]{:S(2)}) collective-permute-start(f32[6,16,512]{2,1,0:T(8,128)S(1)} %fusion.11.refs_0_), channel_id=1, source_target_pairs={{0,64},{32,96},{64,0},{96,32},{128,192},{160,224},{192,128},{224,1... | collective-permute-start | bytes 589832 | tf_op jit(solution)/shard_map/ppermute | solution.py:26
  159.7 21.5 %collective-permute-start.35 = (f32[2,80,512]{2,1,0:T(8,128)S(1)}, f32[2,80,512]{2,1,0:T(8,128)S(1)}, u32[]{:S(2)}, u32[]{:S(2)}) collective-permute-start(f32[2,80,512]{2,1,0:T(8,128)S(1)} %get-tuple-element.111), channel_id=1, source_target_pairs={{0,4},{4,8},{8,12},{12,16},{16,20},{20,24},{24,28},{1,5},{5,9},{9,... | collective-permute-start | bytes 983048 | tf_op jit(solution)/shard_map/ppermute | solution.py:309
  161.0 20.2 %collective-permute-start.36 = (f32[2,80,512]{2,1,0:T(8,128)S(1)}, f32[2,80,512]{2,1,0:T(8,128)S(1)}, u32[]{:S(2)}, u32[]{:S(2)}) collective-permute-start(f32[2,80,512]{2,1,0:T(8,128)S(1)} %get-tuple-element.112), channel_id=1, source_target_pairs={{4,0},{8,4},{12,8},{16,12},{20,16},{24,20},{28,24},{5,1},{9,5},{13... | collective-permute-start | bytes 983048 | tf_op jit(solution)/shard_map/ppermute | solution.py:309
  170.8 8.1 %collective-permute-start.24 = (f32[6,16,512]{2,1,0:T(8,128)S(1)}, f32[6,16,512]{2,1,0:T(8,128)S(1)}, u32[]{:S(2)}, u32[]{:S(2)}) collective-permute-start(f32[6,16,512]{2,1,0:T(8,128)S(1)} %collective-permute-done.23.refs_4_), channel_id=1, source_target_pairs={{0,32},{32,64},{64,96},{96,0},{128,160},{160,192},{192,224},{224,1... | collective-permute-start | bytes 589832 | tf_op jit(solution)/shard_map/ppermute | solution.py:26
  170.8 8.9 %collective-permute-start.25 = (f32[6,16,512]{2,1,0:T(8,128)S(1)}, f32[6,16,512]{2,1,0:T(8,128)S(1)}, u32[]{:S(2)}, u32[]{:S(2)}) collective-permute-start(f32[6,16,512]{2,1,0:T(8,128)S(1)} %collective-permute-done.23.refs_4_), channel_id=1, source_target_pairs={{32,0},{64,32},{96,64},{0,96},{160,128},{192,160},{224,192},{128,2... | collective-permute-start | bytes 589832 | tf_op jit(solution)/shard_map/ppermute | solution.py:26
  174.0 7.2 %collective-permute-start.26 = (f32[6,16,512]{2,1,0:T(8,128)S(1)}, f32[6,16,512]{2,1,0:T(8,128)S(1)}, u32[]{:S(2)}, u32[]{:S(2)}) collective-permute-start(f32[6,16,512]{2,1,0:T(8,128)S(1)} %collective-permute-done.23.refs_4_), channel_id=1, source_target_pairs={{0,64},{32,96},{64,0},{96,32},{128,192},{160,224},{192,128},{224,1... | collective-permute-start | bytes 589832 | tf_op jit(solution)/shard_map/ppermute | solution.py:26
  (4 other events, 3.2 us)
